TPU v7x, 32 devices: a whole 2x2x4 slice. The times are simulated.
32 devices in a mesh: groups: 2 (over y), space: 8 (over z, x), inst: 2 (over core).
Axes of the slice: x: 2, y: 2, z: 4, core: 2. Of those that a mesh axis runs over, the one named last changes fastest.
Arguments:
- flow_state: float32 [12, 8, 64, 256], P('groups', 'inst', 'space'), parts along dimension 0, may hold values from -6 to 6
- jac_pitch: float32 [12, 6], P('groups'), parts along dimension 0, may hold values from -2.5 to 2.5
- jac_axial: float32 [12, 6], P('groups'), parts along dimension 0, may hold values from -2.5 to 2.5
- pseudo_step: float32 [64, 512], P('space', 'groups'), parts along dimension 1, may hold values from 0.05 to 0.5
- partner: int32 [4, 8], P('groups'), parts along dimension 0, may hold values from 0 to 7, as said below
- iface_index: int32 [4, 64], P('groups', 'space'), parts along dimension 0, may hold values from 0 to 63, as said below
Outputs:
- new_state: float32 [12, 8, 64, 256], P('groups', 'inst', 'space'), parts along dimension 0
- smoothed: float32 [12, 8, 64, 256], P('groups', 'inst', 'space'), parts along dimension 0
There are 2 independent parts, one for each index of `groups`. A program takes and returns all parts, laid end to end along the dimension named above; each array names one. Nothing has to cross between parts.
Inputs may be any that keep to these rules, and one draw needn't show every extreme that they name: Row k of partner is the cyclic shift n -> (n + s_k) mod 8 with s_k from 1 to 7. Row k of iface_index is the cyclic shift p -> (p + o_k) mod 64 of the pitch positions.
All inputs are finite; a program needn't handle non-finite values.
Results may differ from a plain program's by a relative error of at most 0.000088.
Values sent between devices are 32-bit elements; how exact they have to be, the bound alone decides.
No kernel may reach another device: no remote copies, remote signals or barrier semaphores. Data moves between devices by JAX's collectives and lax.ppermute only.
A program may use at most 64 MiB of HBM per device.

v0:
```python
import jax
import jax.numpy as jnp
from jax import lax
from jax.sharding import PartitionSpec as P

INST = 8
NA = 256
IFACES = 2
SWEEPS = 3


VISCOUS = 0.25
SMOOTHING = 1.0


def with_halo(block, sides, width):
    for axis, dim in sides:
        count = lax.axis_size(axis)
        forward = [(i, i + 1) for i in range(count - 1)]
        forward.append((count - 1, 0))
        backward = [(target, source) for source, target in forward]
        low = lax.ppermute(
            lax.slice_in_dim(block, block.shape[dim] - width, None, axis=dim), axis, forward
        )
        high = lax.ppermute(lax.slice_in_dim(block, 0, width, axis=dim), axis, backward)
        block = jnp.concatenate([low, block, high], axis=dim)
    return block


def spectral_table(instances):
    rows = jnp.arange(instances)[:, None]
    cols = jnp.arange(instances)[None, :]
    sign = (1 - 2 * ((rows - cols) % 2)).astype(jnp.float32)
    spacing = jnp.where(rows == cols, 0.5, (rows - cols).astype(jnp.float32))
    values = 0.5 * sign / jnp.tan(jnp.pi * spacing / instances)
    return jnp.where(rows == cols, 0.0, values)


def interface_planes(axial_cells, planes_count):
    return [(plane_no + 1) * axial_cells // (planes_count + 1) for plane_no in range(planes_count)]


def mix_vars(matrix, field):
    return jnp.einsum("uv,vnpa->unpa", matrix, field, precision=lax.Precision.HIGHEST)


def flux_terms(centre, pitch_next, pitch_prev, time_term, inflow, jac_pitch, jac_axial, planes):
    zeros_edge = jnp.zeros_like(centre[..., :1])
    upstream = jnp.concatenate([zeros_edge, centre[..., :-1]], axis=3)
    downstream = jnp.concatenate([centre[..., 1:], centre[..., -1:]], axis=3)
    for plane_no, plane in enumerate(planes):
        upstream = upstream.at[..., plane].set(inflow[plane_no])
        downstream = downstream.at[..., plane - 1].set(centre[..., plane - 1])
    pitch_part = mix_vars(jac_pitch, 0.5 * (pitch_next - pitch_prev))
    axial_part = mix_vars(jac_axial, centre - upstream)
    spread = pitch_next + pitch_prev + upstream + downstream - 4.0 * centre
    return pitch_part + axial_part - VISCOUS * spread + time_term


def relax(source, pitch_pair, current):
    axial_prev = jnp.pad(current[..., :-1], ((0, 0), (0, 0), (0, 0), (1, 0)))
    axial_next = jnp.pad(current[..., 1:], ((0, 0), (0, 0), (0, 0), (0, 1)))
    return (source + SMOOTHING * (pitch_pair + axial_prev + axial_next)) / (1.0 + 4.0 * SMOOTHING)


def shards(flow_state, jac_pitch, jac_axial, pseudo_step, partner, iface_index):
    inst_local = flow_state.shape[1]
    offset_inst = lax.axis_index("inst") * inst_local
    spectral = spectral_table(INST)
    rows_mine = lax.dynamic_slice_in_dim(spectral, offset_inst, inst_local, 0)
    time_term = jnp.einsum(
        "nj,vjpa->vnpa",
        rows_mine,
        lax.all_gather(flow_state, "inst", axis=1, tiled=True),
        precision=lax.Precision.HIGHEST,
    )
    planes = interface_planes(NA, IFACES)
    plane_lines = jnp.stack([flow_state[:, :, :, plane - 1] for plane in planes])
    every_inst = lax.all_gather(plane_lines, "inst", axis=2, tiled=True)
    mine_partner = lax.dynamic_slice_in_dim(partner, offset_inst, inst_local, 1)
    inflow = []
    gathered = lax.all_gather(every_inst, "space", axis=3, tiled=True)
    for plane_no in range(IFACES):
        facing = jnp.take(gathered[plane_no], iface_index[plane_no], axis=2)
        inflow.append(jnp.take(facing, mine_partner[plane_no], axis=1))
    padded = with_halo(flow_state, (("space", 2),), 1)
    residual = flux_terms(
        flow_state,
        padded[:, :, 2:],
        padded[:, :, :-2],
        time_term,
        inflow,
        jac_pitch,
        jac_axial,
        planes,
    )
    smoothed = residual
    for sweep_no in range(SWEEPS):
        rimmed = with_halo(smoothed, (("space", 2),), 1)
        smoothed = relax(residual, rimmed[:, :, 2:] + rimmed[:, :, :-2], smoothed)
    new_state = flow_state - pseudo_step[None, None] * smoothed
    return (new_state, smoothed)


def solution(mesh):
    in_specs = (
        P("groups", "inst", "space", None),
        P("groups", None),
        P("groups", None),
        P("space", "groups"),
        P("groups", None),
        P("groups", "space"),
    )
    out_specs = (P("groups", "inst", "space", None), P("groups", "inst", "space", None))
    return jax.shard_map(shards, mesh=mesh, in_specs=in_specs, out_specs=out_specs, check_vma=False)
```

profile of v0, /device:TPU:0, one launch (start us, length us, event | category | flops | bytes accessed | tf_op | source)
XLA Modules:
  0.0 87.9 jit_solution(15190155129163998638)
XLA Ops:
  0.6 0.0 copy-start
  0.6 1.1 %copy.97 = f32[6,4,8,256]{3,0,2,1:T(8,128)S(1)} copy(f32[6,4,8,256]{3,2,1,0:T(8,128)} %param.18) | data formatting | bytes 393216 | tf_op args[0]
  1.7 6.0 %collective-permute-start = (f32[6,4,1,256]{3,0,2,1:T(8,128)S(1)}, f32[6,4,1,256]{3,0,2,1:T(8,128)S(1)}, u32[]{:S(2)}, u32[]{:S(2)}) collective-permute-start(f32[6,4,1,256]{3,0,2,1:T(8,128)S(1)} %get-tuple-element.85), channel_id=1, source_target_pairs={{2,0},{4,2},{6,4},{8,6},{10,8},{12,10},{14,12},{0,14},{3,1},{5,3},... | collective-permute-start | bytes 73736 | tf_op jit(solution)/shard_map/ppermute | solution.py:25
  7.7 0.0 collective-permute-start.1
  7.7 0.2 fusion.53
  7.9 0.0 copy-start.1
  7.9 0.1 fusion.52
  8.1 0.8 copy-done.1
  8.9 0.1 fusion.27
  8.9 0.2 copy.79
  9.1 0.2 copy.81
  9.4 1.8 %all_gather.9 = f32[2,6,8,8]{3,0,1,2:T(2,128)S(1)} all-gather(f32[2,6,4,8]{3,0,1,2:T(2,128)S(1)} %copy.82), channel_id=1, replica_groups=mesh['groups'=2,'space'=8,'inst'=2] {'inst'}, dimensions={2}, use_global_device_ids=true | all-gather | bytes 4608 | tf_op jit(solution)/shard_map/all_gather | solution.py:79
  11.2 0.1 copy.83
  11.3 31.3 %all_gather.10 = f32[2,6,8,64]{2,1,3,0:T(8,128)S(1)} all-gather(f32[2,6,8,8]{2,1,3,0:T(8,128)S(1)} %copy.83), channel_id=1, replica_groups=mesh['groups'=2,'space'=8,'inst'=2] {'space'}, dimensions={3}, use_global_device_ids=true | all-gather | bytes 27648 | tf_op jit(solution)/shard_map/all_gather | solution.py:82
  42.7 0.6 copy-done.4
  43.4 0.6 gather_fusion
  43.9 0.6 gather_fusion.2
  44.5 0.1 select_bitcast_fusion
  44.6 0.1 copy.84
  44.7 0.7 copy-done.5
  45.4 0.1 constant_dynamic-slice_fusion
  45.5 0.6 gather_fusion.1
  46.0 0.1 select_bitcast_fusion.3
  46.1 0.3 copy.86
  46.4 0.1 copy.87
  46.5 0.6 gather_fusion.3
  47.0 0.1 select_bitcast_fusion.2
  47.1 0.3 copy.89
  47.4 2.2 %all_gather.11 = f32[6,8,8,256]{3,2,0,1:T(8,128)S(1)} all-gather(f32[6,4,8,256]{3,2,0,1:T(8,128)S(1)} %copy.94), channel_id=1, replica_groups=mesh['groups'=2,'space'=8,'inst'=2] {'inst'}, dimensions={1}, use_global_device_ids=true | all-gather | bytes 589824 | tf_op jit(solution)/shard_map/all_gather | solution.py:74
  49.6 0.0 copy-done.2
  49.6 0.1 concatenate.44
  49.7 2.4 %scatter.14 = f32[6,4,8,256]{3,0,2,1:T(8,128)S(1)} dynamic-update-slice(f32[6,4,8,256]{3,0,2,1:T(8,128)S(1)} %concatenate.44, f32[6,4,8,1]{3,0,2,1:T(8,128)S(1)} %copy.86, s32[]{:T(128)} %constant.166.clone.1, s32[]{:T(128)} %constant.166.clone.1, s32[]{:T(128)} %constant.166.clone.1, s32[]{:T(128)} %constant.170.clone.1) | dynamic-update-slice | bytes 1540 | tf_op jit(solution)/shard_map/scatter | solution.py:52
  52.1 2.4 %scatter.15 = f32[6,4,8,256]{3,0,2,1:T(8,128)S(1)} dynamic-update-slice(f32[6,4,8,256]{3,0,2,1:T(8,128)S(1)} %scatter.14, f32[6,4,8,1]{3,0,2,1:T(8,128)S(1)} %copy.89, s32[]{:T(128)} %constant.166.clone.1, s32[]{:T(128)} %constant.166.clone.1, s32[]{:T(128)} %constant.166.clone.1, s32[]{:T(128)} %constant.171.clone.1) | dynamic-update-slice | bytes 1540 | tf_op jit(solution)/shard_map/scatter | solution.py:52
  54.5 0.0 copy-done
  54.5 0.5 fusion.19
  54.9 0.6 fusion.3
  55.6 0.1 pad_maximum_fusion.8
  55.7 2.4 %scatter.16 = f32[6,4,8,256]{3,0,2,1:T(8,128)S(1)} dynamic-update-slice(f32[6,4,8,256]{3,0,2,1:T(8,128)S(1)} %pad_maximum_fusion.8, f32[6,4,8,1]{3,0,2,1:T(8,128)S(1)} %get-tuple-element.89, s32[]{:T(128)} %constant.166.clone.1, s32[]{:T(128)} %constant.166.clone.1, s32[]{:T(128)} %constant.166.clone.1, s32[]{:T(128)} %constant.172.clone.1) | dynamic-update-slice | bytes 1540 | tf_op jit(solution)/shard_map/scatter | solution.py:53
  58.1 0.0 copy-start.3
  58.1 2.4 %scatter.19 = f32[6,4,8,256]{3,0,2,1:T(8,128)S(1)} dynamic-update-slice(f32[6,4,8,256]{3,0,2,1:T(8,128)S(1)} %scatter.16, f32[6,4,8,1]{3,0,2,1:T(8,128)S(1)} %get-tuple-element.90, s32[]{:T(128)} %constant.166.clone.1, s32[]{:T(128)} %constant.166.clone.1, s32[]{:T(128)} %constant.166.clone.1, s32[]{:T(128)} %constant.173.clone.1) | dynamic-update-slice | bytes 1540 | tf_op jit(solution)/shard_map/scatter | solution.py:53
  60.5 0.0 collective-permute-done
  60.5 0.0 collective-permute-done.1
  60.5 0.5 fusion.2
  61.0 4.8 %collective-permute-start.2 = (f32[6,4,1,256]{3,0,2,1:T(8,128)S(1)}, f32[6,4,1,256]{3,0,2,1:T(8,128)S(1)}, u32[]{:S(2)}, u32[]{:S(2)}) collective-permute-start(f32[6,4,1,256]{3,0,2,1:T(8,128)S(1)} %get-tuple-element.82), channel_id=1, source_target_pairs={{2,0},{4,2},{6,4},{8,6},{10,8},{12,10},{14,12},{0,14},{3,1},{5,3},... | collective-permute-start | bytes 73736 | tf_op jit(solution)/shard_map/ppermute | solution.py:25
  65.8 0.0 collective-permute-start.3
  65.8 0.1 fusion.49
  65.9 1.5 %collective-permute-done.2 = f32[6,4,1,256]{3,0,2,1:T(8,128)S(1)} collective-permute-done((f32[6,4,1,256]{3,0,2,1:T(8,128)S(1)}, f32[6,4,1,256]{3,0,2,1:T(8,128)S(1)}, u32[]{:S(2)}, u32[]{:S(2)}) %collective-permute-start.2) | collective-permute-done | bytes 24608 | tf_op jit(solution)/shard_map/ppermute | solution.py:25
  67.4 5.0 %collective-permute-done.3 = f32[6,4,1,256]{3,0,2,1:T(8,128)S(1)} collective-permute-done((f32[6,4,1,256]{3,0,2,1:T(8,128)S(1)}, f32[6,4,1,256]{3,0,2,1:T(8,128)S(1)}, u32[]{:S(2)}, u32[]{:S(2)}) %collective-permute-start.3) | collective-permute-done | bytes 24608 | tf_op jit(solution)/shard_map/ppermute | solution.py:22
  72.4 0.1 fusion.18
  72.6 0.1 collective-permute-start.4
  72.6 2.0 %collective-permute-start.5 = (f32[6,4,1,256]{3,0,2,1:T(8,128)S(1)}, f32[6,4,1,256]{3,0,2,1:T(8,128)S(1)}, u32[]{:S(2)}, u32[]{:S(2)}) collective-permute-start(f32[6,4,1,256]{3,0,2,1:T(8,128)S(1)} %get-tuple-element.79), channel_id=1, source_target_pairs={{0,2},{2,4},{4,6},{6,8},{8,10},{10,12},{12,14},{14,0},{1,3},{3,5},... | collective-permute-start | bytes 73736 | tf_op jit(solution)/shard_map/ppermute | solution.py:22
  74.6 0.1 fusion.47
  74.8 1.8 %collective-permute-done.4 = f32[6,4,1,256]{3,0,2,1:T(8,128)S(1)} collective-permute-done((f32[6,4,1,256]{3,0,2,1:T(8,128)S(1)}, f32[6,4,1,256]{3,0,2,1:T(8,128)S(1)}, u32[]{:S(2)}, u32[]{:S(2)}) %collective-permute-start.4) | collective-permute-done | bytes 24608 | tf_op jit(solution)/shard_map/ppermute | solution.py:25
  76.5 2.8 %collective-permute-done.5 = f32[6,4,1,256]{3,0,2,1:T(8,128)S(1)} collective-permute-done((f32[6,4,1,256]{3,0,2,1:T(8,128)S(1)}, f32[6,4,1,256]{3,0,2,1:T(8,128)S(1)}, u32[]{:S(2)}, u32[]{:S(2)}) %collective-permute-start.5) | collective-permute-done | bytes 24608 | tf_op jit(solution)/shard_map/ppermute | solution.py:22
  79.3 0.1 fusion.13
  79.4 0.1 collective-permute-start.6
  79.5 2.0 %collective-permute-start.7 = (f32[6,4,1,256]{3,0,2,1:T(8,128)S(1)}, f32[6,4,1,256]{3,0,2,1:T(8,128)S(1)}, u32[]{:S(2)}, u32[]{:S(2)}) collective-permute-start(f32[6,4,1,256]{3,0,2,1:T(8,128)S(1)} %get-tuple-element.73), channel_id=1, source_target_pairs={{0,2},{2,4},{4,6},{6,8},{8,10},{10,12},{12,14},{14,0},{1,3},{3,5},... | collective-permute-start | bytes 73736 | tf_op jit(solution)/shard_map/ppermute | solution.py:22
  81.5 0.1 fusion.46
  81.7 1.8 %collective-permute-done.6 = f32[6,4,1,256]{3,0,2,1:T(8,128)S(1)} collective-permute-done((f32[6,4,1,256]{3,0,2,1:T(8,128)S(1)}, f32[6,4,1,256]{3,0,2,1:T(8,128)S(1)}, u32[]{:S(2)}, u32[]{:S(2)}) %collective-permute-start.6) | collective-permute-done | bytes 24608 | tf_op jit(solution)/shard_map/ppermute | solution.py:25
  83.4 2.8 %collective-permute-done.7 = f32[6,4,1,256]{3,0,2,1:T(8,128)S(1)} collective-permute-done((f32[6,4,1,256]{3,0,2,1:T(8,128)S(1)}, f32[6,4,1,256]{3,0,2,1:T(8,128)S(1)}, u32[]{:S(2)}, u32[]{:S(2)}) %collective-permute-start.7) | collective-permute-done | bytes 24608 | tf_op jit(solution)/shard_map/ppermute | solution.py:22
  86.2 0.1 broadcast_multiply_fusion
  86.3 0.1 multiply_subtract_fusion
  86.5 0.7 copy.98
  87.2 0.7 copy.99
  (18 shorter events, 0.1 us)
Async XLA Ops:
  0.6 53.8 %copy-start = (f32[6,6]{1,0:T(8,128)S(1)}, f32[6,6]{1,0:T(8,128)}, u32[]{:S(2)}) copy-start(f32[6,6]{1,0:T(8,128)} %param.20) | copy-start | bytes 436
  1.7 58.7 %collective-permute-start = (f32[6,4,1,256]{3,0,2,1:T(8,128)S(1)}, f32[6,4,1,256]{3,0,2,1:T(8,128)S(1)}, u32[]{:S(2)}, u32[]{:S(2)}) collective-permute-start(f32[6,4,1,256]{3,0,2,1:T(8,128)S(1)} %get-tuple-element.85), channel_id=1, source_target_pairs={{2,0},{4,2},{6,4},{8,6},{10,8},{12,10},{14,12},{0,14},{3,1},{5,3},... | collective-permute-start | bytes 73736 | tf_op jit(solution)/shard_map/ppermute | solution.py:25
  7.7 52.7 %collective-permute-start.1 = (f32[6,4,1,256]{3,0,2,1:T(8,128)S(1)}, f32[6,4,1,256]{3,0,2,1:T(8,128)S(1)}, u32[]{:S(2)}, u32[]{:S(2)}) collective-permute-start(f32[6,4,1,256]{3,0,2,1:T(8,128)S(1)} %get-tuple-element.84), channel_id=1, source_target_pairs={{0,2},{2,4},{4,6},{6,8},{8,10},{10,12},{12,14},{14,0},{1,3},{3,5},... | collective-permute-start | bytes 73736 | tf_op jit(solution)/shard_map/ppermute | solution.py:22
  7.9 0.9 %copy-start.1 = (f32[6,4,8,256]{3,2,1,0:T(8,128)S(1)}, f32[6,4,8,256]{3,2,1,0:T(8,128)}, u32[]{:S(2)}) copy-start(f32[6,4,8,256]{3,2,1,0:T(8,128)} %param.18) | copy-start | bytes 589828
  42.7 0.7 copy-start.4
  44.7 0.7 copy-start.5
  47.4 2.2 %copy-start.2 = (f32[8,256]{1,0:T(8,128)S(1)}, f32[8,256]{1,0:T(8,128)}, u32[]{:S(2)}) copy-start(f32[8,256]{1,0:T(8,128)} %param.21) | copy-start | bytes 24580
  58.1 2.4 %copy-start.3 = (f32[6,6]{1,0:T(8,128)S(1)}, f32[6,6]{1,0:T(8,128)}, u32[]{:S(2)}) copy-start(f32[6,6]{1,0:T(8,128)} %param.19) | copy-start | bytes 436
  61.0 6.4 %collective-permute-start.2 = (f32[6,4,1,256]{3,0,2,1:T(8,128)S(1)}, f32[6,4,1,256]{3,0,2,1:T(8,128)S(1)}, u32[]{:S(2)}, u32[]{:S(2)}) collective-permute-start(f32[6,4,1,256]{3,0,2,1:T(8,128)S(1)} %get-tuple-element.82), channel_id=1, source_target_pairs={{2,0},{4,2},{6,4},{8,6},{10,8},{12,10},{14,12},{0,14},{3,1},{5,3},... | collective-permute-start | bytes 73736 | tf_op jit(solution)/shard_map/ppermute | solution.py:25
  65.8 6.6 %collective-permute-start.3 = (f32[6,4,1,256]{3,0,2,1:T(8,128)S(1)}, f32[6,4,1,256]{3,0,2,1:T(8,128)S(1)}, u32[]{:S(2)}, u32[]{:S(2)}) collective-permute-start(f32[6,4,1,256]{3,0,2,1:T(8,128)S(1)} %get-tuple-element.83), channel_id=1, source_target_pairs={{0,2},{2,4},{4,6},{6,8},{8,10},{10,12},{12,14},{14,0},{1,3},{3,5},... | collective-permute-start | bytes 73736 | tf_op jit(solution)/shard_map/ppermute | solution.py:22
  72.6 4.0 %collective-permute-start.4 = (f32[6,4,1,256]{3,0,2,1:T(8,128)S(1)}, f32[6,4,1,256]{3,0,2,1:T(8,128)S(1)}, u32[]{:S(2)}, u32[]{:S(2)}) collective-permute-start(f32[6,4,1,256]{3,0,2,1:T(8,128)S(1)} %get-tuple-element.78), channel_id=1, source_target_pairs={{2,0},{4,2},{6,4},{8,6},{10,8},{12,10},{14,12},{0,14},{3,1},{5,3},... | collective-permute-start | bytes 73736 | tf_op jit(solution)/shard_map/ppermute | solution.py:25
  72.6 6.7 %collective-permute-start.5 = (f32[6,4,1,256]{3,0,2,1:T(8,128)S(1)}, f32[6,4,1,256]{3,0,2,1:T(8,128)S(1)}, u32[]{:S(2)}, u32[]{:S(2)}) collective-permute-start(f32[6,4,1,256]{3,0,2,1:T(8,128)S(1)} %get-tuple-element.79), channel_id=1, source_target_pairs={{0,2},{2,4},{4,6},{6,8},{8,10},{10,12},{12,14},{14,0},{1,3},{3,5},... | collective-permute-start | bytes 73736 | tf_op jit(solution)/shard_map/ppermute | solution.py:22
  79.4 4.0 %collective-permute-start.6 = (f32[6,4,1,256]{3,0,2,1:T(8,128)S(1)}, f32[6,4,1,256]{3,0,2,1:T(8,128)S(1)}, u32[]{:S(2)}, u32[]{:S(2)}) collective-permute-start(f32[6,4,1,256]{3,0,2,1:T(8,128)S(1)} %get-tuple-element.72), channel_id=1, source_target_pairs={{2,0},{4,2},{6,4},{8,6},{10,8},{12,10},{14,12},{0,14},{3,1},{5,3},... | collective-permute-start | bytes 73736 | tf_op jit(solution)/shard_map/ppermute | solution.py:25
  79.5 6.7 %collective-permute-start.7 = (f32[6,4,1,256]{3,0,2,1:T(8,128)S(1)}, f32[6,4,1,256]{3,0,2,1:T(8,128)S(1)}, u32[]{:S(2)}, u32[]{:S(2)}) collective-permute-start(f32[6,4,1,256]{3,0,2,1:T(8,128)S(1)} %get-tuple-element.73), channel_id=1, source_target_pairs={{0,2},{2,4},{4,6},{6,8},{8,10},{10,12},{12,14},{14,0},{1,3},{3,5},... | collective-permute-start | bytes 73736 | tf_op jit(solution)/shard_map/ppermute | solution.py:22
where the time goes:
time: 88.2 us; the launch traced here: 87.9 us
  blocking collectives  35.4 us (40%)
  local copies, waits for them, and re-layouts  18.6 us (21%)
  waiting for transfers between devices  15.5 us (18%)
  starting transfers between devices  14.9 us (17%)
  matrix products  1.62 us (2%)
  other arithmetic  0.98 us (1%)
  between operations  0.98 us (1%)
    all_gather x1, blocking collectives, shards(): gathered = lax.all_gather(every_inst, 'space', axis=3, tiled=True)  31.3 us
    ppermute x4, starting transfers between devices, with_halo(): lax.ppermute(lax.slice_in_dim(block, 0, width, axis=dim), axis, backward)  10.9 us
    ppermute x4, waiting for transfers between devices, with_halo(): lax.ppermute(lax.slice_in_dim(block, block.shape[dim] - width, None, axis...  10.5 us
    ppermute x4, waiting for transfers between devices, with_halo(): lax.ppermute(lax.slice_in_dim(block, 0, width, axis=dim), axis, backward)  4.97 us
    scatter x2, local copies, waits for them, and re-layouts, flux_terms(): downstream = downstream.at[..., plane - 1].set(centre[..., plane - 1])  4.73 us
    scatter x2, local copies, waits for them, and re-layouts, flux_terms(): upstream = upstream.at[..., plane].set(inflow[plane_no])  4.73 us
    unnamed x16, local copies, waits for them, and re-layouts  4.67 us
    ppermute x4, starting transfers between devices, with_halo(): lax.ppermute(lax.slice_in_dim(block, block.shape[dim] - width, None, axis...  4.03 us
  transfers between devices with their start and end apart: 8, of which 6 were waited for; matrix products, arithmetic and copies ran while one was open for 18% of the time, Pallas kernels for 0%

commit v1 on v0

v1 whole, which is shorter than its diff:
```python
import functools
import math

import jax
import jax.numpy as jnp
from jax import lax
from jax.experimental import pallas as pl
from jax.experimental.pallas import tpu as pltpu
from jax.sharding import PartitionSpec as P

IFACES = 2
SWEEPS = 3
VISCOUS = 0.25
SMOOTHING = 1.0
HALO = 4
ROWS = 8
LANES = 128


def spectral_entry(shift, instances):
    shift %= instances
    if shift == 0:
        return 0.0
    return 0.5 * (-1) ** shift / math.tan(math.pi * shift / instances)


def interface_planes(axial_cells, planes_count):
    return [(plane_no + 1) * axial_cells // (planes_count + 1) for plane_no in range(planes_count)]


def pack_kernel(planes, own_ref, oth_ref, line_ref, edge_ref):
    core = lax.axis_index("inst")
    low = lax.rem(lax.axis_index("space") + core, 2) == 0
    nvar, ninst = own_ref.shape[:2]
    lane = lax.broadcasted_iota(jnp.int32, (ROWS, LANES), 1)
    line = jnp.zeros((ROWS, LANES), jnp.float32)
    for plane_no, plane in enumerate(planes):
        for v in range(nvar):
            for half, ref in enumerate((own_ref, oth_ref)):
                for n in range(ninst):
                    at = (plane_no * nvar + v) * 2 * ninst + half * ninst + n
                    cell = jnp.broadcast_to(ref[v, n, :, plane - 1 : plane], (ROWS, LANES))
                    line = jnp.where(lane == at, cell, line)
    swapped = jnp.where(
        lax.rem(lane, 2 * ninst) < ninst,
        pltpu.roll(line, LANES - ninst, 1),
        pltpu.roll(line, ninst, 1),
    )
    line_ref[...] = jnp.where(core == 0, line, swapped)
    axial = own_ref.shape[3]
    row = lax.broadcasted_iota(jnp.int32, (ROWS, axial), 0)
    for v in range(nvar):
        for n in range(ninst):
            own, oth = own_ref[v, n], oth_ref[v, n]
            first = jnp.where(core == 0, own, oth)
            second = jnp.where(core == 0, oth, own)
            low_rows = jnp.where(row < HALO, first, pltpu.roll(second, HALO, 0))
            high_rows = jnp.where(row < HALO, pltpu.roll(first, HALO, 0), second)
            edge_ref[v, n] = jnp.where(low, low_rows, high_rows)


def step_kernel(
    planes,
    spaces,
    jac_pitch_ref,
    jac_axial_ref,
    partner_ref,
    index_ref,
    own_ref,
    oth_ref,
    near_ref,
    far_ref,
    lines_ref,
    step_ref,
    new_ref,
    out_ref,
    field_ref,
    window_ref,
    res_ref,
):
    core = lax.axis_index("inst")
    space = lax.axis_index("space")
    low = lax.rem(space + core, 2) == 0
    nvar, ninst, _, axial = own_ref.shape
    row8 = lax.broadcasted_iota(jnp.int32, (ROWS, axial), 0)
    for v in range(nvar):
        for n in range(ninst):
            near, far = near_ref[v, n], far_ref[v, n]
            below = jnp.where(low, near, far)
            above = jnp.where(low, far, near)
            field_ref[core, v, n, 0:ROWS] = own_ref[v, n]
            field_ref[1 - core, v, n, 0:ROWS] = oth_ref[v, n]
            field_ref[0, v, n, ROWS : 2 * ROWS] = jnp.where(
                row8 < HALO, above, pltpu.roll(below, HALO, 0)
            )
            field_ref[1, v, n, ROWS : 2 * ROWS] = jnp.where(
                row8 < HALO, pltpu.roll(above, HALO, 0), below
            )
    lane8 = lax.broadcasted_iota(jnp.int32, (ROWS, LANES), 1)
    row_l = lax.broadcasted_iota(jnp.int32, (ROWS, LANES), 0)
    facing = []
    for plane_no in range(len(planes)):
        first = index_ref[plane_no, 0]
        block, offset = first // ROWS, lax.rem(first, ROWS)
        for k in range(4):
            node = lax.rem(block + (spaces - 1 + k), spaces)
            at = pl.multiple_of((space ^ node) * ROWS, ROWS)
            window_ref[plane_no, pl.ds(k * ROWS, ROWS), :] = lines_ref[pl.ds(at, ROWS), :]
        mine = window_ref[plane_no, pl.ds(ROWS + offset, ROWS), :]
        after = window_ref[plane_no, pl.ds(2 * ROWS + offset, ROWS), :]
        before = window_ref[plane_no, pl.ds(offset, ROWS), :]
        shift = lax.rem(partner_ref[plane_no, 0], 2 * ninst)
        tiles = []
        for tile in (mine, jnp.where(row_l < HALO, after, before)):
            turned = jnp.where(
                lax.rem(lane8, 2 * ninst) + shift < 2 * ninst,
                pltpu.roll(tile, LANES - shift, 1),
                pltpu.roll(tile, 2 * ninst - shift, 1),
            )
            tiles.append(pltpu.roll(turned, lax.rem(LANES - ninst * core, LANES), 1))
        facing.append(jnp.concatenate(tiles, 0))

    lane = lax.broadcasted_iota(jnp.int32, (2 * ROWS, axial), 1)
    for n in range(ninst):
        centre, slope, inward, spread = [], [], [], []
        for v in range(nvar):
            c = field_ref[core, v, n]
            nxt, prv = pltpu.roll(c, 2 * ROWS - 1, 0), pltpu.roll(c, 1, 0)
            up = jnp.where(lane == 0, 0.0, pltpu.roll(c, 1, 1))
            down = jnp.where(lane == axial - 1, c, pltpu.roll(c, axial - 1, 1))
            for plane_no, plane in enumerate(planes):
                at = (plane_no * nvar + v) * 2 * ninst + n
                up = jnp.where(lane == plane, facing[plane_no][:, at : at + 1], up)
                down = jnp.where(lane == plane - 1, c, down)
            centre.append(c)
            slope.append(0.5 * (nxt - prv))
            inward.append(c - up)
            spread.append(nxt + prv + up + down - 4.0 * c)
        for u in range(nvar):
            total = -VISCOUS * spread[u]
            for v in range(nvar):
                total += jac_pitch_ref[u, v] * slope[v]
                total += jac_axial_ref[u, v] * inward[v]
            for j in range(ninst):
                if j != n:
                    total += spectral_entry(n - j, 2 * ninst) * field_ref[core, u, j]
                total += spectral_entry(n - j - ninst, 2 * ninst) * field_ref[1 - core, u, j]
            res_ref[u, n] = total

    scale = 1.0 / (1.0 + 4.0 * SMOOTHING)
    step = step_ref[...]
    for n in range(ninst):
        for u in range(nvar):
            res = res_ref[u, n]
            s = res
            for _ in range(SWEEPS):
                pair = pltpu.roll(s, 2 * ROWS - 1, 0) + pltpu.roll(s, 1, 0)
                prv = jnp.where(lane == 0, 0.0, pltpu.roll(s, 1, 1))
                nxt = jnp.where(lane == axial - 1, 0.0, pltpu.roll(s, axial - 1, 1))
                s = (res + SMOOTHING * (pair + prv + nxt)) * scale
            smoothed = s[0:ROWS]
            out_ref[u, n] = smoothed
            new_ref[u, n] = own_ref[u, n] - step * smoothed


def shards(flow_state, jac_pitch, jac_axial, pseudo_step, partner, iface_index):
    nvar, ninst, rows, axial = flow_state.shape
    spaces = lax.axis_size("space")
    planes = interface_planes(axial, IFACES)
    both = ("space", "inst")
    vmem = pl.BlockSpec(memory_space=pltpu.VMEM)
    smem = pl.BlockSpec(memory_space=pltpu.SMEM)

    other = lax.ppermute(flow_state, "inst", [(0, 1), (1, 0)])
    line, edge = pl.pallas_call(
        functools.partial(pack_kernel, planes),
        out_shape=(
            jax.ShapeDtypeStruct((rows, LANES), jnp.float32),
            jax.ShapeDtypeStruct((nvar, ninst, rows, axial), jnp.float32),
        ),
        in_specs=[vmem, vmem],
        out_specs=(vmem, vmem),
    )(flow_state, other)

    pairs = []
    for i in range(spaces):
        odd = (i + 1) % spaces if i % 2 else (i - 1) % spaces
        pairs += [(2 * i, 2 * odd), (2 * i + 1, 2 * (i ^ 1) + 1)]
    near = lax.ppermute(edge, both, pairs)
    far = lax.ppermute(near, "inst", [(0, 1), (1, 0)])

    lines, bit = line, 1
    while bit < spaces:
        got = lax.ppermute(lines, both, [(2 * i + 1, 2 * (i ^ bit) + 1) for i in range(spaces)])
        lines = jnp.concatenate([lines, got], axis=0)
        bit *= 2
    sent = lax.ppermute(lines, "inst", [(1, 0)])
    lines = jnp.where(lax.axis_index("inst") == 0, sent, lines)

    return pl.pallas_call(
        functools.partial(step_kernel, planes, spaces),
        out_shape=(
            jax.ShapeDtypeStruct(flow_state.shape, jnp.float32),
            jax.ShapeDtypeStruct(flow_state.shape, jnp.float32),
        ),
        in_specs=[smem] * 4 + [vmem] * 6,
        out_specs=(vmem, vmem),
        scratch_shapes=[
            pltpu.VMEM((2, nvar, ninst, 2 * rows, axial), jnp.float32),
            pltpu.VMEM((IFACES, 4 * rows + rows, LANES), jnp.float32),
            pltpu.VMEM((nvar, ninst, 2 * rows, axial), jnp.float32),
        ],
    )(
        jac_pitch, jac_axial, partner, iface_index,
        flow_state, other, near, far, lines, pseudo_step,
    )


def solution(mesh):
    in_specs = (
        P("groups", "inst", "space", None),
        P("groups", None),
        P("groups", None),
        P("space", "groups"),
        P("groups", None),
        P("groups", "space"),
    )
    out_specs = (P("groups", "inst", "space", None), P("groups", "inst", "space", None))
    return jax.shard_map(shards, mesh=mesh, in_specs=in_specs, out_specs=out_specs, check_vma=False)
```

time: 88.2 us -> 30.5 us (0.35)
  blocking collectives: 35.4 us -> 0 us
  local copies, waits for them, and re-layouts: 18.6 us -> 2.06 us
  waiting for transfers between devices: 15.5 us -> 3.12 us
  Pallas kernels: 0 us -> 7.81 us
  matrix products: 1.62 us -> 0 us
  starting transfers between devices: 14.9 us -> 15.9 us
    all_gather x3 -> x0, blocking collectives: 35.4 us -> none  [the longest x1 31.3 us: shards(): gathered = lax.all_gather(every_inst, 'space', axis=3, tiled=True)]
    ppermute x8 -> x7, waiting for transfers between devices: 15.5 us -> 3.12 us  [the longest x1 1.28 us: shards(): other = lax.ppermute(flow_state, 'inst', [(0, 1), (1, 0)])]
    scatter x4 -> x0, local copies, waits for them, and re-layouts: 9.46 us -> none  [the longest x2 4.73 us: flux_terms(): downstream = downstream.at[..., plane - 1].set(centre[..., plane - 1])]
    pallas_call x0 -> x2, Pallas kernels: none -> 7.81 us  [the longest x1 5.9 us: shards(): pl.pallas_call(functools.partial(step_kernel, planes, spaces), out_shape=...]
    unnamed x16 -> x11, local copies, waits for them, and re-layouts: 4.67 us -> 2.06 us
    gather x4 -> x0, local copies, waits for them, and re-layouts: 2.21 us -> none  [the longest x2 1.11 us: shards(): facing = jnp.take(gathered[plane_no], iface_index[plane_no], axis=2)]
    dot_general x3 -> x0, matrix products: 1.62 us -> none  [the longest x2 0.98 us: mix_vars(): jnp.einsum('uv,vnpa->unpa', matrix, field, precision=lax.Precision.HIGHEST)]
    slice x11 -> x0, local copies, waits for them, and re-layouts: 1.15 us -> none  [the longest x2 0.45 us: shards(): flow_state[:, :, :, plane - 1]]
  transfers between devices with their start and end apart: 8 -> 7, of which waited for: 6 -> 3; matrix products, arithmetic and copies ran while one was open for 18% -> 4% of each run, Pallas kernels for 0% -> 0%
where the time goes in v1:
time: 30.5 us; the launch traced here: 30.3 us
  starting transfers between devices  15.9 us (52%)
  Pallas kernels  7.81 us (26%)
  waiting for transfers between devices  3.12 us (10%)
  local copies, waits for them, and re-layouts  2.06 us (7%)
  between operations  0.73 us (2%)
  other arithmetic  0.61 us (2%)
    ppermute x1, starting transfers between devices, shards(): far = lax.ppermute(near, 'inst', [(0, 1), (1, 0)])  6.13 us
    pallas_call x1, Pallas kernels, shards(): pl.pallas_call(functools.partial(step_kernel, planes, spaces), out_shape=...  5.9 us
    ppermute x1, starting transfers between devices, shards(): near = lax.ppermute(edge, both, pairs)  5.9 us
    ppermute x3, starting transfers between devices, shards(): lax.ppermute(lines, both, [(2 * i + 1, 2 * (i ^ bit) + 1) for i in range(...  2.1 us
    unnamed x11, local copies, waits for them, and re-layouts  2.06 us
    pallas_call x1, Pallas kernels, shards(): pl.pallas_call(functools.partial(pack_kernel, planes), out_shape=(jax.Sha...  1.9 us
    ppermute x1, starting transfers between devices, shards(): sent = lax.ppermute(lines, 'inst', [(1, 0)])  1.29 us
    ppermute x1, waiting for transfers between devices, shards(): other = lax.ppermute(flow_state, 'inst', [(0, 1), (1, 0)])  1.28 us
  transfers between devices with their start and end apart: 7, of which 3 were waited for; matrix products, arithmetic and copies ran while one was open for 4% of the time, Pallas kernels for 0%

profile of v1, /device:TPU:0, one launch (start us, length us, event | category | flops | bytes accessed | tf_op | source)
XLA Modules:
  0.0 30.3 jit_solution(6100680589901449393)
XLA Ops:
  0.6 0.5 %collective-permute-start = (f32[6,4,8,256]{3,2,1,0:T(8,128)}, f32[6,4,8,256]{3,2,1,0:T(8,128)S(1)}, u32[]{:S(2)}, u32[]{:S(2)}) collective-permute-start(f32[6,4,8,256]{3,2,1,0:T(8,128)} %own_ref.3), channel_id=1, source_target_pairs={{0,1},{1,0},{2,3},{3,2},{4,5},{5,4},{6,7},{7,6},{8,9},{9,8},{10,11... | collective-permute-start | bytes 589832 | tf_op jit(solution)/shard_map/ppermute | solution.py:174
  1.1 1.3 %collective-permute-done.oth_ref = f32[6,4,8,256]{3,2,1,0:T(8,128)S(1)} collective-permute-done((f32[6,4,8,256]{3,2,1,0:T(8,128)}, f32[6,4,8,256]{3,2,1,0:T(8,128)S(1)}, u32[]{:S(2)}, u32[]{:S(2)}) %collective-permute-start) | collective-permute-done | bytes 196640 | tf_op jit(solution)/shard_map/ppermute | solution.py:174
  2.4 0.0 copy-start
  2.4 0.7 %copy-done = f32[6,4,8,256]{3,2,1,0:T(8,128)} copy-done((f32[6,4,8,256]{3,2,1,0:T(8,128)}, f32[6,4,8,256]{3,2,1,0:T(8,128)S(1)}, u32[]{:S(2)}) %copy-start) | copy-done | bytes 196632
  3.1 1.9 %shard_map.77 = (f32[8,128]{1,0:T(8,128)}, f32[6,4,8,256]{3,2,1,0:T(8,128)}) custom-call(f32[6,4,8,256]{3,2,1,0:T(8,128)} %own_ref.3, f32[6,4,8,256]{3,2,1,0:T(8,128)} %copy-done), custom_call_target="tpu_custom_call" | custom-call | tf_op jit(solution)/shard_map/pallas_call | solution.py:175
  5.0 0.0 copy-start.3
  5.0 0.8 %collective-permute-start.3 = (f32[8,128]{1,0:T(8,128)}, f32[8,128]{1,0:T(8,128)S(1)}, u32[]{:S(2)}, u32[]{:S(2)}) collective-permute-start(f32[8,128]{1,0:T(8,128)} %get-tuple-element.5), channel_id=1, source_target_pairs={{1,3},{3,1},{5,7},{7,5},{9,11},{11,9},{13,15},{15,13},{17,19},{19,... | collective-permute-start | bytes 12296 | tf_op jit(solution)/shard_map/ppermute | solution.py:194
  5.8 0.7 %constant_dynamic-update-slice_fusion.3 = f32[64,128]{1,0:T(8,128)S(1)} fusion(f32[8,128]{1,0:T(8,128)} %get-tuple-element.5), kind=kLoop, calls=%fused_computation.5 | loop fusion | bytes 8192
  6.5 5.9 %collective-permute-start.1 = (f32[6,4,8,256]{3,2,1,0:T(8,128)}, f32[6,4,8,256]{3,2,1,0:T(8,128)S(1)}, u32[]{:S(2)}, u32[]{:S(2)}) collective-permute-start(f32[6,4,8,256]{3,2,1,0:T(8,128)} %get-tuple-element.4), channel_id=1, source_target_pairs={{0,14},{1,3},{2,4},{3,1},{4,2},{5,7},{6,8},{7,5},{8,6},{9,11},{10,... | collective-permute-start | bytes 589832 | tf_op jit(solution)/shard_map/ppermute | solution.py:189
  12.4 0.0 collective-permute-done.3
  12.4 0.0 copy-done.3
  12.4 0.7 %collective-permute-start.4 = (f32[16,128]{1,0:T(8,128)S(1)}, f32[16,128]{1,0:T(8,128)S(1)}, u32[]{:S(2)}, u32[]{:S(2)}) collective-permute-start(f32[16,128]{1,0:T(8,128)S(1)} %pad_maximum_fusion.1), channel_id=1, source_target_pairs={{1,5},{3,7},{5,1},{7,3},{9,13},{11,15},{13,9},{15,11},{17,21},{19,... | collective-permute-start | bytes 24584 | tf_op jit(solution)/shard_map/ppermute | solution.py:194
  13.1 0.0 collective-permute-done.4
  13.1 0.7 %collective-permute-start.5 = (f32[32,128]{1,0:T(8,128)S(1)}, f32[32,128]{1,0:T(8,128)S(1)}, u32[]{:S(2)}, u32[]{:S(2)}) collective-permute-start(f32[32,128]{1,0:T(8,128)S(1)} %pad_maximum_fusion), channel_id=1, source_target_pairs={{1,9},{3,11},{5,13},{7,15},{9,1},{11,3},{13,5},{15,7},{17,25},{19,... | collective-permute-start | bytes 49160 | tf_op jit(solution)/shard_map/ppermute | solution.py:194
  13.8 0.0 collective-permute-done.5
  13.8 1.3 %collective-permute-start.6 = (f32[64,128]{1,0:T(8,128)S(1)}, f32[64,128]{1,0:T(8,128)S(1)}, u32[]{:S(2)}, u32[]{:S(2)}) collective-permute-start(f32[64,128]{1,0:T(8,128)S(1)} %constant_dynamic-update-slice_fusion), channel_id=1, source_target_pairs={{1,0},{3,2},{5,4},{7,6},{9,8},{11,10},{13,12},{15,14},{17,16},{19,... | collective-permute-start | bytes 98312 | tf_op jit(solution)/shard_map/ppermute | solution.py:197
  15.1 1.2 %collective-permute-done.1.near_ref = f32[6,4,8,256]{3,2,1,0:T(8,128)S(1)} collective-permute-done((f32[6,4,8,256]{3,2,1,0:T(8,128)}, f32[6,4,8,256]{3,2,1,0:T(8,128)S(1)}, u32[]{:S(2)}, u32[]{:S(2)}) %collective-permute-start.1) | collective-permute-done | bytes 196640 | tf_op jit(solution)/shard_map/ppermute | solution.py:189
  16.4 0.0 copy-start.1
  16.4 6.1 %collective-permute-start.2 = (f32[6,4,8,256]{3,2,1,0:T(8,128)S(1)}, f32[6,4,8,256]{3,2,1,0:T(8,128)S(1)}, u32[]{:S(2)}, u32[]{:S(2)}) collective-permute-start(f32[6,4,8,256]{3,2,1,0:T(8,128)S(1)} %collective-permute-done.1.near_ref), channel_id=1, source_target_pairs={{0,1},{1,0},{2,3},{3,2},{4,5},{5,4},{6,7},{7,6},{8,9},{9,8},{10,11... | collective-permute-start | bytes 589832 | tf_op jit(solution)/shard_map/ppermute | solution.py:190
  22.5 0.6 %collective-permute-done.6 = f32[64,128]{1,0:T(8,128)S(1)} collective-permute-done((f32[64,128]{1,0:T(8,128)S(1)}, f32[64,128]{1,0:T(8,128)S(1)}, u32[]{:S(2)}, u32[]{:S(2)}) %collective-permute-start.6) | collective-permute-done | bytes 32800 | tf_op jit(solution)/shard_map/ppermute | solution.py:197
  23.1 0.6 %broadcast_select_fusion.lines_ref = f32[64,128]{1,0:T(8,128)} fusion(f32[64,128]{1,0:T(8,128)S(1)} %collective-permute-done.6, f32[64,128]{1,0:T(8,128)S(1)} %constant_dynamic-update-slice_fusion, pred[]{:T(512)S(6)} %eq.3), kind=kLoop, calls=%fused_computation.1 | loop fusion | flops 8192 | bytes 98305 | tf_op jit(solution)/shard_map/jit(_where)/select_n | solution.py:198
  23.7 0.0 collective-permute-done.2.far_ref
  23.7 0.0 copy-done.1
  23.7 0.0 copy-start.2
  23.7 0.7 %copy-done.2 = f32[6,4,8,256]{3,2,1,0:T(8,128)} copy-done((f32[6,4,8,256]{3,2,1,0:T(8,128)}, f32[6,4,8,256]{3,2,1,0:T(8,128)S(1)}, u32[]{:S(2)}) %copy-start.2) | copy-done | bytes 196632
  24.4 5.9 %shard_map.78 = (f32[6,4,8,256]{3,2,1,0:T(8,128)}, f32[6,4,8,256]{3,2,1,0:T(8,128)}) custom-call(f32[6,6]{1,0:T(8,128)} %jac_pitch_ref.1, f32[6,6]{1,0:T(8,128)} %jac_axial_ref.1, s32[2,8]{1,0:T(2,128)} %partner_ref.1, s32[2,8]{1,0:T(2,128)} %index_ref.1, f32[6,4,8,256]{3,2,1,0:T(8,128)} %own_ref.3, f32[6,4,8,256]{3,2,1,0:T(8,128)} %copy-done, ...), custom_call_target="tpu_custom_call" | custom-call | tf_op jit(solution)/shard_map/pallas_call | solution.py:200
  (5 shorter events, 0.0 us)
Async XLA Ops:
  0.6 1.8 %collective-permute-start = (f32[6,4,8,256]{3,2,1,0:T(8,128)}, f32[6,4,8,256]{3,2,1,0:T(8,128)S(1)}, u32[]{:S(2)}, u32[]{:S(2)}) collective-permute-start(f32[6,4,8,256]{3,2,1,0:T(8,128)} %own_ref.3), channel_id=1, source_target_pairs={{0,1},{1,0},{2,3},{3,2},{4,5},{5,4},{6,7},{7,6},{8,9},{9,8},{10,11... | collective-permute-start | bytes 589832 | tf_op jit(solution)/shard_map/ppermute | solution.py:174
  2.4 0.7 %copy-start = (f32[6,4,8,256]{3,2,1,0:T(8,128)}, f32[6,4,8,256]{3,2,1,0:T(8,128)S(1)}, u32[]{:S(2)}) copy-start(f32[6,4,8,256]{3,2,1,0:T(8,128)S(1)} %collective-permute-done.oth_ref) | copy-start | bytes 589828
  5.0 7.4 %copy-start.3 = (f32[8,128]{1,0:T(8,128)S(1)}, f32[8,128]{1,0:T(8,128)}, u32[]{:S(2)}) copy-start(f32[8,128]{1,0:T(8,128)} %get-tuple-element.5) | copy-start | bytes 12292
  5.0 7.4 %collective-permute-start.3 = (f32[8,128]{1,0:T(8,128)}, f32[8,128]{1,0:T(8,128)S(1)}, u32[]{:S(2)}, u32[]{:S(2)}) collective-permute-start(f32[8,128]{1,0:T(8,128)} %get-tuple-element.5), channel_id=1, source_target_pairs={{1,3},{3,1},{5,7},{7,5},{9,11},{11,9},{13,15},{15,13},{17,19},{19,... | collective-permute-start | bytes 12296 | tf_op jit(solution)/shard_map/ppermute | solution.py:194
  6.5 9.9 %collective-permute-start.1 = (f32[6,4,8,256]{3,2,1,0:T(8,128)}, f32[6,4,8,256]{3,2,1,0:T(8,128)S(1)}, u32[]{:S(2)}, u32[]{:S(2)}) collective-permute-start(f32[6,4,8,256]{3,2,1,0:T(8,128)} %get-tuple-element.4), channel_id=1, source_target_pairs={{0,14},{1,3},{2,4},{3,1},{4,2},{5,7},{6,8},{7,5},{8,6},{9,11},{10,... | collective-permute-start | bytes 589832 | tf_op jit(solution)/shard_map/ppermute | solution.py:189
  12.4 0.7 %collective-permute-start.4 = (f32[16,128]{1,0:T(8,128)S(1)}, f32[16,128]{1,0:T(8,128)S(1)}, u32[]{:S(2)}, u32[]{:S(2)}) collective-permute-start(f32[16,128]{1,0:T(8,128)S(1)} %pad_maximum_fusion.1), channel_id=1, source_target_pairs={{1,5},{3,7},{5,1},{7,3},{9,13},{11,15},{13,9},{15,11},{17,21},{19,... | collective-permute-start | bytes 24584 | tf_op jit(solution)/shard_map/ppermute | solution.py:194
  13.1 0.7 %collective-permute-start.5 = (f32[32,128]{1,0:T(8,128)S(1)}, f32[32,128]{1,0:T(8,128)S(1)}, u32[]{:S(2)}, u32[]{:S(2)}) collective-permute-start(f32[32,128]{1,0:T(8,128)S(1)} %pad_maximum_fusion), channel_id=1, source_target_pairs={{1,9},{3,11},{5,13},{7,15},{9,1},{11,3},{13,5},{15,7},{17,25},{19,... | collective-permute-start | bytes 49160 | tf_op jit(solution)/shard_map/ppermute | solution.py:194
  13.8 9.3 %collective-permute-start.6 = (f32[64,128]{1,0:T(8,128)S(1)}, f32[64,128]{1,0:T(8,128)S(1)}, u32[]{:S(2)}, u32[]{:S(2)}) collective-permute-start(f32[64,128]{1,0:T(8,128)S(1)} %constant_dynamic-update-slice_fusion), channel_id=1, source_target_pairs={{1,0},{3,2},{5,4},{7,6},{9,8},{11,10},{13,12},{15,14},{17,16},{19,... | collective-permute-start | bytes 98312 | tf_op jit(solution)/shard_map/ppermute | solution.py:197
  16.4 7.3 %copy-start.1 = (f32[6,4,8,256]{3,2,1,0:T(8,128)}, f32[6,4,8,256]{3,2,1,0:T(8,128)S(1)}, u32[]{:S(2)}) copy-start(f32[6,4,8,256]{3,2,1,0:T(8,128)S(1)} %collective-permute-done.1.near_ref) | copy-start | bytes 589828
  16.4 7.3 %collective-permute-start.2 = (f32[6,4,8,256]{3,2,1,0:T(8,128)S(1)}, f32[6,4,8,256]{3,2,1,0:T(8,128)S(1)}, u32[]{:S(2)}, u32[]{:S(2)}) collective-permute-start(f32[6,4,8,256]{3,2,1,0:T(8,128)S(1)} %collective-permute-done.1.near_ref), channel_id=1, source_target_pairs={{0,1},{1,0},{2,3},{3,2},{4,5},{5,4},{6,7},{7,6},{8,9},{9,8},{10,11... | collective-permute-start | bytes 589832 | tf_op jit(solution)/shard_map/ppermute | solution.py:190
  23.7 0.7 %copy-start.2 = (f32[6,4,8,256]{3,2,1,0:T(8,128)}, f32[6,4,8,256]{3,2,1,0:T(8,128)S(1)}, u32[]{:S(2)}) copy-start(f32[6,4,8,256]{3,2,1,0:T(8,128)S(1)} %collective-permute-done.2.far_ref) | copy-start | bytes 589828

commit v2 on v1

--- a/solution.py
+++ b/solution.py
@@ -15,6 +15,7 @@
 HALO = 4
 ROWS = 8
 LANES = 128
+VMEM_LIMIT = 16 * 1024 * 1024
 
 
 def spectral_entry(shift, instances):
@@ -28,9 +29,13 @@
     return [(plane_no + 1) * axial_cells // (planes_count + 1) for plane_no in range(planes_count)]
 
 
+def stage_kernel(flow_ref, own_ref):
+    own_ref[...] = flow_ref[...]
+
+
 def pack_kernel(planes, own_ref, oth_ref, line_ref, edge_ref):
     core = lax.axis_index("inst")
-    low = lax.rem(lax.axis_index("space") + core, 2) == 0
+    low = lax.rem(lax.axis_index("space") + core, 2) == 1
     nvar, ninst = own_ref.shape[:2]
     lane = lax.broadcasted_iota(jnp.int32, (ROWS, LANES), 1)
     line = jnp.zeros((ROWS, LANES), jnp.float32)
@@ -80,7 +85,7 @@
 ):
     core = lax.axis_index("inst")
     space = lax.axis_index("space")
-    low = lax.rem(space + core, 2) == 0
+    low = lax.rem(space + core, 2) == 1
     nvar, ninst, _, axial = own_ref.shape
     row8 = lax.broadcasted_iota(jnp.int32, (ROWS, axial), 0)
     for v in range(nvar):
@@ -147,20 +152,37 @@
                 total += spectral_entry(n - j - ninst, 2 * ninst) * field_ref[1 - core, u, j]
             res_ref[u, n] = total
 
-    scale = 1.0 / (1.0 + 4.0 * SMOOTHING)
     step = step_ref[...]
+    lane = lax.broadcasted_iota(jnp.int32, (ROWS, axial), 1)
+    k = SMOOTHING / (1.0 + 4.0 * SMOOTHING)
+    base = 1.0 / (1.0 + 4.0 * SMOOTHING)
+    c0, c1, c2, c3 = base, base * k, base * k * k, k * k * k
     for n in range(ninst):
         for u in range(nvar):
-            res = res_ref[u, n]
-            s = res
-            for _ in range(SWEEPS):
-                pair = pltpu.roll(s, 2 * ROWS - 1, 0) + pltpu.roll(s, 1, 0)
+            r0 = res_ref[u, n]
+            r1 = pltpu.roll(r0, 2 * ROWS - 1, 0) + pltpu.roll(r0, 1, 0)
+            r2 = pltpu.roll(r1, 2 * ROWS - 1, 0) + pltpu.roll(r1, 1, 0)
+            r3 = pltpu.roll(r2, 2 * ROWS - 1, 0) + pltpu.roll(r2, 1, 0)
+            r0, r1, r2, r3 = (r[0:ROWS] for r in (r0, r1, r2, r3))
+            s = c3 * r0
+            for more in (
+                c2 * r0 + 3.0 * c3 * r1,
+                c1 * r0 + 2.0 * c2 * r1 + 3.0 * c3 * r2,
+                c0 * r0 + c1 * r1 + c2 * r2 + c3 * r3,
+            ):
                 prv = jnp.where(lane == 0, 0.0, pltpu.roll(s, 1, 1))
                 nxt = jnp.where(lane == axial - 1, 0.0, pltpu.roll(s, axial - 1, 1))
-                s = (res + SMOOTHING * (pair + prv + nxt)) * scale
-            smoothed = s[0:ROWS]
-            out_ref[u, n] = smoothed
-            new_ref[u, n] = own_ref[u, n] - step * smoothed
+                s = more + prv + nxt
+            out_ref[u, n] = s
+            new_ref[u, n] = own_ref[u, n] - step * s
+
+
+def here(array):
+    return pltpu.with_memory_space_constraint(array, pltpu.VMEM)
+
+
+def scalars(array):
+    return pltpu.with_memory_space_constraint(array, pltpu.SMEM)
 
 
 def shards(flow_state, jac_pitch, jac_axial, pseudo_step, partner, iface_index):
@@ -172,30 +194,39 @@
     smem = pl.BlockSpec(memory_space=pltpu.SMEM)
 
     other = lax.ppermute(flow_state, "inst", [(0, 1), (1, 0)])
+    own = pl.pallas_call(
+        stage_kernel,
+        out_shape=pltpu.VMEM(flow_state.shape, jnp.float32),
+        in_specs=[vmem],
+        out_specs=vmem,
+        compiler_params=pltpu.CompilerParams(vmem_limit_bytes=VMEM_LIMIT),
+    )(flow_state)
+    other = here(other)
     line, edge = pl.pallas_call(
         functools.partial(pack_kernel, planes),
         out_shape=(
-            jax.ShapeDtypeStruct((rows, LANES), jnp.float32),
-            jax.ShapeDtypeStruct((nvar, ninst, rows, axial), jnp.float32),
+            pltpu.VMEM((rows, LANES), jnp.float32),
+            pltpu.VMEM((nvar, ninst, rows, axial), jnp.float32),
         ),
         in_specs=[vmem, vmem],
         out_specs=(vmem, vmem),
-    )(flow_state, other)
+        compiler_params=pltpu.CompilerParams(vmem_limit_bytes=VMEM_LIMIT),
+    )(here(own), other)
 
     pairs = []
     for i in range(spaces):
         odd = (i + 1) % spaces if i % 2 else (i - 1) % spaces
-        pairs += [(2 * i, 2 * odd), (2 * i + 1, 2 * (i ^ 1) + 1)]
+        pairs += [(2 * i, 2 * (i ^ 1)), (2 * i + 1, 2 * odd + 1)]
     near = lax.ppermute(edge, both, pairs)
     far = lax.ppermute(near, "inst", [(0, 1), (1, 0)])
 
     lines, bit = line, 1
     while bit < spaces:
-        got = lax.ppermute(lines, both, [(2 * i + 1, 2 * (i ^ bit) + 1) for i in range(spaces)])
+        got = lax.ppermute(
+            lines, both, [(2 * i + c, 2 * (i ^ bit) + 1 - c) for i in range(spaces) for c in (0, 1)]
+        )
         lines = jnp.concatenate([lines, got], axis=0)
         bit *= 2
-    sent = lax.ppermute(lines, "inst", [(1, 0)])
-    lines = jnp.where(lax.axis_index("inst") == 0, sent, lines)
 
     return pl.pallas_call(
         functools.partial(step_kernel, planes, spaces),
@@ -205,14 +236,15 @@
         ),
         in_specs=[smem] * 4 + [vmem] * 6,
         out_specs=(vmem, vmem),
+        compiler_params=pltpu.CompilerParams(vmem_limit_bytes=VMEM_LIMIT),
         scratch_shapes=[
             pltpu.VMEM((2, nvar, ninst, 2 * rows, axial), jnp.float32),
             pltpu.VMEM((IFACES, 4 * rows + rows, LANES), jnp.float32),
             pltpu.VMEM((nvar, ninst, 2 * rows, axial), jnp.float32),
         ],
     )(
-        jac_pitch, jac_axial, partner, iface_index,
-        flow_state, other, near, far, lines, pseudo_step,
+        *[scalars(a) for a in (jac_pitch, jac_axial, partner, iface_index)],
+        here(own), other, here(near), here(far), here(lines), here(pseudo_step),
     )
 
 

time: 30.5 us -> 23.8 us (0.78)
  starting transfers between devices: 15.9 us -> 9.46 us
  waiting for transfers between devices: 3.12 us -> 7.52 us
  Pallas kernels: 7.81 us -> 5.06 us
  local copies, waits for them, and re-layouts: 2.06 us -> 0.95 us
  other arithmetic: 0.61 us -> 0.01 us
    ppermute x4 -> x3, waiting for transfers between devices: 0.59 us -> 7.18 us  [shards(): lax.ppermute(lines, both, [(2 * i + c, 2 * (i ^ bit) + 1 - c) for i in ra...]
    ppermute x1, starting transfers between devices: 6.13 us -> 0.01 us  [shards(): far = lax.ppermute(near, 'inst', [(0, 1), (1, 0)])]
    ppermute x1, starting transfers between devices: 5.9 us -> 2.9 us  [shards(): near = lax.ppermute(edge, both, pairs)]
    ppermute x4 -> x3, starting transfers between devices: 3.4 us -> 6.04 us  [shards(): lax.ppermute(lines, both, [(2 * i + c, 2 * (i ^ bit) + 1 - c) for i in ra...]
    pallas_call x1 -> x2, Pallas kernels: 1.9 us -> 0.25 us  [the longest x1 0.23 us: shards(): pl.pallas_call(functools.partial(pack_kernel, planes), out_shape=(pltpu.V...]
    ppermute x1, waiting for transfers between devices: 1.24 us -> 0.01 us  [shards(): near = lax.ppermute(edge, both, pairs)]
    unnamed x11 -> x12, local copies, waits for them, and re-layouts: 2.06 us -> 0.95 us
    pallas_call x1, Pallas kernels: 5.9 us -> 4.82 us  [shards(): pl.pallas_call(functools.partial(step_kernel, planes, spaces), out_shape=...]
  transfers between devices with their start and end apart: 7 -> 6, of which waited for: 3 -> 4; matrix products, arithmetic and copies ran while one was open for 4% -> 0% of each run, Pallas kernels for 0% -> 0%
where the time goes in v2:
time: 23.8 us; the launch traced here: 23.7 us
  starting transfers between devices  9.46 us (40%)
  waiting for transfers between devices  7.52 us (32%)
  Pallas kernels  5.06 us (21%)
  local copies, waits for them, and re-layouts  0.95 us (4%)
  between operations  0.7 us (3%)
    ppermute x3, waiting for transfers between devices, shards(): lax.ppermute(lines, both, [(2 * i + c, 2 * (i ^ bit) + 1 - c) for i in ra...  7.18 us
    ppermute x3, starting transfers between devices, shards(): lax.ppermute(lines, both, [(2 * i + c, 2 * (i ^ bit) + 1 - c) for i in ra...  6.04 us
    pallas_call x1, Pallas kernels, shards(): pl.pallas_call(functools.partial(step_kernel, planes, spaces), out_shape=...  4.82 us
    ppermute x1, starting transfers between devices, shards(): near = lax.ppermute(edge, both, pairs)  2.9 us
    unnamed x12, local copies, waits for them, and re-layouts  0.95 us
    ppermute x1, starting transfers between devices, shards(): other = lax.ppermute(flow_state, 'inst', [(0, 1), (1, 0)])  0.52 us
  transfers between devices with their start and end apart: 6, of which 4 were waited for; matrix products, arithmetic and copies ran while one was open for 0% of the time, Pallas kernels for 0%

profile of v2, /device:TPU:0, one launch (start us, length us, event | category | flops | bytes accessed | tf_op | source)
XLA Modules:
  0.0 23.7 jit_solution(17983583277624546331)
XLA Ops:
  0.6 0.5 %collective-permute-start = (f32[6,4,8,256]{3,2,1,0:T(8,128)}, f32[6,4,8,256]{3,2,1,0:T(8,128)S(1)}, u32[]{:S(2)}, u32[]{:S(2)}) collective-permute-start(f32[6,4,8,256]{3,2,1,0:T(8,128)} %flow_ref.1), channel_id=1, source_target_pairs={{0,1},{1,0},{2,3},{3,2},{4,5},{5,4},{6,7},{7,6},{8,9},{9,8},{10,11... | collective-permute-start | bytes 589832 | tf_op jit(solution)/shard_map/ppermute | solution.py:196
  1.1 0.0 copy-start
  1.1 0.9 %copy-done = f32[6,4,8,256]{3,2,1,0:T(8,128)S(1)} copy-done((f32[6,4,8,256]{3,2,1,0:T(8,128)S(1)}, f32[6,4,8,256]{3,2,1,0:T(8,128)}, u32[]{:S(2)}) %copy-start) | copy-done | bytes 196632
  2.1 0.3 %collective-permute-done.oth_ref = f32[6,4,8,256]{3,2,1,0:T(8,128)S(1)} collective-permute-done((f32[6,4,8,256]{3,2,1,0:T(8,128)}, f32[6,4,8,256]{3,2,1,0:T(8,128)S(1)}, u32[]{:S(2)}, u32[]{:S(2)}) %collective-permute-start) | collective-permute-done | bytes 196640 | tf_op jit(solution)/shard_map/ppermute | solution.py:196
  2.4 0.2 shard_map.78
  2.7 2.9 %collective-permute-start.1 = (f32[6,4,8,256]{3,2,1,0:T(8,128)S(1)}, f32[6,4,8,256]{3,2,1,0:T(8,128)S(1)}, u32[]{:S(2)}, u32[]{:S(2)}) collective-permute-start(f32[6,4,8,256]{3,2,1,0:T(8,128)S(1)} %get-tuple-element.4), channel_id=1, source_target_pairs={{0,2},{1,15},{2,0},{3,5},{4,6},{5,3},{6,4},{7,9},{8,10},{9,7},{10,... | collective-permute-start | bytes 589832 | tf_op jit(solution)/shard_map/ppermute | solution.py:220
  5.6 1.0 %collective-permute-start.3 = (f32[8,128]{1,0:T(8,128)S(1)}, f32[8,128]{1,0:T(8,128)S(1)}, u32[]{:S(2)}, u32[]{:S(2)}) collective-permute-start(f32[8,128]{1,0:T(8,128)S(1)} %get-tuple-element.5), channel_id=1, source_target_pairs={{0,3},{1,2},{2,1},{3,0},{4,7},{5,6},{6,5},{7,4},{8,11},{9,10},{10,... | collective-permute-start | bytes 12296 | tf_op jit(solution)/shard_map/ppermute | solution.py:225
  6.6 4.4 %collective-permute-done.3 = f32[8,128]{1,0:T(8,128)S(1)} collective-permute-done((f32[8,128]{1,0:T(8,128)S(1)}, f32[8,128]{1,0:T(8,128)S(1)}, u32[]{:S(2)}, u32[]{:S(2)}) %collective-permute-start.3) | collective-permute-done | bytes 4128 | tf_op jit(solution)/shard_map/ppermute | solution.py:225
  10.9 2.2 %collective-permute-start.4 = (f32[16,128]{1,0:T(8,128)S(1)}, f32[16,128]{1,0:T(8,128)S(1)}, u32[]{:S(2)}, u32[]{:S(2)}) collective-permute-start(f32[16,128]{1,0:T(8,128)S(1)} %pad_maximum_fusion.2), channel_id=1, source_target_pairs={{0,5},{1,4},{2,7},{3,6},{4,1},{5,0},{6,3},{7,2},{8,13},{9,12},{10,... | collective-permute-start | bytes 24584 | tf_op jit(solution)/shard_map/ppermute | solution.py:225
  13.2 0.0 collective-permute-done.1.near_ref
  13.2 0.0 collective-permute-start.2
  13.2 1.4 %collective-permute-done.4 = f32[16,128]{1,0:T(8,128)S(1)} collective-permute-done((f32[16,128]{1,0:T(8,128)S(1)}, f32[16,128]{1,0:T(8,128)S(1)}, u32[]{:S(2)}, u32[]{:S(2)}) %collective-permute-start.4) | collective-permute-done | bytes 8224 | tf_op jit(solution)/shard_map/ppermute | solution.py:225
  14.6 0.0 copy-start.1
  14.6 0.0 copy-start.2
  14.6 0.0 copy-start.3
  14.6 0.0 copy-start.4
  14.6 0.0 copy-start.5
  14.6 2.8 %collective-permute-start.5 = (f32[32,128]{1,0:T(8,128)S(1)}, f32[32,128]{1,0:T(8,128)S(1)}, u32[]{:S(2)}, u32[]{:S(2)}) collective-permute-start(f32[32,128]{1,0:T(8,128)S(1)} %pad_maximum_fusion.1), channel_id=1, source_target_pairs={{0,9},{1,8},{2,11},{3,10},{4,13},{5,12},{6,15},{7,14},{8,1},{9,0},... | collective-permute-start | bytes 49160 | tf_op jit(solution)/shard_map/ppermute | solution.py:225
  17.4 1.4 %collective-permute-done.5 = f32[32,128]{1,0:T(8,128)S(1)} collective-permute-done((f32[32,128]{1,0:T(8,128)S(1)}, f32[32,128]{1,0:T(8,128)S(1)}, u32[]{:S(2)}, u32[]{:S(2)}) %collective-permute-start.5) | collective-permute-done | bytes 16416 | tf_op jit(solution)/shard_map/ppermute | solution.py:225
  18.8 0.0 collective-permute-done.2.far_ref
  18.8 0.0 copy-done.1
  18.8 0.0 copy-done.2
  18.9 0.0 copy-done.3
  18.9 0.0 copy-done.4
  18.9 0.0 copy-done.5
  18.9 4.8 %shard_map.79 = (f32[6,4,8,256]{3,2,1,0:T(8,128)}, f32[6,4,8,256]{3,2,1,0:T(8,128)}) custom-call(f32[6,6]{1,0:T(8,128)S(1)} %copy-done.2, f32[6,6]{1,0:T(8,128)S(1)} %copy-done.3, s32[2,8]{1,0:T(2,128)S(1)} %copy-done.4, s32[2,8]{1,0:T(2,128)S(1)} %copy-done.5, f32[6,4,8,256]{3,2,1,0:T(8,128)S(1)} %shard_map.77.own_ref, ...), custom_call_target="tpu_custom_call" | custom-call | tf_op jit(solution)/shard_map/pallas_call | solution.py:231
  (4 shorter events, 0.0 us)
Async XLA Ops:
  0.6 1.8 %collective-permute-start = (f32[6,4,8,256]{3,2,1,0:T(8,128)}, f32[6,4,8,256]{3,2,1,0:T(8,128)S(1)}, u32[]{:S(2)}, u32[]{:S(2)}) collective-permute-start(f32[6,4,8,256]{3,2,1,0:T(8,128)} %flow_ref.1), channel_id=1, source_target_pairs={{0,1},{1,0},{2,3},{3,2},{4,5},{5,4},{6,7},{7,6},{8,9},{9,8},{10,11... | collective-permute-start | bytes 589832 | tf_op jit(solution)/shard_map/ppermute | solution.py:196
  1.1 0.9 %copy-start = (f32[6,4,8,256]{3,2,1,0:T(8,128)S(1)}, f32[6,4,8,256]{3,2,1,0:T(8,128)}, u32[]{:S(2)}) copy-start(f32[6,4,8,256]{3,2,1,0:T(8,128)} %flow_ref.1) | copy-start | bytes 589828
  2.7 10.5 %collective-permute-start.1 = (f32[6,4,8,256]{3,2,1,0:T(8,128)S(1)}, f32[6,4,8,256]{3,2,1,0:T(8,128)S(1)}, u32[]{:S(2)}, u32[]{:S(2)}) collective-permute-start(f32[6,4,8,256]{3,2,1,0:T(8,128)S(1)} %get-tuple-element.4), channel_id=1, source_target_pairs={{0,2},{1,15},{2,0},{3,5},{4,6},{5,3},{6,4},{7,9},{8,10},{9,7},{10,... | collective-permute-start | bytes 589832 | tf_op jit(solution)/shard_map/ppermute | solution.py:220
  5.6 5.4 %collective-permute-start.3 = (f32[8,128]{1,0:T(8,128)S(1)}, f32[8,128]{1,0:T(8,128)S(1)}, u32[]{:S(2)}, u32[]{:S(2)}) collective-permute-start(f32[8,128]{1,0:T(8,128)S(1)} %get-tuple-element.5), channel_id=1, source_target_pairs={{0,3},{1,2},{2,1},{3,0},{4,7},{5,6},{6,5},{7,4},{8,11},{9,10},{10,... | collective-permute-start | bytes 12296 | tf_op jit(solution)/shard_map/ppermute | solution.py:225
  10.9 3.6 %collective-permute-start.4 = (f32[16,128]{1,0:T(8,128)S(1)}, f32[16,128]{1,0:T(8,128)S(1)}, u32[]{:S(2)}, u32[]{:S(2)}) collective-permute-start(f32[16,128]{1,0:T(8,128)S(1)} %pad_maximum_fusion.2), channel_id=1, source_target_pairs={{0,5},{1,4},{2,7},{3,6},{4,1},{5,0},{6,3},{7,2},{8,13},{9,12},{10,... | collective-permute-start | bytes 24584 | tf_op jit(solution)/shard_map/ppermute | solution.py:225
  13.2 5.6 %collective-permute-start.2 = (f32[6,4,8,256]{3,2,1,0:T(8,128)S(1)}, f32[6,4,8,256]{3,2,1,0:T(8,128)S(1)}, u32[]{:S(2)}, u32[]{:S(2)}) collective-permute-start(f32[6,4,8,256]{3,2,1,0:T(8,128)S(1)} %collective-permute-done.1.near_ref), channel_id=1, source_target_pairs={{0,1},{1,0},{2,3},{3,2},{4,5},{5,4},{6,7},{7,6},{8,9},{9,8},{10,11... | collective-permute-start | bytes 589832 | tf_op jit(solution)/shard_map/ppermute | solution.py:221
  14.6 4.3 %copy-start.1 = (f32[8,256]{1,0:T(8,128)S(1)}, f32[8,256]{1,0:T(8,128)}, u32[]{:S(2)}) copy-start(f32[8,256]{1,0:T(8,128)} %step_ref.1) | copy-start | bytes 24580
  14.6 4.3 %copy-start.2 = (f32[6,6]{1,0:T(8,128)S(1)}, f32[6,6]{1,0:T(8,128)}, u32[]{:S(2)}) copy-start(f32[6,6]{1,0:T(8,128)} %jac_pitch_ref.1) | copy-start | bytes 436
  14.6 4.3 %copy-start.3 = (f32[6,6]{1,0:T(8,128)S(1)}, f32[6,6]{1,0:T(8,128)}, u32[]{:S(2)}) copy-start(f32[6,6]{1,0:T(8,128)} %jac_axial_ref.1) | copy-start | bytes 436
  14.6 4.3 %copy-start.4 = (s32[2,8]{1,0:T(2,128)S(1)}, s32[2,8]{1,0:T(2,128)}, u32[]{:S(2)}) copy-start(s32[2,8]{1,0:T(2,128)} %partner_ref.1) | copy-start | bytes 196
  14.6 4.3 %copy-start.5 = (s32[2,8]{1,0:T(2,128)S(1)}, s32[2,8]{1,0:T(2,128)}, u32[]{:S(2)}) copy-start(s32[2,8]{1,0:T(2,128)} %index_ref.1) | copy-start | bytes 196
  14.6 4.2 %collective-permute-start.5 = (f32[32,128]{1,0:T(8,128)S(1)}, f32[32,128]{1,0:T(8,128)S(1)}, u32[]{:S(2)}, u32[]{:S(2)}) collective-permute-start(f32[32,128]{1,0:T(8,128)S(1)} %pad_maximum_fusion.1), channel_id=1, source_target_pairs={{0,9},{1,8},{2,11},{3,10},{4,13},{5,12},{6,15},{7,14},{8,1},{9,0},... | collective-permute-start | bytes 49160 | tf_op jit(solution)/shard_map/ppermute | solution.py:225

commit v3 on v2

v3 whole, which is shorter than its diff:
```python
import functools
import math

import jax
import jax.numpy as jnp
from jax import lax
from jax.experimental import pallas as pl
from jax.experimental.pallas import tpu as pltpu
from jax.sharding import PartitionSpec as P

IFACES = 2
SWEEPS = 3
VISCOUS = 0.25
SMOOTHING = 1.0
HALO = 4
ROWS = 8
LANES = 128
GROUP = 8
VMEM_LIMIT = 16 * 1024 * 1024


def spectral_entry(shift, instances):
    shift %= instances
    if shift == 0:
        return 0.0
    return 0.5 * (-1) ** shift / math.tan(math.pi * shift / instances)


def interface_planes(axial_cells, planes_count):
    return [(plane_no + 1) * axial_cells // (planes_count + 1) for plane_no in range(planes_count)]


def sweep_weights():
    k = SMOOTHING / (1.0 + 4.0 * SMOOTHING)
    base = 1.0 / (1.0 + 4.0 * SMOOTHING)
    return [base * k**m for m in range(SWEEPS)] + [k**SWEEPS]


def spread_weight(m, distance):
    weights = sweep_weights() + [0.0] * 4
    paths = {0: {0: 1, 2: 2}, 1: {1: 1, 3: 3}, 2: {2: 1}, 3: {3: 1}}[distance]
    return sum(count * math.comb(m + j, m) * weights[m + j] for j, count in paths.items())


def round_bits(spaces):
    bits = list(range(spaces.bit_length() - 1))
    return bits[1:] + bits[:1]


def stage_kernel(flow_ref, own_ref):
    own_ref[...] = flow_ref[...]


def line_kernel(planes, own_ref, oth_ref, line_ref):
    core = lax.axis_index("inst")
    nvar, ninst = own_ref.shape[:2]
    lane = lax.broadcasted_iota(jnp.int32, (ROWS, LANES), 1)
    line = jnp.zeros((ROWS, LANES), jnp.float32)
    for plane_no, plane in enumerate(planes):
        for v in range(nvar):
            for half, ref in enumerate((own_ref, oth_ref)):
                for n in range(ninst):
                    at = (plane_no * nvar + v) * 2 * ninst + half * ninst + n
                    cell = jnp.broadcast_to(ref[v, n, :, plane - 1 : plane], (ROWS, LANES))
                    line = jnp.where(lane == at, cell, line)
    swapped = jnp.where(
        lax.rem(lane, 2 * ninst) < ninst,
        pltpu.roll(line, LANES - ninst, 1),
        pltpu.roll(line, ninst, 1),
    )
    line_ref[...] = jnp.where(core == 0, line, swapped)


def low_side():
    return lax.rem(lax.axis_index("space") + lax.axis_index("inst"), 2) == 1


def edge_kernel(own_ref, oth_ref, after_ref, edge_ref):
    del after_ref
    core = lax.axis_index("inst")
    low = low_side()
    nvar, ninst, _, axial = own_ref.shape
    row = lax.broadcasted_iota(jnp.int32, (ROWS, axial), 0)
    for v in range(nvar):
        for n in range(ninst):
            own, oth = own_ref[v, n], oth_ref[v, n]
            first = jnp.where(core == 0, own, oth)
            second = jnp.where(core == 0, oth, own)
            low_rows = jnp.where(row < HALO, first, pltpu.roll(second, HALO, 0))
            high_rows = jnp.where(row < HALO, pltpu.roll(first, HALO, 0), second)
            edge_ref[v, n] = jnp.where(low, low_rows, high_rows)


def local_terms(planes, jac, own, oth, n):
    nvar, ninst, rows, axial = own.shape
    lane = lax.broadcasted_iota(jnp.int32, (rows, axial), 1)
    inward, spread = [], []
    for v in range(nvar):
        c = own[v, n]
        up, down = pltpu.roll(c, 1, 1), pltpu.roll(c, axial - 1, 1)
        for plane in [0, *planes]:
            up = jnp.where(lane == plane, 0.0, up)
        for plane in [*planes, axial]:
            down = jnp.where(lane == plane - 1, c, down)
        inward.append(c - up)
        spread.append(up + down - 4.0 * c)
    terms = []
    for u in range(nvar):
        total = -VISCOUS * spread[u]
        for v in range(nvar):
            total += jac(u, v) * inward[v]
        for j in range(ninst):
            if j != n:
                total += spectral_entry(n - j, 2 * ninst) * own[u, j]
            total += spectral_entry(n - j - ninst, 2 * ninst) * oth[u, j]
        terms.append(total)
    return terms


def prepare_kernel(
    planes,
    spaces,
    jac_pitch_ref,
    jac_axial_ref,
    partner_ref,
    index_ref,
    own_ref,
    oth_ref,
    after_ref,
    local_ref,
    jac_ref,
    pick_ref,
    mix_ref,
):
    del after_ref
    core, space = lax.axis_index("inst"), lax.axis_index("space")
    nvar, ninst, _, axial = own_ref.shape
    for n in range(ninst):
        terms = local_terms(planes, lambda u, v: jac_axial_ref[u, v], own_ref, oth_ref, n)
        for u in range(nvar):
            local_ref[u, n] = terms[u]
    for which, ref in enumerate((jac_pitch_ref, jac_axial_ref)):
        for u in range(nvar):
            for v in range(nvar):
                at = (which * nvar + u) * nvar + v
                jac_ref[at : at + 1, :] = jnp.full((1, axial), ref[u, v], jnp.float32)

    total = spaces * ROWS
    row = lax.broadcasted_iota(jnp.int32, (2 * ROWS, total), 0)
    ahead = jnp.where(row < ROWS + HALO, row, row - 2 * ROWS)
    lane = lax.broadcasted_iota(jnp.int32, (2 * ROWS, total), 1)
    for plane_no in range(len(planes)):
        pitch = index_ref[plane_no, 0] + ahead
        pitch = jnp.where(pitch < 0, pitch + total, pitch)
        pitch = jnp.where(pitch >= total, pitch - total, pitch)
        apart = (pitch >> 3) ^ space
        place = pitch & 7
        for turn, bit in enumerate(round_bits(spaces)):
            place += ((apart >> bit) & 1) << (turn + 3)
        pick_ref[pl.ds(plane_no * 2 * ROWS, 2 * ROWS), :] = jnp.where(lane == place, 1.0, 0.0)

    lane = lax.broadcasted_iota(jnp.int32, (ROWS, 2 * LANES), 1) // GROUP
    row = lax.broadcasted_iota(jnp.int32, (ROWS, 2 * LANES), 0)
    to_var, to_inst = lane // ninst, lax.rem(lane, ninst) + ninst * core
    mix_ref[...] = jnp.zeros(mix_ref.shape, jnp.float32)
    for v in range(nvar):
        block = jnp.zeros((ROWS, 2 * LANES), jnp.float32)
        for u in range(nvar):
            value = -jac_axial_ref[u, v] - (VISCOUS if u == v else 0.0)
            block = jnp.where(to_var == u, value, block)
        for plane_no in range(len(planes)):
            source = lax.rem(to_inst + partner_ref[plane_no, 0], 2 * ninst)
            at = (plane_no * nvar + v) * 2 * ninst
            mix_ref[plane_no, at : at + ROWS, :] = jnp.where(row == source, block, 0.0)


def sweep_kernel(
    planes, own_ref, oth_ref, near_ref, *refs
):
    *far_refs, local_ref, jac_ref, swept_ref, halo_own, halo_oth = refs
    core = lax.axis_index("inst")
    low = low_side()
    nvar, ninst, _, axial = own_ref.shape
    cut = nvar // len(far_refs)
    row = lax.broadcasted_iota(jnp.int32, (ROWS, axial), 0)
    for v in range(nvar):
        for n in range(ninst):
            near, far = near_ref[v, n], far_refs[v // cut][v % cut, n]
            below = jnp.where(low, near, far)
            above = jnp.where(low, far, near)
            first = jnp.where(row < HALO, above, pltpu.roll(below, HALO, 0))
            second = jnp.where(row < HALO, pltpu.roll(above, HALO, 0), below)
            halo_own[v, n] = jnp.where(core == 0, first, second)
            halo_oth[v, n] = jnp.where(core == 0, second, first)
    c0, c1, c2, c3 = sweep_weights()
    lane = lax.broadcasted_iota(jnp.int32, (ROWS, axial), 1)

    def jac(which, u, v):
        at = (which * nvar + u) * nvar + v
        return jac_ref[at : at + 1, :]

    for n in range(ninst):
        terms = local_terms(planes, functools.partial(jac, 1), halo_own, halo_oth, n)
        slope, spread = [], []
        for v in range(nvar):
            c = jnp.concatenate([own_ref[v, n], halo_own[v, n]], axis=0)
            nxt, prv = pltpu.roll(c, 2 * ROWS - 1, 0), pltpu.roll(c, 1, 0)
            slope.append(0.5 * (nxt - prv))
            spread.append(nxt + prv)
        for u in range(nvar):
            r0 = jnp.concatenate([local_ref[u, n], terms[u]], axis=0) - VISCOUS * spread[u]
            for v in range(nvar):
                r0 += jac(0, u, v) * slope[v]
            r1 = pltpu.roll(r0, 2 * ROWS - 1, 0) + pltpu.roll(r0, 1, 0)
            r2 = pltpu.roll(r1, 2 * ROWS - 1, 0) + pltpu.roll(r1, 1, 0)
            r3 = pltpu.roll(r2, 2 * ROWS - 1, 0) + pltpu.roll(r2, 1, 0)
            r0, r1, r2, r3 = (r[0:ROWS] for r in (r0, r1, r2, r3))
            s = c3 * r0
            for more in (
                c2 * r0 + 3.0 * c3 * r1,
                c1 * r0 + 2.0 * c2 * r1 + 3.0 * c3 * r2,
                c0 * r0 + c1 * r1 + c2 * r2 + c3 * r3,
            ):
                prv = jnp.where(lane == 0, 0.0, pltpu.roll(s, 1, 1))
                nxt = jnp.where(lane == axial - 1, 0.0, pltpu.roll(s, axial - 1, 1))
                s = more + prv + nxt
            swept_ref[u, n] = s


def finish_kernel(
    planes, own_ref, swept_ref, lines_ref, pick_ref, mix_ref, step_ref, new_ref, out_ref
):
    nvar, ninst, _, axial = own_ref.shape
    exact = dict(precision=lax.Precision.HIGHEST, preferred_element_type=jnp.float32)
    facing = jnp.dot(pick_ref[...], lines_ref[...], **exact)
    lane = lax.rem(lax.broadcasted_iota(jnp.int32, (ROWS, 2 * LANES), 1), GROUP)
    spread = []
    for plane_no in range(len(planes)):
        power = jnp.dot(
            facing[plane_no * 2 * ROWS : (plane_no + 1) * 2 * ROWS], mix_ref[plane_no], **exact
        )
        total = jnp.zeros((ROWS, 2 * LANES), jnp.float32)
        for m in range(SWEEPS + 1):
            weight = jnp.zeros((ROWS, 2 * LANES), jnp.float32)
            for d in range(-SWEEPS, SWEEPS + 1):
                weight = jnp.where(lane == d + SWEEPS, spread_weight(m, abs(d)), weight)
            total += weight * power[0:ROWS]
            if m < SWEEPS:
                power = pltpu.roll(power, 2 * ROWS - 1, 0) + pltpu.roll(power, 1, 0)
        spread.append(total)
    step = step_ref[...]
    lane = lax.broadcasted_iota(jnp.int32, (ROWS, LANES), 1)
    for n in range(ninst):
        for u in range(nvar):
            tiles = [swept_ref[u, n, :, t : t + LANES] for t in range(0, axial, LANES)]
            group = (u * ninst + n) * GROUP
            for plane_no, plane in enumerate(planes):
                tile, at = divmod(plane - SWEEPS, LANES)
                assert at + GROUP <= LANES
                start = group // LANES * LANES
                moved = pltpu.roll(
                    spread[plane_no][:, start : start + LANES], (at - group) % LANES, 1
                )
                inside = (lane >= at) & (lane < at + GROUP)
                tiles[tile] = tiles[tile] + jnp.where(inside, moved, 0.0)
            swept = jnp.concatenate(tiles, axis=1)
            out_ref[u, n] = swept
            new_ref[u, n] = own_ref[u, n] - step * swept


def here(array):
    return pltpu.with_memory_space_constraint(array, pltpu.VMEM)


def shards(flow_state, jac_pitch, jac_axial, pseudo_step, partner, iface_index):
    nvar, ninst, rows, axial = flow_state.shape
    spaces = lax.axis_size("space")
    planes = interface_planes(axial, IFACES)
    both = ("space", "inst")
    vmem = pl.BlockSpec(memory_space=pltpu.VMEM)
    smem = pl.BlockSpec(memory_space=pltpu.SMEM)
    anywhere = pl.BlockSpec(memory_space=pl.ANY)
    params = pltpu.CompilerParams(vmem_limit_bytes=VMEM_LIMIT)
    block = pltpu.VMEM(flow_state.shape, jnp.float32)
    cores = [(0, 1), (1, 0)]

    other = here(lax.ppermute(flow_state, "inst", cores))
    own = here(
        pl.pallas_call(
            stage_kernel, out_shape=block, in_specs=[vmem], out_specs=vmem, compiler_params=params
        )(flow_state)
    )
    line = pl.pallas_call(
        functools.partial(line_kernel, planes),
        out_shape=pltpu.VMEM((rows, LANES), jnp.float32),
        in_specs=[vmem, vmem],
        out_specs=vmem,
        compiler_params=params,
    )(own, other)

    lines, got = line, []
    for bit in round_bits(spaces):
        got.append(
            lax.ppermute(
                lines, both, [(2 * i + c, 2 * (i ^ (1 << bit)) + 1 - c) for i in range(spaces) for c in (0, 1)]
            )
        )
        lines = jnp.concatenate([lines, got[-1]], axis=0)

    edge = pl.pallas_call(
        edge_kernel,
        out_shape=block,
        in_specs=[vmem, vmem, anywhere],
        out_specs=vmem,
        compiler_params=params,
    )(own, other, line)
    pairs = []
    for i in range(spaces):
        odd = (i + 1) % spaces if i % 2 else (i - 1) % spaces
        pairs += [(2 * i, 2 * (i ^ 1)), (2 * i + 1, 2 * odd + 1)]
    near = lax.ppermute(edge, both, pairs)
    cut = nvar // 2
    far = [
        here(lax.ppermute(near[v : v + cut], "inst", cores)) for v in range(0, nvar, cut)
    ]

    local, jac, pick, mix = pl.pallas_call(
        functools.partial(prepare_kernel, planes, spaces),
        out_shape=(
            block,
            pltpu.VMEM((2 * nvar * nvar, axial), jnp.float32),
            pltpu.VMEM((IFACES * 2 * rows, spaces * rows), jnp.float32),
            pltpu.VMEM((IFACES, LANES, 2 * LANES), jnp.float32),
        ),
        in_specs=[smem] * 4 + [vmem] * 2 + [anywhere],
        out_specs=(vmem,) * 4,
        compiler_params=params,
    )(jac_pitch, jac_axial, partner, iface_index, own, other, got[0])

    swept = pl.pallas_call(
        functools.partial(sweep_kernel, planes),
        out_shape=block,
        in_specs=[vmem] * (5 + len(far)),
        out_specs=vmem,
        scratch_shapes=[block, block],
        compiler_params=params,
    )(own, other, here(near), *far, here(local), here(jac))

    return pl.pallas_call(
        functools.partial(finish_kernel, planes),
        out_shape=(jax.ShapeDtypeStruct(flow_state.shape, jnp.float32),) * 2,
        in_specs=[vmem] * 6,
        out_specs=(vmem, vmem),
        compiler_params=params,
    )(own, here(swept), here(lines), here(pick), here(mix), here(pseudo_step))


def solution(mesh):
    in_specs = (
        P("groups", "inst", "space", None),
        P("groups", None),
        P("groups", None),
        P("space", "groups"),
        P("groups", None),
        P("groups", "space"),
    )
    out_specs = (P("groups", "inst", "space", None), P("groups", "inst", "space", None))
    return jax.shard_map(shards, mesh=mesh, in_specs=in_specs, out_specs=out_specs, check_vma=False)
```

time: 23.8 us -> 18.7 us (0.79)
  waiting for transfers between devices: 7.52 us -> 2.68 us
  Pallas kernels: 5.06 us -> 4.21 us
  starting transfers between devices: 9.46 us -> 9.97 us
    ppermute x5 -> x6, waiting for transfers between devices: 7.51 us -> 2.68 us  [the longest x3 2 us: shards(): lax.ppermute(lines, both, [(2 * i + c, 2 * (i ^ 1 << bit) + 1 - c) for i...]
    ppermute x5 -> x6, starting transfers between devices: 6.56 us -> 8.41 us  [the longest x3 7.32 us: shards(): lax.ppermute(lines, both, [(2 * i + c, 2 * (i ^ 1 << bit) + 1 - c) for i...]
    ppermute x1, starting transfers between devices: 2.9 us -> 1.56 us  [shards(): near = lax.ppermute(edge, both, pairs)]
    pallas_call x3 -> x6, Pallas kernels: 5.06 us -> 4.21 us  [the longest x1 1.57 us: shards(): pl.pallas_call(functools.partial(sweep_kernel, planes), out_shape=block,...]
  transfers between devices with their start and end apart: 6 -> 7, of which waited for: 4 -> 4; matrix products, arithmetic and copies ran while one was open for 0% -> 0% of each run, Pallas kernels for 0% -> 6%
where the time goes in v3:
time: 18.7 us; the launch traced here: 18.5 us
  starting transfers between devices  9.97 us (53%)
  Pallas kernels  4.21 us (23%)
  waiting for transfers between devices  2.68 us (14%)
  local copies, waits for them, and re-layouts  0.97 us (5%)
  between operations  0.71 us (4%)
    ppermute x3, starting transfers between devices, shards(): lax.ppermute(lines, both, [(2 * i + c, 2 * (i ^ 1 << bit) + 1 - c) for i...  7.32 us
    ppermute x3, waiting for transfers between devices, shards(): lax.ppermute(lines, both, [(2 * i + c, 2 * (i ^ 1 << bit) + 1 - c) for i...  2 us
    pallas_call x1, Pallas kernels, shards(): pl.pallas_call(functools.partial(sweep_kernel, planes), out_shape=block,...  1.57 us
    ppermute x1, starting transfers between devices, shards(): near = lax.ppermute(edge, both, pairs)  1.56 us
    pallas_call x1, Pallas kernels, shards(): pl.pallas_call(functools.partial(finish_kernel, planes), out_shape=(jax.S...  1.26 us
    pallas_call x1, Pallas kernels, shards(): pl.pallas_call(functools.partial(prepare_kernel, planes, spaces), out_sha...  1.08 us
    unnamed x12, local copies, waits for them, and re-layouts  0.96 us
    ppermute x2, starting transfers between devices, shards(): lax.ppermute(near[v:v + cut], 'inst', cores)  0.58 us
  transfers between devices with their start and end apart: 7, of which 4 were waited for; matrix products, arithmetic and copies ran while one was open for 0% of the time, Pallas kernels for 6%

profile of v3, /device:TPU:0, one launch (start us, length us, event | category | flops | bytes accessed | tf_op | source)
XLA Modules:
  0.0 18.5 jit_solution(5153867219293587564)
XLA Ops:
  0.6 0.5 %collective-permute-start = (f32[6,4,8,256]{3,2,1,0:T(8,128)}, f32[6,4,8,256]{3,2,1,0:T(8,128)S(1)}, u32[]{:S(2)}, u32[]{:S(2)}) collective-permute-start(f32[6,4,8,256]{3,2,1,0:T(8,128)} %flow_ref.1), channel_id=1, source_target_pairs={{0,1},{1,0},{2,3},{3,2},{4,5},{5,4},{6,7},{7,6},{8,9},{9,8},{10,11... | collective-permute-start | bytes 589832 | tf_op jit(solution)/shard_map/ppermute | solution.py:287
  1.1 0.0 copy-start
  1.1 0.9 %copy-done = f32[6,4,8,256]{3,2,1,0:T(8,128)S(1)} copy-done((f32[6,4,8,256]{3,2,1,0:T(8,128)S(1)}, f32[6,4,8,256]{3,2,1,0:T(8,128)}, u32[]{:S(2)}) %copy-start) | copy-done | bytes 196632
  2.1 0.3 %collective-permute-done.oth_ref = f32[6,4,8,256]{3,2,1,0:T(8,128)S(1)} collective-permute-done((f32[6,4,8,256]{3,2,1,0:T(8,128)}, f32[6,4,8,256]{3,2,1,0:T(8,128)S(1)}, u32[]{:S(2)}, u32[]{:S(2)}) %collective-permute-start) | collective-permute-done | bytes 196640 | tf_op jit(solution)/shard_map/ppermute | solution.py:287
  2.4 0.2 %shard_map.78.after_ref = f32[8,128]{1,0:T(8,128)S(1)} custom-call(f32[6,4,8,256]{3,2,1,0:T(8,128)S(1)} %shard_map.77.own_ref, f32[6,4,8,256]{3,2,1,0:T(8,128)S(1)} %collective-permute-done.oth_ref), custom_call_target="tpu_custom_call" | custom-call | tf_op jit(solution)/shard_map/pallas_call | solution.py:293
  2.7 2.7 %collective-permute-start.4 = (f32[8,128]{1,0:T(8,128)S(1)}, f32[8,128]{1,0:T(8,128)S(1)}, u32[]{:S(2)}, u32[]{:S(2)}) collective-permute-start(f32[8,128]{1,0:T(8,128)S(1)} %shard_map.78.after_ref), channel_id=1, source_target_pairs={{0,5},{1,4},{2,7},{3,6},{4,1},{5,0},{6,3},{7,2},{8,13},{9,12},{10,... | collective-permute-start | bytes 12296 | tf_op jit(solution)/shard_map/ppermute | solution.py:304
  5.4 0.1 shard_map.79
  5.4 0.0 copy-start.2
  5.4 0.0 copy-start.3
  5.4 0.0 copy-start.4
  5.4 0.0 copy-start.5
  5.5 1.6 %collective-permute-start.1 = (f32[6,4,8,256]{3,2,1,0:T(8,128)S(1)}, f32[6,4,8,256]{3,2,1,0:T(8,128)S(1)}, u32[]{:S(2)}, u32[]{:S(2)}) collective-permute-start(f32[6,4,8,256]{3,2,1,0:T(8,128)S(1)} %shard_map.79), channel_id=1, source_target_pairs={{0,2},{1,15},{2,0},{3,5},{4,6},{5,3},{6,4},{7,9},{8,10},{9,7},{10,... | collective-permute-start | bytes 589832 | tf_op jit(solution)/shard_map/ppermute | solution.py:321
  7.0 0.0 collective-permute-done.4.after_ref
  7.0 2.4 %collective-permute-start.5 = (f32[16,128]{1,0:T(8,128)S(1)}, f32[16,128]{1,0:T(8,128)S(1)}, u32[]{:S(2)}, u32[]{:S(2)}) collective-permute-start(f32[16,128]{1,0:T(8,128)S(1)} %pad_maximum_fusion.2), channel_id=1, source_target_pairs={{0,9},{1,8},{2,11},{3,10},{4,13},{5,12},{6,15},{7,14},{8,1},{9,0},... | collective-permute-start | bytes 24584 | tf_op jit(solution)/shard_map/ppermute | solution.py:304
  9.4 0.0 copy-done.2
  9.4 0.0 copy-done.3
  9.4 0.0 copy-done.4
  9.4 0.0 copy-done.5
  9.4 1.1 %shard_map.80 = (f32[6,4,8,256]{3,2,1,0:T(8,128)S(1)}, f32[72,256]{1,0:T(8,128)S(1)}, f32[32,64]{1,0:T(8,128)S(1)}, f32[2,128,256]{2,1,0:T(8,128)S(1)}) custom-call(f32[6,6]{1,0:T(8,128)S(1)} %copy-done.2, f32[6,6]{1,0:T(8,128)S(1)} %copy-done.3, s32[2,8]{1,0:T(2,128)S(1)} %copy-done.4, s32[2,8]{1,0:T(2,128)S(1)} %copy-done.5, ...), custom_call_target="tpu_custom_call" | custom-call | tf_op jit(solution)/shard_map/pallas_call | solution.py:327
  10.5 1.2 %collective-permute-done.5 = f32[16,128]{1,0:T(8,128)S(1)} collective-permute-done((f32[16,128]{1,0:T(8,128)S(1)}, f32[16,128]{1,0:T(8,128)S(1)}, u32[]{:S(2)}, u32[]{:S(2)}) %collective-permute-start.5) | collective-permute-done | bytes 8224 | tf_op jit(solution)/shard_map/ppermute | solution.py:304
  11.7 2.2 %collective-permute-start.6 = (f32[32,128]{1,0:T(8,128)S(1)}, f32[32,128]{1,0:T(8,128)S(1)}, u32[]{:S(2)}, u32[]{:S(2)}) collective-permute-start(f32[32,128]{1,0:T(8,128)S(1)} %pad_maximum_fusion.1), channel_id=1, source_target_pairs={{0,3},{1,2},{2,1},{3,0},{4,7},{5,6},{6,5},{7,4},{8,11},{9,10},{10,... | collective-permute-start | bytes 49160 | tf_op jit(solution)/shard_map/ppermute | solution.py:304
  13.9 0.0 collective-permute-done.1.near_ref
  13.9 0.5 %collective-permute-start.2 = (f32[3,4,8,256]{3,2,1,0:T(8,128)S(1)}, f32[3,4,8,256]{3,2,1,0:T(8,128)S(1)}, u32[]{:S(2)}, u32[]{:S(2)}) collective-permute-start(f32[3,4,8,256]{3,2,1,0:T(8,128)S(1)} %get-tuple-element.11), channel_id=1, source_target_pairs={{0,1},{1,0},{2,3},{3,2},{4,5},{5,4},{6,7},{7,6},{8,9},{9,8},{10,11... | collective-permute-start | bytes 294920 | tf_op jit(solution)/shard_map/ppermute | solution.py:324
  14.4 0.1 collective-permute-start.3
  14.5 0.8 %collective-permute-done.6 = f32[32,128]{1,0:T(8,128)S(1)} collective-permute-done((f32[32,128]{1,0:T(8,128)S(1)}, f32[32,128]{1,0:T(8,128)S(1)}, u32[]{:S(2)}, u32[]{:S(2)}) %collective-permute-start.6) | collective-permute-done | bytes 16416 | tf_op jit(solution)/shard_map/ppermute | solution.py:304
  15.4 0.0 collective-permute-done.2.refs_0_
  15.4 0.3 %collective-permute-done.3.refs_1_ = f32[3,4,8,256]{3,2,1,0:T(8,128)S(1)} collective-permute-done((f32[3,4,8,256]{3,2,1,0:T(8,128)S(1)}, f32[3,4,8,256]{3,2,1,0:T(8,128)S(1)}, u32[]{:S(2)}, u32[]{:S(2)}) %collective-permute-start.3) | collective-permute-done | bytes 98336 | tf_op jit(solution)/shard_map/ppermute | solution.py:324
  15.7 0.0 copy-start.1
  15.7 1.6 %shard_map.81.swept_ref = f32[6,4,8,256]{3,2,1,0:T(8,128)S(1)} custom-call(f32[6,4,8,256]{3,2,1,0:T(8,128)S(1)} %shard_map.77.own_ref, f32[6,4,8,256]{3,2,1,0:T(8,128)S(1)} %collective-permute-done.oth_ref, f32[6,4,8,256]{3,2,1,0:T(8,128)S(1)} %collective-permute-done.1.near_ref, f32[3,4,8,256]{3,2,1,0:T(8,128)S(1)} %collective-permute-done.2.refs_0_, ...), custom_call_target="tpu_custom_call" | custom-call | tf_op jit(solution)/shard_map/pallas_call | solution.py:340
  17.3 0.0 copy-done.1
  17.3 1.3 %shard_map.82 = (f32[6,4,8,256]{3,2,1,0:T(8,128)}, f32[6,4,8,256]{3,2,1,0:T(8,128)}) custom-call(f32[6,4,8,256]{3,2,1,0:T(8,128)S(1)} %shard_map.77.own_ref, f32[6,4,8,256]{3,2,1,0:T(8,128)S(1)} %shard_map.81.swept_ref, f32[64,128]{1,0:T(8,128)S(1)} %pad_maximum_fusion.lines_ref, f32[32,64]{1,0:T(8,128)S(1)} %get-tuple-element.8.pick_ref, ...), custom_call_target="tpu_custom_call" | custom-call | tf_op jit(solution)/shard_map/pallas_call | solution.py:349
  (5 shorter events, 0.0 us)
Async XLA Ops:
  0.6 1.8 %collective-permute-start = (f32[6,4,8,256]{3,2,1,0:T(8,128)}, f32[6,4,8,256]{3,2,1,0:T(8,128)S(1)}, u32[]{:S(2)}, u32[]{:S(2)}) collective-permute-start(f32[6,4,8,256]{3,2,1,0:T(8,128)} %flow_ref.1), channel_id=1, source_target_pairs={{0,1},{1,0},{2,3},{3,2},{4,5},{5,4},{6,7},{7,6},{8,9},{9,8},{10,11... | collective-permute-start | bytes 589832 | tf_op jit(solution)/shard_map/ppermute | solution.py:287
  1.1 0.9 %copy-start = (f32[6,4,8,256]{3,2,1,0:T(8,128)S(1)}, f32[6,4,8,256]{3,2,1,0:T(8,128)}, u32[]{:S(2)}) copy-start(f32[6,4,8,256]{3,2,1,0:T(8,128)} %flow_ref.1) | copy-start | bytes 589828
  2.7 4.4 %collective-permute-start.4 = (f32[8,128]{1,0:T(8,128)S(1)}, f32[8,128]{1,0:T(8,128)S(1)}, u32[]{:S(2)}, u32[]{:S(2)}) collective-permute-start(f32[8,128]{1,0:T(8,128)S(1)} %shard_map.78.after_ref), channel_id=1, source_target_pairs={{0,5},{1,4},{2,7},{3,6},{4,1},{5,0},{6,3},{7,2},{8,13},{9,12},{10,... | collective-permute-start | bytes 12296 | tf_op jit(solution)/shard_map/ppermute | solution.py:304
  5.4 4.0 %copy-start.2 = (f32[6,6]{1,0:T(8,128)S(1)}, f32[6,6]{1,0:T(8,128)}, u32[]{:S(2)}) copy-start(f32[6,6]{1,0:T(8,128)} %jac_pitch_ref.1) | copy-start | bytes 436
  5.4 4.0 %copy-start.3 = (f32[6,6]{1,0:T(8,128)S(1)}, f32[6,6]{1,0:T(8,128)}, u32[]{:S(2)}) copy-start(f32[6,6]{1,0:T(8,128)} %jac_axial_ref.1) | copy-start | bytes 436
  5.4 4.0 %copy-start.4 = (s32[2,8]{1,0:T(2,128)S(1)}, s32[2,8]{1,0:T(2,128)}, u32[]{:S(2)}) copy-start(s32[2,8]{1,0:T(2,128)} %partner_ref.1) | copy-start | bytes 196
  5.4 4.0 %copy-start.5 = (s32[2,8]{1,0:T(2,128)S(1)}, s32[2,8]{1,0:T(2,128)}, u32[]{:S(2)}) copy-start(s32[2,8]{1,0:T(2,128)} %index_ref.1) | copy-start | bytes 196
  5.5 8.4 %collective-permute-start.1 = (f32[6,4,8,256]{3,2,1,0:T(8,128)S(1)}, f32[6,4,8,256]{3,2,1,0:T(8,128)S(1)}, u32[]{:S(2)}, u32[]{:S(2)}) collective-permute-start(f32[6,4,8,256]{3,2,1,0:T(8,128)S(1)} %shard_map.79), channel_id=1, source_target_pairs={{0,2},{1,15},{2,0},{3,5},{4,6},{5,3},{6,4},{7,9},{8,10},{9,7},{10,... | collective-permute-start | bytes 589832 | tf_op jit(solution)/shard_map/ppermute | solution.py:321
  7.0 4.6 %collective-permute-start.5 = (f32[16,128]{1,0:T(8,128)S(1)}, f32[16,128]{1,0:T(8,128)S(1)}, u32[]{:S(2)}, u32[]{:S(2)}) collective-permute-start(f32[16,128]{1,0:T(8,128)S(1)} %pad_maximum_fusion.2), channel_id=1, source_target_pairs={{0,9},{1,8},{2,11},{3,10},{4,13},{5,12},{6,15},{7,14},{8,1},{9,0},... | collective-permute-start | bytes 24584 | tf_op jit(solution)/shard_map/ppermute | solution.py:304
  11.7 3.7 %collective-permute-start.6 = (f32[32,128]{1,0:T(8,128)S(1)}, f32[32,128]{1,0:T(8,128)S(1)}, u32[]{:S(2)}, u32[]{:S(2)}) collective-permute-start(f32[32,128]{1,0:T(8,128)S(1)} %pad_maximum_fusion.1), channel_id=1, source_target_pairs={{0,3},{1,2},{2,1},{3,0},{4,7},{5,6},{6,5},{7,4},{8,11},{9,10},{10,... | collective-permute-start | bytes 49160 | tf_op jit(solution)/shard_map/ppermute | solution.py:304
  13.9 1.4 %collective-permute-start.2 = (f32[3,4,8,256]{3,2,1,0:T(8,128)S(1)}, f32[3,4,8,256]{3,2,1,0:T(8,128)S(1)}, u32[]{:S(2)}, u32[]{:S(2)}) collective-permute-start(f32[3,4,8,256]{3,2,1,0:T(8,128)S(1)} %get-tuple-element.11), channel_id=1, source_target_pairs={{0,1},{1,0},{2,3},{3,2},{4,5},{5,4},{6,7},{7,6},{8,9},{9,8},{10,11... | collective-permute-start | bytes 294920 | tf_op jit(solution)/shard_map/ppermute | solution.py:324
  14.4 1.3 %collective-permute-start.3 = (f32[3,4,8,256]{3,2,1,0:T(8,128)S(1)}, f32[3,4,8,256]{3,2,1,0:T(8,128)S(1)}, u32[]{:S(2)}, u32[]{:S(2)}) collective-permute-start(f32[3,4,8,256]{3,2,1,0:T(8,128)S(1)} %get-tuple-element.10), channel_id=1, source_target_pairs={{0,1},{1,0},{2,3},{3,2},{4,5},{5,4},{6,7},{7,6},{8,9},{9,8},{10,11... | collective-permute-start | bytes 294920 | tf_op jit(solution)/shard_map/ppermute | solution.py:324
  15.7 1.6 %copy-start.1 = (f32[8,256]{1,0:T(8,128)S(1)}, f32[8,256]{1,0:T(8,128)}, u32[]{:S(2)}) copy-start(f32[8,256]{1,0:T(8,128)} %step_ref.1) | copy-start | bytes 24580

commit v4 on v3

--- a/solution.py
+++ b/solution.py
@@ -47,8 +47,27 @@
     return bits[1:] + bits[:1]
 
 
-def stage_kernel(flow_ref, own_ref):
+def stage_kernel(planes, flow_ref, own_ref, shift_ref, sweep_ref):
     own_ref[...] = flow_ref[...]
+    axial = flow_ref.shape[3]
+    source = lax.broadcasted_iota(jnp.int32, (axial, axial), 0)
+    target = lax.broadcasted_iota(jnp.int32, (axial, axial), 1)
+    ahead = target - source
+    up, down = jnp.where(ahead == 1, 1.0, 0.0), jnp.where(ahead == -1, 1.0, 0.0)
+    once = up + down
+    for plane in planes:
+        up = jnp.where(target == plane, 0.0, up)
+    for plane in [*planes, axial]:
+        down = jnp.where(target == plane - 1, jnp.where(ahead == 0, 1.0, 0.0), down)
+    shift_ref[0:axial, :] = up.astype(jnp.bfloat16)
+    shift_ref[axial : 2 * axial, :] = (VISCOUS * (up + down)).astype(jnp.bfloat16)
+    far, edges = jnp.abs(ahead), source + target
+    corner = (edges == 0) | (edges == 2 * axial - 2)
+    beside = (edges == 1) | (edges == 2 * axial - 3)
+    twice = jnp.where(far == 2, 1.0, jnp.where(far == 0, jnp.where(corner, 1.0, 2.0), 0.0))
+    thrice = jnp.where(far == 3, 1.0, jnp.where(far == 1, jnp.where(beside, 2.0, 3.0), 0.0))
+    for power, value in enumerate((once, twice, thrice)):
+        sweep_ref[power * axial : (power + 1) * axial, :] = value.astype(jnp.bfloat16)
 
 
 def line_kernel(planes, own_ref, oth_ref, line_ref):
@@ -126,13 +145,16 @@
     index_ref,
     own_ref,
     oth_ref,
+    step_in_ref,
     after_ref,
+    step_ref,
     local_ref,
     jac_ref,
     pick_ref,
     mix_ref,
 ):
     del after_ref
+    step_ref[...] = step_in_ref[...]
     core, space = lax.axis_index("inst"), lax.axis_index("space")
     nvar, ninst, _, axial = own_ref.shape
     for n in range(ninst):
@@ -174,63 +196,15 @@
             mix_ref[plane_no, at : at + ROWS, :] = jnp.where(row == source, block, 0.0)
 
 
-def sweep_kernel(
-    planes, own_ref, oth_ref, near_ref, *refs
-):
-    *far_refs, local_ref, jac_ref, swept_ref, halo_own, halo_oth = refs
-    core = lax.axis_index("inst")
-    low = low_side()
-    nvar, ninst, _, axial = own_ref.shape
-    cut = nvar // len(far_refs)
-    row = lax.broadcasted_iota(jnp.int32, (ROWS, axial), 0)
-    for v in range(nvar):
-        for n in range(ninst):
-            near, far = near_ref[v, n], far_refs[v // cut][v % cut, n]
-            below = jnp.where(low, near, far)
-            above = jnp.where(low, far, near)
-            first = jnp.where(row < HALO, above, pltpu.roll(below, HALO, 0))
-            second = jnp.where(row < HALO, pltpu.roll(above, HALO, 0), below)
-            halo_own[v, n] = jnp.where(core == 0, first, second)
-            halo_oth[v, n] = jnp.where(core == 0, second, first)
-    c0, c1, c2, c3 = sweep_weights()
-    lane = lax.broadcasted_iota(jnp.int32, (ROWS, axial), 1)
-
-    def jac(which, u, v):
-        at = (which * nvar + u) * nvar + v
-        return jac_ref[at : at + 1, :]
-
-    for n in range(ninst):
-        terms = local_terms(planes, functools.partial(jac, 1), halo_own, halo_oth, n)
-        slope, spread = [], []
-        for v in range(nvar):
-            c = jnp.concatenate([own_ref[v, n], halo_own[v, n]], axis=0)
-            nxt, prv = pltpu.roll(c, 2 * ROWS - 1, 0), pltpu.roll(c, 1, 0)
-            slope.append(0.5 * (nxt - prv))
-            spread.append(nxt + prv)
-        for u in range(nvar):
-            r0 = jnp.concatenate([local_ref[u, n], terms[u]], axis=0) - VISCOUS * spread[u]
-            for v in range(nvar):
-                r0 += jac(0, u, v) * slope[v]
-            r1 = pltpu.roll(r0, 2 * ROWS - 1, 0) + pltpu.roll(r0, 1, 0)
-            r2 = pltpu.roll(r1, 2 * ROWS - 1, 0) + pltpu.roll(r1, 1, 0)
-            r3 = pltpu.roll(r2, 2 * ROWS - 1, 0) + pltpu.roll(r2, 1, 0)
-            r0, r1, r2, r3 = (r[0:ROWS] for r in (r0, r1, r2, r3))
-            s = c3 * r0
-            for more in (
-                c2 * r0 + 3.0 * c3 * r1,
-                c1 * r0 + 2.0 * c2 * r1 + 3.0 * c3 * r2,
-                c0 * r0 + c1 * r1 + c2 * r2 + c3 * r3,
-            ):
-                prv = jnp.where(lane == 0, 0.0, pltpu.roll(s, 1, 1))
-                nxt = jnp.where(lane == axial - 1, 0.0, pltpu.roll(s, axial - 1, 1))
-                s = more + prv + nxt
-            swept_ref[u, n] = s
-
-
-def finish_kernel(
-    planes, own_ref, swept_ref, lines_ref, pick_ref, mix_ref, step_ref, new_ref, out_ref
-):
-    nvar, ninst, _, axial = own_ref.shape
+def times(left, right):
+    first = left.astype(jnp.bfloat16)
+    second = (left - first.astype(jnp.float32)).astype(jnp.bfloat16)
+    return jnp.dot(first, right, preferred_element_type=jnp.float32) + jnp.dot(
+        second, right, preferred_element_type=jnp.float32
+    )
+
+
+def inflow_spread(planes, lines_ref, pick_ref, mix_ref):
     exact = dict(precision=lax.Precision.HIGHEST, preferred_element_type=jnp.float32)
     facing = jnp.dot(pick_ref[...], lines_ref[...], **exact)
     lane = lax.rem(lax.broadcasted_iota(jnp.int32, (ROWS, 2 * LANES), 1), GROUP)
@@ -248,11 +222,80 @@
             if m < SWEEPS:
                 power = pltpu.roll(power, 2 * ROWS - 1, 0) + pltpu.roll(power, 1, 0)
         spread.append(total)
+    return spread
+
+
+def step_kernel(planes, cuts, *refs):
+    own_ref, oth_ref, near_ref, *refs = refs
+    far_refs, refs = refs[:cuts], refs[cuts:]
+    local_ref, jac_ref, shift_ref, sweep_ref, lines_ref, pick_ref, mix_ref, step_ref, *refs = refs
+    new_ref, out_ref, halo_own, halo_oth, parts_ref, rest_ref, terms_ref, base_ref = refs
+    core = lax.axis_index("inst")
+    low = low_side()
+    nvar, ninst, _, axial = own_ref.shape
+    cut = nvar // cuts
+    row = lax.broadcasted_iota(jnp.int32, (ROWS, axial), 0)
+    spread = inflow_spread(planes, lines_ref, pick_ref, mix_ref)
+    for v in range(nvar):
+        for n in range(ninst):
+            near, far = near_ref[v, n], far_refs[v // cut][v % cut, n]
+            below = jnp.where(low, near, far)
+            above = jnp.where(low, far, near)
+            first = jnp.where(row < HALO, above, pltpu.roll(below, HALO, 0))
+            second = jnp.where(row < HALO, pltpu.roll(above, HALO, 0), below)
+            halo_own[v, n] = jnp.where(core == 0, first, second)
+            halo_oth[v, n] = jnp.where(core == 0, second, first)
+
+    def jac(which, u, v):
+        at = (which * nvar + u) * nvar + v
+        return jac_ref[at : at + 1, :]
+
+    def lines_of(u, n):
+        at = (u * ninst + n) * ROWS
+        return slice(at, at + ROWS)
+
+    for n in range(ninst):
+        centre = [halo_own[v, n] for v in range(nvar)]
+        for u in range(nvar):
+            z = sum(jac(1, u, v) * centre[v] for v in range(nvar))
+            rest = z + 4.0 * VISCOUS * centre[u]
+            for j in range(ninst):
+                if j != n:
+                    rest += spectral_entry(n - j, 2 * ninst) * halo_own[u, j]
+                rest += spectral_entry(n - j - ninst, 2 * ninst) * halo_oth[u, j]
+            rest_ref[lines_of(u, n), :] = rest
+            parts_ref[lines_of(u, n), 0:axial] = z
+            parts_ref[lines_of(u, n), axial : 2 * axial] = centre[u]
+    rest_ref[...] = rest_ref[...] - times(parts_ref[...], shift_ref[...])
+
+    c0, c1, c2, c3 = sweep_weights()
+    for n in range(ninst):
+        slope, around = [], []
+        for v in range(nvar):
+            c = jnp.concatenate([own_ref[v, n], halo_own[v, n]], axis=0)
+            nxt, prv = pltpu.roll(c, 2 * ROWS - 1, 0), pltpu.roll(c, 1, 0)
+            slope.append(0.5 * (nxt - prv))
+            around.append(nxt + prv)
+        for u in range(nvar):
+            at = lines_of(u, n)
+            r0 = jnp.concatenate([local_ref[u, n], rest_ref[at, :]], axis=0) - VISCOUS * around[u]
+            for v in range(nvar):
+                r0 += jac(0, u, v) * slope[v]
+            r1 = pltpu.roll(r0, 2 * ROWS - 1, 0) + pltpu.roll(r0, 1, 0)
+            r2 = pltpu.roll(r1, 2 * ROWS - 1, 0) + pltpu.roll(r1, 1, 0)
+            r3 = pltpu.roll(r2, 2 * ROWS - 1, 0) + pltpu.roll(r2, 1, 0)
+            r0, r1, r2, r3 = (r[0:ROWS] for r in (r0, r1, r2, r3))
+            base_ref[at, :] = c0 * r0 + c1 * r1 + c2 * r2 + c3 * r3
+            terms_ref[at, 0:axial] = c1 * r0 + 2.0 * c2 * r1 + 3.0 * c3 * r2
+            terms_ref[at, axial : 2 * axial] = c2 * r0 + 3.0 * c3 * r1
+            terms_ref[at, 2 * axial : 3 * axial] = c3 * r0
+    base_ref[...] = base_ref[...] + times(terms_ref[...], sweep_ref[...])
+
     step = step_ref[...]
     lane = lax.broadcasted_iota(jnp.int32, (ROWS, LANES), 1)
     for n in range(ninst):
         for u in range(nvar):
-            tiles = [swept_ref[u, n, :, t : t + LANES] for t in range(0, axial, LANES)]
+            tiles = [base_ref[lines_of(u, n), t : t + LANES] for t in range(0, axial, LANES)]
             group = (u * ninst + n) * GROUP
             for plane_no, plane in enumerate(planes):
                 tile, at = divmod(plane - SWEEPS, LANES)
@@ -285,11 +328,18 @@
     cores = [(0, 1), (1, 0)]
 
     other = here(lax.ppermute(flow_state, "inst", cores))
-    own = here(
-        pl.pallas_call(
-            stage_kernel, out_shape=block, in_specs=[vmem], out_specs=vmem, compiler_params=params
-        )(flow_state)
-    )
+    own, shift, sweep = pl.pallas_call(
+        functools.partial(stage_kernel, planes),
+        out_shape=(
+            block,
+            pltpu.VMEM((2 * axial, axial), jnp.bfloat16),
+            pltpu.VMEM((SWEEPS * axial, axial), jnp.bfloat16),
+        ),
+        in_specs=[vmem],
+        out_specs=(vmem,) * 3,
+        compiler_params=params,
+    )(flow_state)
+    own = here(own)
     line = pl.pallas_call(
         functools.partial(line_kernel, planes),
         out_shape=pltpu.VMEM((rows, LANES), jnp.float32),
@@ -324,35 +374,39 @@
         here(lax.ppermute(near[v : v + cut], "inst", cores)) for v in range(0, nvar, cut)
     ]
 
-    local, jac, pick, mix = pl.pallas_call(
+    step, local, jac, pick, mix = pl.pallas_call(
         functools.partial(prepare_kernel, planes, spaces),
         out_shape=(
+            pltpu.VMEM(pseudo_step.shape, jnp.float32),
             block,
             pltpu.VMEM((2 * nvar * nvar, axial), jnp.float32),
             pltpu.VMEM((IFACES * 2 * rows, spaces * rows), jnp.float32),
             pltpu.VMEM((IFACES, LANES, 2 * LANES), jnp.float32),
         ),
-        in_specs=[smem] * 4 + [vmem] * 2 + [anywhere],
-        out_specs=(vmem,) * 4,
+        in_specs=[smem] * 4 + [vmem] * 3 + [anywhere],
+        out_specs=(vmem,) * 5,
         compiler_params=params,
-    )(jac_pitch, jac_axial, partner, iface_index, own, other, got[0])
-
-    swept = pl.pallas_call(
-        functools.partial(sweep_kernel, planes),
-        out_shape=block,
-        in_specs=[vmem] * (5 + len(far)),
-        out_specs=vmem,
-        scratch_shapes=[block, block],
+    )(jac_pitch, jac_axial, partner, iface_index, own, other, pseudo_step, got[0])
+
+    lined = nvar * ninst * rows
+    return pl.pallas_call(
+        functools.partial(step_kernel, planes, len(far)),
+        out_shape=(jax.ShapeDtypeStruct(flow_state.shape, jnp.float32),) * 2,
+        in_specs=[vmem] * (11 + len(far)),
+        out_specs=(vmem, vmem),
+        scratch_shapes=[
+            block,
+            block,
+            pltpu.VMEM((lined, 2 * axial), jnp.float32),
+            pltpu.VMEM((lined, axial), jnp.float32),
+            pltpu.VMEM((lined, SWEEPS * axial), jnp.float32),
+            pltpu.VMEM((lined, axial), jnp.float32),
+        ],
         compiler_params=params,
-    )(own, other, here(near), *far, here(local), here(jac))
-
-    return pl.pallas_call(
-        functools.partial(finish_kernel, planes),
-        out_shape=(jax.ShapeDtypeStruct(flow_state.shape, jnp.float32),) * 2,
-        in_specs=[vmem] * 6,
-        out_specs=(vmem, vmem),
-        compiler_params=params,
-    )(own, here(swept), here(lines), here(pick), here(mix), here(pseudo_step))
+    )(
+        own, other, here(near), *far,
+        *[here(a) for a in (local, jac, shift, sweep, lines, pick, mix, step)],
+    )
 
 
 def solution(mesh):

time: 18.7 us -> 18.1 us (0.968)
  Pallas kernels: 4.21 us -> 3.72 us
    pallas_call x3 -> x2, Pallas kernels: 2.84 us -> 2.35 us  [the longest x1 2.21 us: shards(): pl.pallas_call(functools.partial(step_kernel, planes, len(far)), out_shap...]
  transfers between devices with their start and end apart: 7 -> 7, of which waited for: 4 -> 4; matrix products, arithmetic and copies ran while one was open for 0% -> 0% of each run, Pallas kernels for 6% -> 7%
where the time goes in v4:
time: 18.1 us; the launch traced here: 17.9 us
  starting transfers between devices  9.97 us (55%)
  Pallas kernels  3.72 us (21%)
  waiting for transfers between devices  2.54 us (14%)
  local copies, waits for them, and re-layouts  0.97 us (5%)
  between operations  0.7 us (4%)
    ppermute x3, starting transfers between devices, shards(): lax.ppermute(lines, both, [(2 * i + c, 2 * (i ^ 1 << bit) + 1 - c) for i...  7.32 us
    pallas_call x1, Pallas kernels, shards(): pl.pallas_call(functools.partial(step_kernel, planes, len(far)), out_shap...  2.21 us
    ppermute x3, waiting for transfers between devices, shards(): lax.ppermute(lines, both, [(2 * i + c, 2 * (i ^ 1 << bit) + 1 - c) for i...  2 us
    ppermute x1, starting transfers between devices, shards(): near = lax.ppermute(edge, both, pairs)  1.56 us
    pallas_call x1, Pallas kernels, shards(): pl.pallas_call(functools.partial(prepare_kernel, planes, spaces), out_sha...  1.07 us
    unnamed x12, local copies, waits for them, and re-layouts  0.95 us
    ppermute x2, starting transfers between devices, shards(): lax.ppermute(near[v:v + cut], 'inst', cores)  0.58 us
    ppermute x1, starting transfers between devices, shards(): other = here(lax.ppermute(flow_state, 'inst', cores))  0.52 us
  transfers between devices with their start and end apart: 7, of which 4 were waited for; matrix products, arithmetic and copies ran while one was open for 0% of the time, Pallas kernels for 7%

profile of v4, /device:TPU:0, one launch (start us, length us, event | category | flops | bytes accessed | tf_op | source)
XLA Modules:
  0.0 17.9 jit_solution(7732631918839133252)
XLA Ops:
  0.6 0.5 %collective-permute-start = (f32[6,4,8,256]{3,2,1,0:T(8,128)}, f32[6,4,8,256]{3,2,1,0:T(8,128)S(1)}, u32[]{:S(2)}, u32[]{:S(2)}) collective-permute-start(f32[6,4,8,256]{3,2,1,0:T(8,128)} %flow_ref.1), channel_id=1, source_target_pairs={{0,1},{1,0},{2,3},{3,2},{4,5},{5,4},{6,7},{7,6},{8,9},{9,8},{10,11... | collective-permute-start | bytes 589832 | tf_op jit(solution)/shard_map/ppermute | solution.py:330
  1.1 0.0 copy-start
  1.1 0.9 %copy-done = f32[6,4,8,256]{3,2,1,0:T(8,128)S(1)} copy-done((f32[6,4,8,256]{3,2,1,0:T(8,128)S(1)}, f32[6,4,8,256]{3,2,1,0:T(8,128)}, u32[]{:S(2)}) %copy-start) | copy-done | bytes 196632
  2.1 0.1 shard_map.77
  2.2 0.2 %collective-permute-done.oth_ref.refs_1_ = f32[6,4,8,256]{3,2,1,0:T(8,128)S(1)} collective-permute-done((f32[6,4,8,256]{3,2,1,0:T(8,128)}, f32[6,4,8,256]{3,2,1,0:T(8,128)S(1)}, u32[]{:S(2)}, u32[]{:S(2)}) %collective-permute-start) | collective-permute-done | bytes 196640 | tf_op jit(solution)/shard_map/ppermute | solution.py:330
  2.4 0.2 %shard_map.78.after_ref = f32[8,128]{1,0:T(8,128)S(1)} custom-call(f32[6,4,8,256]{3,2,1,0:T(8,128)S(1)} %get-tuple-element.10.own_ref.refs_0_, f32[6,4,8,256]{3,2,1,0:T(8,128)S(1)} %collective-permute-done.oth_ref.refs_1_), custom_call_target="tpu_custom_call" | custom-call | tf_op jit(solution)/shard_map/pallas_call | solution.py:343
  2.7 2.7 %collective-permute-start.4 = (f32[8,128]{1,0:T(8,128)S(1)}, f32[8,128]{1,0:T(8,128)S(1)}, u32[]{:S(2)}, u32[]{:S(2)}) collective-permute-start(f32[8,128]{1,0:T(8,128)S(1)} %shard_map.78.after_ref), channel_id=1, source_target_pairs={{0,5},{1,4},{2,7},{3,6},{4,1},{5,0},{6,3},{7,2},{8,13},{9,12},{10,... | collective-permute-start | bytes 12296 | tf_op jit(solution)/shard_map/ppermute | solution.py:354
  5.4 0.0 copy-start.4
  5.4 0.0 copy-start.5
  5.4 0.1 shard_map.79
  5.4 0.0 copy-start.1
  5.4 0.0 copy-start.2
  5.4 0.0 copy-start.3
  5.5 1.6 %collective-permute-start.1 = (f32[6,4,8,256]{3,2,1,0:T(8,128)S(1)}, f32[6,4,8,256]{3,2,1,0:T(8,128)S(1)}, u32[]{:S(2)}, u32[]{:S(2)}) collective-permute-start(f32[6,4,8,256]{3,2,1,0:T(8,128)S(1)} %shard_map.79), channel_id=1, source_target_pairs={{0,2},{1,15},{2,0},{3,5},{4,6},{5,3},{6,4},{7,9},{8,10},{9,7},{10,... | collective-permute-start | bytes 589832 | tf_op jit(solution)/shard_map/ppermute | solution.py:371
  7.0 0.0 collective-permute-done.4.after_ref
  7.0 2.4 %collective-permute-start.5 = (f32[16,128]{1,0:T(8,128)S(1)}, f32[16,128]{1,0:T(8,128)S(1)}, u32[]{:S(2)}, u32[]{:S(2)}) collective-permute-start(f32[16,128]{1,0:T(8,128)S(1)} %pad_maximum_fusion.2), channel_id=1, source_target_pairs={{0,9},{1,8},{2,11},{3,10},{4,13},{5,12},{6,15},{7,14},{8,1},{9,0},... | collective-permute-start | bytes 24584 | tf_op jit(solution)/shard_map/ppermute | solution.py:354
  9.4 0.0 copy-done.4
  9.4 0.0 copy-done.5
  9.4 0.0 copy-done.1
  9.4 0.0 copy-done.2
  9.4 0.0 copy-done.3
  9.4 1.1 %shard_map.80 = (f32[8,256]{1,0:T(8,128)S(1)}, f32[6,4,8,256]{3,2,1,0:T(8,128)S(1)}, f32[72,256]{1,0:T(8,128)S(1)}, f32[32,64]{1,0:T(8,128)S(1)}, f32[2,128,256]{2,1,0:T(8,128)S(1)}) custom-call(f32[6,6]{1,0:T(8,128)S(1)} %copy-done.2, f32[6,6]{1,0:T(8,128)S(1)} %copy-done.3, s32[2,8]{1,0:T(2,128)S(1)} %copy-done.4, s32[2,8]{1,0:T(2,128)S(1)} %copy-done.5, ...), custom_call_target="tpu_custom_call" | custom-call | tf_op jit(solution)/shard_map/pallas_call | solution.py:377
  10.5 1.1 %collective-permute-done.5 = f32[16,128]{1,0:T(8,128)S(1)} collective-permute-done((f32[16,128]{1,0:T(8,128)S(1)}, f32[16,128]{1,0:T(8,128)S(1)}, u32[]{:S(2)}, u32[]{:S(2)}) %collective-permute-start.5) | collective-permute-done | bytes 8224 | tf_op jit(solution)/shard_map/ppermute | solution.py:354
  11.7 2.2 %collective-permute-start.6 = (f32[32,128]{1,0:T(8,128)S(1)}, f32[32,128]{1,0:T(8,128)S(1)}, u32[]{:S(2)}, u32[]{:S(2)}) collective-permute-start(f32[32,128]{1,0:T(8,128)S(1)} %pad_maximum_fusion.1), channel_id=1, source_target_pairs={{0,3},{1,2},{2,1},{3,0},{4,7},{5,6},{6,5},{7,4},{8,11},{9,10},{10,... | collective-permute-start | bytes 49160 | tf_op jit(solution)/shard_map/ppermute | solution.py:354
  13.9 0.0 collective-permute-done.1.refs_2_
  13.9 0.5 %collective-permute-start.3 = (f32[3,4,8,256]{3,2,1,0:T(8,128)S(1)}, f32[3,4,8,256]{3,2,1,0:T(8,128)S(1)}, u32[]{:S(2)}, u32[]{:S(2)}) collective-permute-start(f32[3,4,8,256]{3,2,1,0:T(8,128)S(1)} %get-tuple-element.18), channel_id=1, source_target_pairs={{0,1},{1,0},{2,3},{3,2},{4,5},{5,4},{6,7},{7,6},{8,9},{9,8},{10,11... | collective-permute-start | bytes 294920 | tf_op jit(solution)/shard_map/ppermute | solution.py:374
  14.4 0.1 collective-permute-start.2
  14.5 0.8 %collective-permute-done.6 = f32[32,128]{1,0:T(8,128)S(1)} collective-permute-done((f32[32,128]{1,0:T(8,128)S(1)}, f32[32,128]{1,0:T(8,128)S(1)}, u32[]{:S(2)}, u32[]{:S(2)}) %collective-permute-start.6) | collective-permute-done | bytes 16416 | tf_op jit(solution)/shard_map/ppermute | solution.py:354
  15.3 0.0 collective-permute-done.3.refs_4_
  15.4 0.3 %collective-permute-done.2.refs_3_ = f32[3,4,8,256]{3,2,1,0:T(8,128)S(1)} collective-permute-done((f32[3,4,8,256]{3,2,1,0:T(8,128)S(1)}, f32[3,4,8,256]{3,2,1,0:T(8,128)S(1)}, u32[]{:S(2)}, u32[]{:S(2)}) %collective-permute-start.2) | collective-permute-done | bytes 98336 | tf_op jit(solution)/shard_map/ppermute | solution.py:374
  15.7 2.2 %shard_map.81 = (f32[6,4,8,256]{3,2,1,0:T(8,128)}, f32[6,4,8,256]{3,2,1,0:T(8,128)}) custom-call(f32[6,4,8,256]{3,2,1,0:T(8,128)S(1)} %get-tuple-element.10.own_ref.refs_0_, f32[6,4,8,256]{3,2,1,0:T(8,128)S(1)} %collective-permute-done.oth_ref.refs_1_, f32[6,4,8,256]{3,2,1,0:T(8,128)S(1)} %collective-permute-done.1.refs_2_, ...), custom_call_target="tpu_custom_call" | custom-call | tf_op jit(solution)/shard_map/pallas_call | solution.py:392
  (4 shorter events, 0.0 us)
Async XLA Ops:
  0.6 1.8 %collective-permute-start = (f32[6,4,8,256]{3,2,1,0:T(8,128)}, f32[6,4,8,256]{3,2,1,0:T(8,128)S(1)}, u32[]{:S(2)}, u32[]{:S(2)}) collective-permute-start(f32[6,4,8,256]{3,2,1,0:T(8,128)} %flow_ref.1), channel_id=1, source_target_pairs={{0,1},{1,0},{2,3},{3,2},{4,5},{5,4},{6,7},{7,6},{8,9},{9,8},{10,11... | collective-permute-start | bytes 589832 | tf_op jit(solution)/shard_map/ppermute | solution.py:330
  1.1 0.9 %copy-start = (f32[6,4,8,256]{3,2,1,0:T(8,128)S(1)}, f32[6,4,8,256]{3,2,1,0:T(8,128)}, u32[]{:S(2)}) copy-start(f32[6,4,8,256]{3,2,1,0:T(8,128)} %flow_ref.1) | copy-start | bytes 589828
  2.7 4.4 %collective-permute-start.4 = (f32[8,128]{1,0:T(8,128)S(1)}, f32[8,128]{1,0:T(8,128)S(1)}, u32[]{:S(2)}, u32[]{:S(2)}) collective-permute-start(f32[8,128]{1,0:T(8,128)S(1)} %shard_map.78.after_ref), channel_id=1, source_target_pairs={{0,5},{1,4},{2,7},{3,6},{4,1},{5,0},{6,3},{7,2},{8,13},{9,12},{10,... | collective-permute-start | bytes 12296 | tf_op jit(solution)/shard_map/ppermute | solution.py:354
  5.4 4.1 %copy-start.4 = (s32[2,8]{1,0:T(2,128)S(1)}, s32[2,8]{1,0:T(2,128)}, u32[]{:S(2)}) copy-start(s32[2,8]{1,0:T(2,128)} %partner_ref.1) | copy-start | bytes 196
  5.4 4.1 %copy-start.5 = (s32[2,8]{1,0:T(2,128)S(1)}, s32[2,8]{1,0:T(2,128)}, u32[]{:S(2)}) copy-start(s32[2,8]{1,0:T(2,128)} %index_ref.1) | copy-start | bytes 196
  5.4 4.0 %copy-start.1 = (f32[8,256]{1,0:T(8,128)S(1)}, f32[8,256]{1,0:T(8,128)}, u32[]{:S(2)}) copy-start(f32[8,256]{1,0:T(8,128)} %step_in_ref.1) | copy-start | bytes 24580
  5.4 4.0 %copy-start.2 = (f32[6,6]{1,0:T(8,128)S(1)}, f32[6,6]{1,0:T(8,128)}, u32[]{:S(2)}) copy-start(f32[6,6]{1,0:T(8,128)} %jac_pitch_ref.1) | copy-start | bytes 436
  5.4 4.0 %copy-start.3 = (f32[6,6]{1,0:T(8,128)S(1)}, f32[6,6]{1,0:T(8,128)}, u32[]{:S(2)}) copy-start(f32[6,6]{1,0:T(8,128)} %jac_axial_ref.1) | copy-start | bytes 436
  5.5 8.4 %collective-permute-start.1 = (f32[6,4,8,256]{3,2,1,0:T(8,128)S(1)}, f32[6,4,8,256]{3,2,1,0:T(8,128)S(1)}, u32[]{:S(2)}, u32[]{:S(2)}) collective-permute-start(f32[6,4,8,256]{3,2,1,0:T(8,128)S(1)} %shard_map.79), channel_id=1, source_target_pairs={{0,2},{1,15},{2,0},{3,5},{4,6},{5,3},{6,4},{7,9},{8,10},{9,7},{10,... | collective-permute-start | bytes 589832 | tf_op jit(solution)/shard_map/ppermute | solution.py:371
  7.0 4.6 %collective-permute-start.5 = (f32[16,128]{1,0:T(8,128)S(1)}, f32[16,128]{1,0:T(8,128)S(1)}, u32[]{:S(2)}, u32[]{:S(2)}) collective-permute-start(f32[16,128]{1,0:T(8,128)S(1)} %pad_maximum_fusion.2), channel_id=1, source_target_pairs={{0,9},{1,8},{2,11},{3,10},{4,13},{5,12},{6,15},{7,14},{8,1},{9,0},... | collective-permute-start | bytes 24584 | tf_op jit(solution)/shard_map/ppermute | solution.py:354
  11.7 3.7 %collective-permute-start.6 = (f32[32,128]{1,0:T(8,128)S(1)}, f32[32,128]{1,0:T(8,128)S(1)}, u32[]{:S(2)}, u32[]{:S(2)}) collective-permute-start(f32[32,128]{1,0:T(8,128)S(1)} %pad_maximum_fusion.1), channel_id=1, source_target_pairs={{0,3},{1,2},{2,1},{3,0},{4,7},{5,6},{6,5},{7,4},{8,11},{9,10},{10,... | collective-permute-start | bytes 49160 | tf_op jit(solution)/shard_map/ppermute | solution.py:354
  13.9 1.4 %collective-permute-start.3 = (f32[3,4,8,256]{3,2,1,0:T(8,128)S(1)}, f32[3,4,8,256]{3,2,1,0:T(8,128)S(1)}, u32[]{:S(2)}, u32[]{:S(2)}) collective-permute-start(f32[3,4,8,256]{3,2,1,0:T(8,128)S(1)} %get-tuple-element.18), channel_id=1, source_target_pairs={{0,1},{1,0},{2,3},{3,2},{4,5},{5,4},{6,7},{7,6},{8,9},{9,8},{10,11... | collective-permute-start | bytes 294920 | tf_op jit(solution)/shard_map/ppermute | solution.py:374
  14.4 1.3 %collective-permute-start.2 = (f32[3,4,8,256]{3,2,1,0:T(8,128)S(1)}, f32[3,4,8,256]{3,2,1,0:T(8,128)S(1)}, u32[]{:S(2)}, u32[]{:S(2)}) collective-permute-start(f32[3,4,8,256]{3,2,1,0:T(8,128)S(1)} %get-tuple-element.19), channel_id=1, source_target_pairs={{0,1},{1,0},{2,3},{3,2},{4,5},{5,4},{6,7},{7,6},{8,9},{9,8},{10,11... | collective-permute-start | bytes 294920 | tf_op jit(solution)/shard_map/ppermute | solution.py:374

commit v5 on v4

--- a/solution.py
+++ b/solution.py
@@ -204,9 +204,10 @@
     )
 
 
-def inflow_spread(planes, lines_ref, pick_ref, mix_ref):
+def inflow_spread(planes, lines_refs, pick_ref, mix_ref):
     exact = dict(precision=lax.Precision.HIGHEST, preferred_element_type=jnp.float32)
-    facing = jnp.dot(pick_ref[...], lines_ref[...], **exact)
+    lines = jnp.concatenate([ref[...] for ref in lines_refs], axis=0)
+    facing = jnp.dot(pick_ref[...], lines, **exact)
     lane = lax.rem(lax.broadcasted_iota(jnp.int32, (ROWS, 2 * LANES), 1), GROUP)
     spread = []
     for plane_no in range(len(planes)):
@@ -225,34 +226,33 @@
     return spread
 
 
-def step_kernel(planes, cuts, *refs):
-    own_ref, oth_ref, near_ref, *refs = refs
-    far_refs, refs = refs[:cuts], refs[cuts:]
-    local_ref, jac_ref, shift_ref, sweep_ref, lines_ref, pick_ref, mix_ref, step_ref, *refs = refs
-    new_ref, out_ref, halo_own, halo_oth, parts_ref, rest_ref, terms_ref, base_ref = refs
+def jac_row(jac_ref, nvar, which, u, v):
+    at = (which * nvar + u) * nvar + v
+    return jac_ref[at : at + 1, :]
+
+
+def lines_of(ninst, u, n):
+    at = (u * ninst + n) * ROWS
+    return slice(at, at + ROWS)
+
+
+def near_kernel(planes, *refs):
+    own_ref, near_ref, local_ref, jac_ref, shift_ref, sweep_ref, base_ref, *refs = refs
+    halo_own, halo_oth, parts_ref, rest_ref, terms_ref = refs
     core = lax.axis_index("inst")
     low = low_side()
     nvar, ninst, _, axial = own_ref.shape
-    cut = nvar // cuts
     row = lax.broadcasted_iota(jnp.int32, (ROWS, axial), 0)
-    spread = inflow_spread(planes, lines_ref, pick_ref, mix_ref)
+    keep = jnp.where(low, row, ROWS - 1 - row) >= HALO
     for v in range(nvar):
         for n in range(ninst):
-            near, far = near_ref[v, n], far_refs[v // cut][v % cut, n]
-            below = jnp.where(low, near, far)
-            above = jnp.where(low, far, near)
-            first = jnp.where(row < HALO, above, pltpu.roll(below, HALO, 0))
-            second = jnp.where(row < HALO, pltpu.roll(above, HALO, 0), below)
+            near = near_ref[v, n]
+            turned = pltpu.roll(near, HALO, 0)
+            first = jnp.where(keep, jnp.where(low, turned, near), 0.0)
+            second = jnp.where(keep, jnp.where(low, near, turned), 0.0)
             halo_own[v, n] = jnp.where(core == 0, first, second)
             halo_oth[v, n] = jnp.where(core == 0, second, first)
-
-    def jac(which, u, v):
-        at = (which * nvar + u) * nvar + v
-        return jac_ref[at : at + 1, :]
-
-    def lines_of(u, n):
-        at = (u * ninst + n) * ROWS
-        return slice(at, at + ROWS)
+    jac = functools.partial(jac_row, jac_ref, nvar)
 
     for n in range(ninst):
         centre = [halo_own[v, n] for v in range(nvar)]
@@ -263,9 +263,10 @@
                 if j != n:
                     rest += spectral_entry(n - j, 2 * ninst) * halo_own[u, j]
                 rest += spectral_entry(n - j - ninst, 2 * ninst) * halo_oth[u, j]
-            rest_ref[lines_of(u, n), :] = rest
-            parts_ref[lines_of(u, n), 0:axial] = z
-            parts_ref[lines_of(u, n), axial : 2 * axial] = centre[u]
+            at = lines_of(ninst, u, n)
+            rest_ref[at, :] = rest
+            parts_ref[at, 0:axial] = z
+            parts_ref[at, axial : 2 * axial] = centre[u]
     rest_ref[...] = rest_ref[...] - times(parts_ref[...], shift_ref[...])
 
     c0, c1, c2, c3 = sweep_weights()
@@ -277,7 +278,7 @@
             slope.append(0.5 * (nxt - prv))
             around.append(nxt + prv)
         for u in range(nvar):
-            at = lines_of(u, n)
+            at = lines_of(ninst, u, n)
             r0 = jnp.concatenate([local_ref[u, n], rest_ref[at, :]], axis=0) - VISCOUS * around[u]
             for v in range(nvar):
                 r0 += jac(0, u, v) * slope[v]
@@ -291,11 +292,95 @@
             terms_ref[at, 2 * axial : 3 * axial] = c3 * r0
     base_ref[...] = base_ref[...] + times(terms_ref[...], sweep_ref[...])
 
+
+def step_kernel(planes, cuts, *refs):
+    before_ref, base_ref, *refs = refs
+    far_refs, refs = refs[:cuts], refs[cuts:]
+    jac_ref, shift_ref, sweep_ref, *lines_refs, pick_ref, mix_ref, step_ref = refs[:8]
+    new_ref, out_ref, far_own, far_oth, parts_ref, rest_ref, terms_ref = refs[8:]
+    core = lax.axis_index("inst")
+    low = low_side()
+    nvar, ninst, _, axial = new_ref.shape
+    cut, packs = nvar // cuts, ninst // 2
+    row = lax.broadcasted_iota(jnp.int32, (ROWS, axial), 0)
+    side = jnp.where(low, row, ROWS - 1 - row)
+    depth = side & (HALO - 1)
+    spread = inflow_spread(planes, lines_refs, pick_ref, mix_ref)
+    jac = functools.partial(jac_row, jac_ref, nvar)
+
+    def shifted(tile, s):
+        moved = pltpu.roll(tile, jnp.where(low, s, ROWS - s), 0)
+        return jnp.where(depth >= s, moved, 0.0)
+
+    for v in range(nvar):
+        for n in range(ninst):
+            tile = far_refs[v // cut][v % cut, n]
+            turned = pltpu.roll(tile, HALO, 0)
+            first = jnp.where(row < HALO, tile, turned)
+            second = jnp.where(row < HALO, turned, tile)
+            far_own[v, n] = jnp.where(core == 0, first, second)
+            far_oth[v, n] = jnp.where(core == 0, second, first)
+
+    def pack_of(ref, v, m):
+        return jnp.where(row < HALO, ref[v, 2 * m], ref[v, 2 * m + 1])
+
+    for m in range(packs):
+        centre = [pack_of(far_own, v, m) for v in range(nvar)]
+        weights = [
+            [
+                jnp.where(
+                    row < HALO,
+                    spectral_entry(2 * m - j - skip, 2 * ninst),
+                    spectral_entry(2 * m + 1 - j - skip, 2 * ninst),
+                )
+                for j in range(ninst)
+            ]
+            for skip in (0, ninst)
+        ]
+        for u in range(nvar):
+            z = sum(jac(1, u, v) * centre[v] for v in range(nvar))
+            rest = z + 4.0 * VISCOUS * centre[u]
+            for j in range(ninst):
+                rest += weights[0][j] * far_own[u, j] + weights[1][j] * far_oth[u, j]
+            at = lines_of(packs, u, m)
+            rest_ref[at, :] = rest
+            parts_ref[at, 0:axial] = z
+            parts_ref[at, axial : 2 * axial] = centre[u]
+    rest_ref[...] = rest_ref[...] - times(parts_ref[...], shift_ref[...])
+
+    half = jnp.where(low, 0.5, -0.5)
+    for m in range(packs):
+        slope, around = [], []
+        for v in range(nvar):
+            c = pack_of(far_own, v, m)
+            behind = shifted(c, 2)
+            slope.append(half * (c - behind))
+            around.append(c + behind)
+        for u in range(nvar):
+            at = lines_of(packs, u, m)
+            r = shifted(rest_ref[at, :], 1) - VISCOUS * around[u]
+            for v in range(nvar):
+                r += jac(0, u, v) * slope[v]
+            moved = [r, *(shifted(r, s) for s in range(1, SWEEPS + 1))]
+            sums = [
+                sum(spread_weight(j, SWEEPS - s) * moved[s] for s in range(j, SWEEPS + 1))
+                for j in range(SWEEPS + 1)
+            ]
+            rest_ref[at, :] = sums[0]
+            for j in range(1, SWEEPS + 1):
+                terms_ref[at, (j - 1) * axial : j * axial] = sums[j]
+    rest_ref[...] = rest_ref[...] + times(terms_ref[...], sweep_ref[...])
+
     step = step_ref[...]
     lane = lax.broadcasted_iota(jnp.int32, (ROWS, LANES), 1)
+    reached = side >= HALO
     for n in range(ninst):
         for u in range(nvar):
-            tiles = [base_ref[lines_of(u, n), t : t + LANES] for t in range(0, axial, LANES)]
+            far = rest_ref[lines_of(packs, u, n // 2), :]
+            turned = pltpu.roll(far, HALO, 0)
+            stays = (1 - n % 2) == jnp.where(low, 0, 1)
+            far = jnp.where(reached, jnp.where(stays, far, turned), 0.0)
+            tiles = [far[:, t : t + LANES] for t in range(0, axial, LANES)]
             group = (u * ninst + n) * GROUP
             for plane_no, plane in enumerate(planes):
                 tile, at = divmod(plane - SWEEPS, LANES)
@@ -306,9 +391,10 @@
                 )
                 inside = (lane >= at) & (lane < at + GROUP)
                 tiles[tile] = tiles[tile] + jnp.where(inside, moved, 0.0)
-            swept = jnp.concatenate(tiles, axis=1)
-            out_ref[u, n] = swept
-            new_ref[u, n] = own_ref[u, n] - step * swept
+            more = jnp.concatenate(tiles, axis=1)
+            at = lines_of(ninst, u, n)
+            out_ref[u, n] = base_ref[at, :] + more
+            new_ref[u, n] = before_ref[at, :] - step * more
 
 
 def here(array):
@@ -339,7 +425,7 @@
         out_specs=(vmem,) * 3,
         compiler_params=params,
     )(flow_state)
-    own = here(own)
+    staged, own = own, here(own)
     line = pl.pallas_call(
         functools.partial(line_kernel, planes),
         out_shape=pltpu.VMEM((rows, LANES), jnp.float32),
@@ -355,7 +441,8 @@
                 lines, both, [(2 * i + c, 2 * (i ^ (1 << bit)) + 1 - c) for i in range(spaces) for c in (0, 1)]
             )
         )
-        lines = jnp.concatenate([lines, got[-1]], axis=0)
+        parts = (lines, got[-1])
+        lines = jnp.concatenate(parts, axis=0)
 
     edge = pl.pallas_call(
         edge_kernel,
@@ -389,24 +476,37 @@
     )(jac_pitch, jac_axial, partner, iface_index, own, other, pseudo_step, got[0])
 
     lined = nvar * ninst * rows
-    return pl.pallas_call(
-        functools.partial(step_kernel, planes, len(far)),
-        out_shape=(jax.ShapeDtypeStruct(flow_state.shape, jnp.float32),) * 2,
-        in_specs=[vmem] * (11 + len(far)),
-        out_specs=(vmem, vmem),
+    base = pl.pallas_call(
+        functools.partial(near_kernel, planes),
+        out_shape=pltpu.VMEM((lined, axial), jnp.float32),
+        in_specs=[vmem] * 6,
+        out_specs=vmem,
         scratch_shapes=[
             block,
             block,
             pltpu.VMEM((lined, 2 * axial), jnp.float32),
             pltpu.VMEM((lined, axial), jnp.float32),
             pltpu.VMEM((lined, SWEEPS * axial), jnp.float32),
-            pltpu.VMEM((lined, axial), jnp.float32),
         ],
         compiler_params=params,
-    )(
-        own, other, here(near), *far,
-        *[here(a) for a in (local, jac, shift, sweep, lines, pick, mix, step)],
-    )
+    )(own, *[here(a) for a in (near, local, jac, shift, sweep)])
+
+    before = (staged - step * base.reshape(staged.shape)).reshape(lined, axial)
+
+    return pl.pallas_call(
+        functools.partial(step_kernel, planes, len(far)),
+        out_shape=(jax.ShapeDtypeStruct(flow_state.shape, jnp.float32),) * 2,
+        in_specs=[vmem] * (10 + len(far)),
+        out_specs=(vmem, vmem),
+        scratch_shapes=[
+            block,
+            block,
+            pltpu.VMEM((lined // 2, 2 * axial), jnp.float32),
+            pltpu.VMEM((lined // 2, axial), jnp.float32),
+            pltpu.VMEM((lined // 2, SWEEPS * axial), jnp.float32),
+        ],
+        compiler_params=params,
+    )(here(before), here(base), *far, *[here(a) for a in (jac, shift, sweep, *parts, pick, mix, step)])
 
 
 def solution(mesh):

time: 18.1 us -> 17.6 us (0.972)
  waiting for transfers between devices: 2.54 us -> 1.34 us
  Pallas kernels: 3.72 us -> 4.45 us
    pallas_call x0 -> x1, Pallas kernels: none -> 1.24 us  [shards(): pl.pallas_call(functools.partial(near_kernel, planes), out_shape=pltpu.VM...]
    ppermute x3, waiting for transfers between devices: 2 us -> 1.13 us  [shards(): lax.ppermute(lines, both, [(2 * i + c, 2 * (i ^ 1 << bit) + 1 - c) for i...]
    pallas_call x1, Pallas kernels: 2.21 us -> 1.68 us  [shards(): pl.pallas_call(functools.partial(step_kernel, planes, len(far)), out_shap...]
    ppermute x2, waiting for transfers between devices: 0.33 us -> 0.01 us  [shards(): lax.ppermute(near[v:v + cut], 'inst', cores)]
  transfers between devices with their start and end apart: 7 -> 7, of which waited for: 4 -> 2; matrix products, arithmetic and copies ran while one was open for 0% -> 0% of each run, Pallas kernels for 7% -> 15%
where the time goes in v5:
time: 17.6 us; the launch traced here: 17.5 us
  starting transfers between devices  9.97 us (57%)
  Pallas kernels  4.45 us (25%)
  waiting for transfers between devices  1.34 us (8%)
  local copies, waits for them, and re-layouts  0.97 us (6%)
  between operations  0.73 us (4%)
    ppermute x3, starting transfers between devices, shards(): lax.ppermute(lines, both, [(2 * i + c, 2 * (i ^ 1 << bit) + 1 - c) for i...  7.32 us
    pallas_call x1, Pallas kernels, shards(): pl.pallas_call(functools.partial(step_kernel, planes, len(far)), out_shap...  1.68 us
    ppermute x1, starting transfers between devices, shards(): near = lax.ppermute(edge, both, pairs)  1.56 us
    pallas_call x1, Pallas kernels, shards(): pl.pallas_call(functools.partial(near_kernel, planes), out_shape=pltpu.VM...  1.24 us
    ppermute x3, waiting for transfers between devices, shards(): lax.ppermute(lines, both, [(2 * i + c, 2 * (i ^ 1 << bit) + 1 - c) for i...  1.13 us
    pallas_call x1, Pallas kernels, shards(): pl.pallas_call(functools.partial(prepare_kernel, planes, spaces), out_sha...  1.1 us
    unnamed x12, local copies, waits for them, and re-layouts  0.95 us
    ppermute x2, starting transfers between devices, shards(): lax.ppermute(near[v:v + cut], 'inst', cores)  0.58 us
  transfers between devices with their start and end apart: 7, of which 2 were waited for; matrix products, arithmetic and copies ran while one was open for 0% of the time, Pallas kernels for 15%

profile of v5, /device:TPU:0, one launch (start us, length us, event | category | flops | bytes accessed | tf_op | source)
XLA Modules:
  0.0 17.5 jit_solution(14072096960856701520)
XLA Ops:
  0.6 0.5 %collective-permute-start = (f32[6,4,8,256]{3,2,1,0:T(8,128)}, f32[6,4,8,256]{3,2,1,0:T(8,128)S(1)}, u32[]{:S(2)}, u32[]{:S(2)}) collective-permute-start(f32[6,4,8,256]{3,2,1,0:T(8,128)} %flow_ref.1), channel_id=1, source_target_pairs={{0,1},{1,0},{2,3},{3,2},{4,5},{5,4},{6,7},{7,6},{8,9},{9,8},{10,11... | collective-permute-start | bytes 589832 | tf_op jit(solution)/shard_map/ppermute | solution.py:416
  1.1 0.0 copy-start
  1.1 0.9 %copy-done = f32[6,4,8,256]{3,2,1,0:T(8,128)S(1)} copy-done((f32[6,4,8,256]{3,2,1,0:T(8,128)S(1)}, f32[6,4,8,256]{3,2,1,0:T(8,128)}, u32[]{:S(2)}) %copy-start) | copy-done | bytes 196632
  2.1 0.1 shard_map.77
  2.2 0.2 %collective-permute-done.oth_ref = f32[6,4,8,256]{3,2,1,0:T(8,128)S(1)} collective-permute-done((f32[6,4,8,256]{3,2,1,0:T(8,128)}, f32[6,4,8,256]{3,2,1,0:T(8,128)S(1)}, u32[]{:S(2)}, u32[]{:S(2)}) %collective-permute-start) | collective-permute-done | bytes 196640 | tf_op jit(solution)/shard_map/ppermute | solution.py:416
  2.4 0.2 %shard_map.78.after_ref = f32[8,128]{1,0:T(8,128)S(1)} custom-call(f32[6,4,8,256]{3,2,1,0:T(8,128)S(1)} %get-tuple-element.10.own_ref.refs_0_, f32[6,4,8,256]{3,2,1,0:T(8,128)S(1)} %collective-permute-done.oth_ref), custom_call_target="tpu_custom_call" | custom-call | tf_op jit(solution)/shard_map/pallas_call | solution.py:429
  2.7 2.7 %collective-permute-start.1 = (f32[8,128]{1,0:T(8,128)S(1)}, f32[8,128]{1,0:T(8,128)S(1)}, u32[]{:S(2)}, u32[]{:S(2)}) collective-permute-start(f32[8,128]{1,0:T(8,128)S(1)} %shard_map.78.after_ref), channel_id=1, source_target_pairs={{0,5},{1,4},{2,7},{3,6},{4,1},{5,0},{6,3},{7,2},{8,13},{9,12},{10,... | collective-permute-start | bytes 12296 | tf_op jit(solution)/shard_map/ppermute | solution.py:440
  5.4 0.0 copy-start.4
  5.4 0.0 copy-start.5
  5.4 0.1 shard_map.80
  5.4 0.0 copy-start.1
  5.4 0.0 copy-start.2
  5.4 0.0 copy-start.3
  5.5 1.6 %collective-permute-start.2 = (f32[6,4,8,256]{3,2,1,0:T(8,128)S(1)}, f32[6,4,8,256]{3,2,1,0:T(8,128)S(1)}, u32[]{:S(2)}, u32[]{:S(2)}) collective-permute-start(f32[6,4,8,256]{3,2,1,0:T(8,128)S(1)} %shard_map.80), channel_id=1, source_target_pairs={{0,2},{1,15},{2,0},{3,5},{4,6},{5,3},{6,4},{7,9},{8,10},{9,7},{10,... | collective-permute-start | bytes 589832 | tf_op jit(solution)/shard_map/ppermute | solution.py:458
  7.0 0.0 collective-permute-done.1.after_ref
  7.0 2.4 %collective-permute-start.5 = (f32[16,128]{1,0:T(8,128)S(1)}, f32[16,128]{1,0:T(8,128)S(1)}, u32[]{:S(2)}, u32[]{:S(2)}) collective-permute-start(f32[16,128]{1,0:T(8,128)S(1)} %pad_maximum_fusion.1), channel_id=1, source_target_pairs={{0,9},{1,8},{2,11},{3,10},{4,13},{5,12},{6,15},{7,14},{8,1},{9,0},... | collective-permute-start | bytes 24584 | tf_op jit(solution)/shard_map/ppermute | solution.py:440
  9.4 0.0 copy-done.4
  9.4 0.0 copy-done.5
  9.4 0.0 copy-done.1
  9.4 0.0 copy-done.2
  9.4 0.0 copy-done.3
  9.4 1.1 %shard_map.79 = (f32[8,256]{1,0:T(8,128)S(1)}, f32[6,4,8,256]{3,2,1,0:T(8,128)S(1)}, f32[72,256]{1,0:T(8,128)S(1)}, f32[32,64]{1,0:T(8,128)S(1)}, f32[2,128,256]{2,1,0:T(8,128)S(1)}) custom-call(f32[6,6]{1,0:T(8,128)S(1)} %copy-done.2, f32[6,6]{1,0:T(8,128)S(1)} %copy-done.3, s32[2,8]{1,0:T(2,128)S(1)} %copy-done.4, s32[2,8]{1,0:T(2,128)S(1)} %copy-done.5, ...), custom_call_target="tpu_custom_call" | custom-call | tf_op jit(solution)/shard_map/pallas_call | solution.py:464
  10.5 1.1 %collective-permute-done.5 = f32[16,128]{1,0:T(8,128)S(1)} collective-permute-done((f32[16,128]{1,0:T(8,128)S(1)}, f32[16,128]{1,0:T(8,128)S(1)}, u32[]{:S(2)}, u32[]{:S(2)}) %collective-permute-start.5) | collective-permute-done | bytes 8224 | tf_op jit(solution)/shard_map/ppermute | solution.py:440
  11.7 2.2 %collective-permute-start.6 = (f32[32,128]{1,0:T(8,128)S(1)}, f32[32,128]{1,0:T(8,128)S(1)}, u32[]{:S(2)}, u32[]{:S(2)}) collective-permute-start(f32[32,128]{1,0:T(8,128)S(1)} %pad_maximum_fusion.refs_7_), channel_id=1, source_target_pairs={{0,3},{1,2},{2,1},{3,0},{4,7},{5,6},{6,5},{7,4},{8,11},{9,10},{10,... | collective-permute-start | bytes 49160 | tf_op jit(solution)/shard_map/ppermute | solution.py:440
  13.9 0.0 collective-permute-done.2.refs_1_
  13.9 0.5 %collective-permute-start.3 = (f32[3,4,8,256]{3,2,1,0:T(8,128)S(1)}, f32[3,4,8,256]{3,2,1,0:T(8,128)S(1)}, u32[]{:S(2)}, u32[]{:S(2)}) collective-permute-start(f32[3,4,8,256]{3,2,1,0:T(8,128)S(1)} %get-tuple-element.19), channel_id=1, source_target_pairs={{0,1},{1,0},{2,3},{3,2},{4,5},{5,4},{6,7},{7,6},{8,9},{9,8},{10,11... | collective-permute-start | bytes 294920 | tf_op jit(solution)/shard_map/ppermute | solution.py:461
  14.4 0.1 collective-permute-start.4
  14.5 1.2 %shard_map.81.refs_1_ = f32[192,256]{1,0:T(8,128)S(1)} custom-call(f32[6,4,8,256]{3,2,1,0:T(8,128)S(1)} %get-tuple-element.10.own_ref.refs_0_, f32[6,4,8,256]{3,2,1,0:T(8,128)S(1)} %collective-permute-done.2.refs_1_, f32[6,4,8,256]{3,2,1,0:T(8,128)S(1)} %get-tuple-element.12.refs_2_, f32[72,256]{1,0:T(8,128)S(1)} %get-tuple-element.13.refs_3_.refs_4_, ...), custom_call_target="tpu_custom_call" | custom-call | tf_op jit(solution)/shard_map/pallas_call | solution.py:479
  15.8 0.0 collective-permute-done.6.refs_8_
  15.8 0.0 collective-permute-done.3.refs_2_
  15.8 0.0 collective-permute-done.4.refs_3_
  15.8 1.7 %shard_map.82 = (f32[6,4,8,256]{3,2,1,0:T(8,128)}, f32[6,4,8,256]{3,2,1,0:T(8,128)}) custom-call(f32[192,256]{1,0:T(8,128)S(1)} %bitcast.3, f32[192,256]{1,0:T(8,128)S(1)} %shard_map.81.refs_1_, f32[3,4,8,256]{3,2,1,0:T(8,128)S(1)} %collective-permute-done.3.refs_2_, f32[3,4,8,256]{3,2,1,0:T(8,128)S(1)} %collective-permute-done.4.refs_3_, ...), custom_call_target="tpu_custom_call" | custom-call | tf_op jit(solution)/shard_map/pallas_call | solution.py:496
  (4 shorter events, 0.0 us)
Async XLA Ops:
  0.6 1.8 %collective-permute-start = (f32[6,4,8,256]{3,2,1,0:T(8,128)}, f32[6,4,8,256]{3,2,1,0:T(8,128)S(1)}, u32[]{:S(2)}, u32[]{:S(2)}) collective-permute-start(f32[6,4,8,256]{3,2,1,0:T(8,128)} %flow_ref.1), channel_id=1, source_target_pairs={{0,1},{1,0},{2,3},{3,2},{4,5},{5,4},{6,7},{7,6},{8,9},{9,8},{10,11... | collective-permute-start | bytes 589832 | tf_op jit(solution)/shard_map/ppermute | solution.py:416
  1.1 0.9 %copy-start = (f32[6,4,8,256]{3,2,1,0:T(8,128)S(1)}, f32[6,4,8,256]{3,2,1,0:T(8,128)}, u32[]{:S(2)}) copy-start(f32[6,4,8,256]{3,2,1,0:T(8,128)} %flow_ref.1) | copy-start | bytes 589828
  2.7 4.4 %collective-permute-start.1 = (f32[8,128]{1,0:T(8,128)S(1)}, f32[8,128]{1,0:T(8,128)S(1)}, u32[]{:S(2)}, u32[]{:S(2)}) collective-permute-start(f32[8,128]{1,0:T(8,128)S(1)} %shard_map.78.after_ref), channel_id=1, source_target_pairs={{0,5},{1,4},{2,7},{3,6},{4,1},{5,0},{6,3},{7,2},{8,13},{9,12},{10,... | collective-permute-start | bytes 12296 | tf_op jit(solution)/shard_map/ppermute | solution.py:440
  5.4 4.1 %copy-start.4 = (s32[2,8]{1,0:T(2,128)S(1)}, s32[2,8]{1,0:T(2,128)}, u32[]{:S(2)}) copy-start(s32[2,8]{1,0:T(2,128)} %partner_ref.1) | copy-start | bytes 196
  5.4 4.1 %copy-start.5 = (s32[2,8]{1,0:T(2,128)S(1)}, s32[2,8]{1,0:T(2,128)}, u32[]{:S(2)}) copy-start(s32[2,8]{1,0:T(2,128)} %index_ref.1) | copy-start | bytes 196
  5.4 4.0 %copy-start.1 = (f32[8,256]{1,0:T(8,128)S(1)}, f32[8,256]{1,0:T(8,128)}, u32[]{:S(2)}) copy-start(f32[8,256]{1,0:T(8,128)} %step_in_ref.1) | copy-start | bytes 24580
  5.4 4.0 %copy-start.2 = (f32[6,6]{1,0:T(8,128)S(1)}, f32[6,6]{1,0:T(8,128)}, u32[]{:S(2)}) copy-start(f32[6,6]{1,0:T(8,128)} %jac_pitch_ref.1) | copy-start | bytes 436
  5.4 4.0 %copy-start.3 = (f32[6,6]{1,0:T(8,128)S(1)}, f32[6,6]{1,0:T(8,128)}, u32[]{:S(2)}) copy-start(f32[6,6]{1,0:T(8,128)} %jac_axial_ref.1) | copy-start | bytes 436
  5.5 8.4 %collective-permute-start.2 = (f32[6,4,8,256]{3,2,1,0:T(8,128)S(1)}, f32[6,4,8,256]{3,2,1,0:T(8,128)S(1)}, u32[]{:S(2)}, u32[]{:S(2)}) collective-permute-start(f32[6,4,8,256]{3,2,1,0:T(8,128)S(1)} %shard_map.80), channel_id=1, source_target_pairs={{0,2},{1,15},{2,0},{3,5},{4,6},{5,3},{6,4},{7,9},{8,10},{9,7},{10,... | collective-permute-start | bytes 589832 | tf_op jit(solution)/shard_map/ppermute | solution.py:458
  7.0 4.6 %collective-permute-start.5 = (f32[16,128]{1,0:T(8,128)S(1)}, f32[16,128]{1,0:T(8,128)S(1)}, u32[]{:S(2)}, u32[]{:S(2)}) collective-permute-start(f32[16,128]{1,0:T(8,128)S(1)} %pad_maximum_fusion.1), channel_id=1, source_target_pairs={{0,9},{1,8},{2,11},{3,10},{4,13},{5,12},{6,15},{7,14},{8,1},{9,0},... | collective-permute-start | bytes 24584 | tf_op jit(solution)/shard_map/ppermute | solution.py:440
  11.7 4.1 %collective-permute-start.6 = (f32[32,128]{1,0:T(8,128)S(1)}, f32[32,128]{1,0:T(8,128)S(1)}, u32[]{:S(2)}, u32[]{:S(2)}) collective-permute-start(f32[32,128]{1,0:T(8,128)S(1)} %pad_maximum_fusion.refs_7_), channel_id=1, source_target_pairs={{0,3},{1,2},{2,1},{3,0},{4,7},{5,6},{6,5},{7,4},{8,11},{9,10},{10,... | collective-permute-start | bytes 49160 | tf_op jit(solution)/shard_map/ppermute | solution.py:440
  13.9 1.9 %collective-permute-start.3 = (f32[3,4,8,256]{3,2,1,0:T(8,128)S(1)}, f32[3,4,8,256]{3,2,1,0:T(8,128)S(1)}, u32[]{:S(2)}, u32[]{:S(2)}) collective-permute-start(f32[3,4,8,256]{3,2,1,0:T(8,128)S(1)} %get-tuple-element.19), channel_id=1, source_target_pairs={{0,1},{1,0},{2,3},{3,2},{4,5},{5,4},{6,7},{7,6},{8,9},{9,8},{10,11... | collective-permute-start | bytes 294920 | tf_op jit(solution)/shard_map/ppermute | solution.py:461
  14.4 1.4 %collective-permute-start.4 = (f32[3,4,8,256]{3,2,1,0:T(8,128)S(1)}, f32[3,4,8,256]{3,2,1,0:T(8,128)S(1)}, u32[]{:S(2)}, u32[]{:S(2)}) collective-permute-start(f32[3,4,8,256]{3,2,1,0:T(8,128)S(1)} %get-tuple-element.18), channel_id=1, source_target_pairs={{0,1},{1,0},{2,3},{3,2},{4,5},{5,4},{6,7},{7,6},{8,9},{9,8},{10,11... | collective-permute-start | bytes 294920 | tf_op jit(solution)/shard_map/ppermute | solution.py:461

commit v6 on v5

--- a/solution.py
+++ b/solution.py
@@ -44,11 +44,36 @@
 
 def round_bits(spaces):
     bits = list(range(spaces.bit_length() - 1))
-    return bits[1:] + bits[:1]
-
-
-def stage_kernel(planes, flow_ref, own_ref, shift_ref, sweep_ref):
+    return bits[:1] + bits[:0:-1]
+
+
+def pack_lines(planes, field_ref, half, line):
+    nvar, ninst = field_ref.shape[:2]
+    lane = lax.broadcasted_iota(jnp.int32, (ROWS, LANES), 1)
+    for plane_no, plane in enumerate(planes):
+        for v in range(nvar):
+            for n in range(ninst):
+                at = (plane_no * nvar + v) * 2 * ninst + half * ninst + n
+                cell = jnp.broadcast_to(field_ref[v, n, :, plane - 1 : plane], (ROWS, LANES))
+                line = jnp.where(lane == at, cell, line)
+    return line
+
+
+def line_kernel(planes, half_ref, oth_ref, line_ref):
+    ninst = oth_ref.shape[1]
+    line = pack_lines(planes, oth_ref, 1, half_ref[...])
+    lane = lax.broadcasted_iota(jnp.int32, (ROWS, LANES), 1)
+    swapped = jnp.where(
+        lax.rem(lane, 2 * ninst) < ninst,
+        pltpu.roll(line, LANES - ninst, 1),
+        pltpu.roll(line, ninst, 1),
+    )
+    line_ref[...] = jnp.where(lax.axis_index("inst") == 0, line, swapped)
+
+
+def stage_kernel(planes, flow_ref, own_ref, half_ref, shift_ref, sweep_ref):
     own_ref[...] = flow_ref[...]
+    half_ref[...] = pack_lines(planes, flow_ref, 0, jnp.zeros((ROWS, LANES), jnp.float32))
     axial = flow_ref.shape[3]
     source = lax.broadcasted_iota(jnp.int32, (axial, axial), 0)
     target = lax.broadcasted_iota(jnp.int32, (axial, axial), 1)
@@ -68,26 +93,6 @@
     thrice = jnp.where(far == 3, 1.0, jnp.where(far == 1, jnp.where(beside, 2.0, 3.0), 0.0))
     for power, value in enumerate((once, twice, thrice)):
         sweep_ref[power * axial : (power + 1) * axial, :] = value.astype(jnp.bfloat16)
-
-
-def line_kernel(planes, own_ref, oth_ref, line_ref):
-    core = lax.axis_index("inst")
-    nvar, ninst = own_ref.shape[:2]
-    lane = lax.broadcasted_iota(jnp.int32, (ROWS, LANES), 1)
-    line = jnp.zeros((ROWS, LANES), jnp.float32)
-    for plane_no, plane in enumerate(planes):
-        for v in range(nvar):
-            for half, ref in enumerate((own_ref, oth_ref)):
-                for n in range(ninst):
-                    at = (plane_no * nvar + v) * 2 * ninst + half * ninst + n
-                    cell = jnp.broadcast_to(ref[v, n, :, plane - 1 : plane], (ROWS, LANES))
-                    line = jnp.where(lane == at, cell, line)
-    swapped = jnp.where(
-        lax.rem(lane, 2 * ninst) < ninst,
-        pltpu.roll(line, LANES - ninst, 1),
-        pltpu.roll(line, ninst, 1),
-    )
-    line_ref[...] = jnp.where(core == 0, line, swapped)
 
 
 def low_side():
@@ -414,15 +419,16 @@
     cores = [(0, 1), (1, 0)]
 
     other = here(lax.ppermute(flow_state, "inst", cores))
-    own, shift, sweep = pl.pallas_call(
+    own, half, shift, sweep = pl.pallas_call(
         functools.partial(stage_kernel, planes),
         out_shape=(
             block,
+            pltpu.VMEM((rows, LANES), jnp.float32),
             pltpu.VMEM((2 * axial, axial), jnp.bfloat16),
             pltpu.VMEM((SWEEPS * axial, axial), jnp.bfloat16),
         ),
         in_specs=[vmem],
-        out_specs=(vmem,) * 3,
+        out_specs=(vmem,) * 4,
         compiler_params=params,
     )(flow_state)
     staged, own = own, here(own)
@@ -432,7 +438,7 @@
         in_specs=[vmem, vmem],
         out_specs=vmem,
         compiler_params=params,
-    )(own, other)
+    )(here(half), other)
 
     lines, got = line, []
     for bit in round_bits(spaces):

time: 17.6 us -> 17.6 us (level)
  the two profiles are of different devices: /device:TPU:0 before, /device:TPU:1 now
where the time goes in v6:
time: 17.6 us; the launch traced here: 17.4 us
  starting transfers between devices  7.64 us (43%)
  Pallas kernels  4.45 us (25%)
  waiting for transfers between devices  3.62 us (21%)
  local copies, waits for them, and re-layouts  0.97 us (6%)
  between operations  0.72 us (4%)
    ppermute x3, starting transfers between devices, shards(): lax.ppermute(lines, both, [(2 * i + c, 2 * (i ^ 1 << bit) + 1 - c) for i...  3.59 us
    ppermute x1, starting transfers between devices, shards(): near = lax.ppermute(edge, both, pairs)  3.36 us
    ppermute x3, waiting for transfers between devices, shards(): lax.ppermute(lines, both, [(2 * i + c, 2 * (i ^ 1 << bit) + 1 - c) for i...  3.15 us
    pallas_call x1, Pallas kernels, shards(): pl.pallas_call(functools.partial(step_kernel, planes, len(far)), out_shap...  1.68 us
    pallas_call x1, Pallas kernels, shards(): pl.pallas_call(functools.partial(near_kernel, planes), out_shape=pltpu.VM...  1.24 us
    pallas_call x1, Pallas kernels, shards(): pl.pallas_call(functools.partial(prepare_kernel, planes, spaces), out_sha...  1.1 us
    unnamed x12, local copies, waits for them, and re-layouts  0.95 us
    ppermute x2, starting transfers between devices, shards(): lax.ppermute(near[v:v + cut], 'inst', cores)  0.57 us
  transfers between devices with their start and end apart: 7, of which 3 were waited for; matrix products, arithmetic and copies ran while one was open for 0% of the time, Pallas kernels for 15%

profile of v6, /device:TPU:1, one launch (start us, length us, event | category | flops | bytes accessed | tf_op | source)
XLA Modules:
  0.0 17.4 jit_solution(4320591111486689217)
XLA Ops:
  0.6 0.1 collective-permute-start
  0.8 0.0 copy-start
  0.8 0.9 %copy-done = f32[6,4,8,256]{3,2,1,0:T(8,128)S(1)} copy-done((f32[6,4,8,256]{3,2,1,0:T(8,128)S(1)}, f32[6,4,8,256]{3,2,1,0:T(8,128)}, u32[]{:S(2)}) %copy-start) | copy-done | bytes 196632
  1.7 0.2 %shard_map.77 = (f32[6,4,8,256]{3,2,1,0:T(8,128)S(1)}, f32[8,128]{1,0:T(8,128)S(1)}, bf16[512,256]{1,0:T(8,128)(2,1)S(1)}, bf16[768,256]{1,0:T(8,128)(2,1)S(1)}) custom-call(f32[6,4,8,256]{3,2,1,0:T(8,128)S(1)} %copy-done), custom_call_target="tpu_custom_call" | custom-call | tf_op jit(solution)/shard_map/pallas_call | solution.py:422
  1.9 0.5 %collective-permute-done.oth_ref = f32[6,4,8,256]{3,2,1,0:T(8,128)S(1)} collective-permute-done((f32[6,4,8,256]{3,2,1,0:T(8,128)}, f32[6,4,8,256]{3,2,1,0:T(8,128)S(1)}, u32[]{:S(2)}, u32[]{:S(2)}) %collective-permute-start) | collective-permute-done | bytes 196640 | tf_op jit(solution)/shard_map/ppermute | solution.py:421
  2.3 0.2 %shard_map.78.after_ref = f32[8,128]{1,0:T(8,128)S(1)} custom-call(f32[8,128]{1,0:T(8,128)S(1)} %get-tuple-element.12.half_ref, f32[6,4,8,256]{3,2,1,0:T(8,128)S(1)} %collective-permute-done.oth_ref), custom_call_target="tpu_custom_call" | custom-call | tf_op jit(solution)/shard_map/pallas_call | solution.py:435
  2.5 2.6 %collective-permute-start.1 = (f32[8,128]{1,0:T(8,128)S(1)}, f32[8,128]{1,0:T(8,128)S(1)}, u32[]{:S(2)}, u32[]{:S(2)}) collective-permute-start(f32[8,128]{1,0:T(8,128)S(1)} %shard_map.78.after_ref), channel_id=1, source_target_pairs={{0,3},{1,2},{2,1},{3,0},{4,7},{5,6},{6,5},{7,4},{8,11},{9,10},{10,... | collective-permute-start | bytes 12296 | tf_op jit(solution)/shard_map/ppermute | solution.py:446
  5.1 0.0 copy-start.4
  5.1 0.0 copy-start.5
  5.1 0.1 shard_map.80
  5.2 0.0 copy-start.1
  5.2 0.0 copy-start.2
  5.2 0.0 copy-start.3
  5.2 3.4 %collective-permute-start.2 = (f32[6,4,8,256]{3,2,1,0:T(8,128)S(1)}, f32[6,4,8,256]{3,2,1,0:T(8,128)S(1)}, u32[]{:S(2)}, u32[]{:S(2)}) collective-permute-start(f32[6,4,8,256]{3,2,1,0:T(8,128)S(1)} %shard_map.80), channel_id=1, source_target_pairs={{0,2},{1,15},{2,0},{3,5},{4,6},{5,3},{6,4},{7,9},{8,10},{9,7},{10,... | collective-permute-start | bytes 589832 | tf_op jit(solution)/shard_map/ppermute | solution.py:464
  8.6 0.0 collective-permute-done.1.after_ref
  8.6 0.7 %collective-permute-start.5 = (f32[16,128]{1,0:T(8,128)S(1)}, f32[16,128]{1,0:T(8,128)S(1)}, u32[]{:S(2)}, u32[]{:S(2)}) collective-permute-start(f32[16,128]{1,0:T(8,128)S(1)} %pad_maximum_fusion.1), channel_id=1, source_target_pairs={{0,9},{1,8},{2,11},{3,10},{4,13},{5,12},{6,15},{7,14},{8,1},{9,0},... | collective-permute-start | bytes 24584 | tf_op jit(solution)/shard_map/ppermute | solution.py:446
  9.3 0.0 copy-done.4
  9.3 0.0 copy-done.5
  9.3 0.0 copy-done.1
  9.3 0.0 copy-done.2
  9.3 0.0 copy-done.3
  9.3 1.1 %shard_map.79 = (f32[8,256]{1,0:T(8,128)S(1)}, f32[6,4,8,256]{3,2,1,0:T(8,128)S(1)}, f32[72,256]{1,0:T(8,128)S(1)}, f32[32,64]{1,0:T(8,128)S(1)}, f32[2,128,256]{2,1,0:T(8,128)S(1)}) custom-call(f32[6,6]{1,0:T(8,128)S(1)} %copy-done.2, f32[6,6]{1,0:T(8,128)S(1)} %copy-done.3, s32[2,8]{1,0:T(2,128)S(1)} %copy-done.4, s32[2,8]{1,0:T(2,128)S(1)} %copy-done.5, ...), custom_call_target="tpu_custom_call" | custom-call | tf_op jit(solution)/shard_map/pallas_call | solution.py:470
  10.4 2.2 %collective-permute-done.5 = f32[16,128]{1,0:T(8,128)S(1)} collective-permute-done((f32[16,128]{1,0:T(8,128)S(1)}, f32[16,128]{1,0:T(8,128)S(1)}, u32[]{:S(2)}, u32[]{:S(2)}) %collective-permute-start.5) | collective-permute-done | bytes 8224 | tf_op jit(solution)/shard_map/ppermute | solution.py:446
  12.6 0.3 %collective-permute-start.6 = (f32[32,128]{1,0:T(8,128)S(1)}, f32[32,128]{1,0:T(8,128)S(1)}, u32[]{:S(2)}, u32[]{:S(2)}) collective-permute-start(f32[32,128]{1,0:T(8,128)S(1)} %pad_maximum_fusion.refs_7_), channel_id=1, source_target_pairs={{0,5},{1,4},{2,7},{3,6},{4,1},{5,0},{6,3},{7,2},{8,13},{9,12},{10,... | collective-permute-start | bytes 49160 | tf_op jit(solution)/shard_map/ppermute | solution.py:446
  12.9 0.0 collective-permute-done.2.refs_1_
  12.9 0.1 collective-permute-start.3
  13.0 0.5 %collective-permute-start.4 = (f32[3,4,8,256]{3,2,1,0:T(8,128)S(1)}, f32[3,4,8,256]{3,2,1,0:T(8,128)S(1)}, u32[]{:S(2)}, u32[]{:S(2)}) collective-permute-start(f32[3,4,8,256]{3,2,1,0:T(8,128)S(1)} %get-tuple-element.20), channel_id=1, source_target_pairs={{0,1},{1,0},{2,3},{3,2},{4,5},{5,4},{6,7},{7,6},{8,9},{9,8},{10,11... | collective-permute-start | bytes 294920 | tf_op jit(solution)/shard_map/ppermute | solution.py:467
  13.5 1.2 %shard_map.81.refs_1_ = f32[192,256]{1,0:T(8,128)S(1)} custom-call(f32[6,4,8,256]{3,2,1,0:T(8,128)S(1)} %get-tuple-element.11.own_ref.refs_0_, f32[6,4,8,256]{3,2,1,0:T(8,128)S(1)} %collective-permute-done.2.refs_1_, f32[6,4,8,256]{3,2,1,0:T(8,128)S(1)} %get-tuple-element.14.refs_2_, f32[72,256]{1,0:T(8,128)S(1)} %get-tuple-element.15.refs_3_.refs_4_, ...), custom_call_target="tpu_custom_call" | custom-call | tf_op jit(solution)/shard_map/pallas_call | solution.py:485
  14.8 1.0 %collective-permute-done.6.refs_8_ = f32[32,128]{1,0:T(8,128)S(1)} collective-permute-done((f32[32,128]{1,0:T(8,128)S(1)}, f32[32,128]{1,0:T(8,128)S(1)}, u32[]{:S(2)}, u32[]{:S(2)}) %collective-permute-start.6) | collective-permute-done | bytes 16416 | tf_op jit(solution)/shard_map/ppermute | solution.py:446
  15.7 0.0 collective-permute-done.3.refs_2_
  15.8 0.0 collective-permute-done.4.refs_3_
  15.8 1.7 %shard_map.82 = (f32[6,4,8,256]{3,2,1,0:T(8,128)}, f32[6,4,8,256]{3,2,1,0:T(8,128)}) custom-call(f32[192,256]{1,0:T(8,128)S(1)} %bitcast.3, f32[192,256]{1,0:T(8,128)S(1)} %shard_map.81.refs_1_, f32[3,4,8,256]{3,2,1,0:T(8,128)S(1)} %collective-permute-done.3.refs_2_, f32[3,4,8,256]{3,2,1,0:T(8,128)S(1)} %collective-permute-done.4.refs_3_, ...), custom_call_target="tpu_custom_call" | custom-call | tf_op jit(solution)/shard_map/pallas_call | solution.py:502
  (4 shorter events, 0.0 us)
Async XLA Ops:
  0.6 1.7 %collective-permute-start = (f32[6,4,8,256]{3,2,1,0:T(8,128)}, f32[6,4,8,256]{3,2,1,0:T(8,128)S(1)}, u32[]{:S(2)}, u32[]{:S(2)}) collective-permute-start(f32[6,4,8,256]{3,2,1,0:T(8,128)} %flow_ref.1), channel_id=1, source_target_pairs={{0,1},{1,0},{2,3},{3,2},{4,5},{5,4},{6,7},{7,6},{8,9},{9,8},{10,11... | collective-permute-start | bytes 589832 | tf_op jit(solution)/shard_map/ppermute | solution.py:421
  0.8 0.9 %copy-start = (f32[6,4,8,256]{3,2,1,0:T(8,128)S(1)}, f32[6,4,8,256]{3,2,1,0:T(8,128)}, u32[]{:S(2)}) copy-start(f32[6,4,8,256]{3,2,1,0:T(8,128)} %flow_ref.1) | copy-start | bytes 589828
  2.5 6.1 %collective-permute-start.1 = (f32[8,128]{1,0:T(8,128)S(1)}, f32[8,128]{1,0:T(8,128)S(1)}, u32[]{:S(2)}, u32[]{:S(2)}) collective-permute-start(f32[8,128]{1,0:T(8,128)S(1)} %shard_map.78.after_ref), channel_id=1, source_target_pairs={{0,3},{1,2},{2,1},{3,0},{4,7},{5,6},{6,5},{7,4},{8,11},{9,10},{10,... | collective-permute-start | bytes 12296 | tf_op jit(solution)/shard_map/ppermute | solution.py:446
  5.1 4.1 %copy-start.4 = (s32[2,8]{1,0:T(2,128)S(1)}, s32[2,8]{1,0:T(2,128)}, u32[]{:S(2)}) copy-start(s32[2,8]{1,0:T(2,128)} %partner_ref.1) | copy-start | bytes 196
  5.1 4.1 %copy-start.5 = (s32[2,8]{1,0:T(2,128)S(1)}, s32[2,8]{1,0:T(2,128)}, u32[]{:S(2)}) copy-start(s32[2,8]{1,0:T(2,128)} %index_ref.1) | copy-start | bytes 196
  5.2 4.1 %copy-start.1 = (f32[8,256]{1,0:T(8,128)S(1)}, f32[8,256]{1,0:T(8,128)}, u32[]{:S(2)}) copy-start(f32[8,256]{1,0:T(8,128)} %step_in_ref.1) | copy-start | bytes 24580
  5.2 4.1 %copy-start.2 = (f32[6,6]{1,0:T(8,128)S(1)}, f32[6,6]{1,0:T(8,128)}, u32[]{:S(2)}) copy-start(f32[6,6]{1,0:T(8,128)} %jac_pitch_ref.1) | copy-start | bytes 436
  5.2 4.1 %copy-start.3 = (f32[6,6]{1,0:T(8,128)S(1)}, f32[6,6]{1,0:T(8,128)}, u32[]{:S(2)}) copy-start(f32[6,6]{1,0:T(8,128)} %jac_axial_ref.1) | copy-start | bytes 436
  5.2 7.7 %collective-permute-start.2 = (f32[6,4,8,256]{3,2,1,0:T(8,128)S(1)}, f32[6,4,8,256]{3,2,1,0:T(8,128)S(1)}, u32[]{:S(2)}, u32[]{:S(2)}) collective-permute-start(f32[6,4,8,256]{3,2,1,0:T(8,128)S(1)} %shard_map.80), channel_id=1, source_target_pairs={{0,2},{1,15},{2,0},{3,5},{4,6},{5,3},{6,4},{7,9},{8,10},{9,7},{10,... | collective-permute-start | bytes 589832 | tf_op jit(solution)/shard_map/ppermute | solution.py:464
  8.6 4.0 %collective-permute-start.5 = (f32[16,128]{1,0:T(8,128)S(1)}, f32[16,128]{1,0:T(8,128)S(1)}, u32[]{:S(2)}, u32[]{:S(2)}) collective-permute-start(f32[16,128]{1,0:T(8,128)S(1)} %pad_maximum_fusion.1), channel_id=1, source_target_pairs={{0,9},{1,8},{2,11},{3,10},{4,13},{5,12},{6,15},{7,14},{8,1},{9,0},... | collective-permute-start | bytes 24584 | tf_op jit(solution)/shard_map/ppermute | solution.py:446
  12.6 3.2 %collective-permute-start.6 = (f32[32,128]{1,0:T(8,128)S(1)}, f32[32,128]{1,0:T(8,128)S(1)}, u32[]{:S(2)}, u32[]{:S(2)}) collective-permute-start(f32[32,128]{1,0:T(8,128)S(1)} %pad_maximum_fusion.refs_7_), channel_id=1, source_target_pairs={{0,5},{1,4},{2,7},{3,6},{4,1},{5,0},{6,3},{7,2},{8,13},{9,12},{10,... | collective-permute-start | bytes 49160 | tf_op jit(solution)/shard_map/ppermute | solution.py:446
  12.9 2.8 %collective-permute-start.3 = (f32[3,4,8,256]{3,2,1,0:T(8,128)S(1)}, f32[3,4,8,256]{3,2,1,0:T(8,128)S(1)}, u32[]{:S(2)}, u32[]{:S(2)}) collective-permute-start(f32[3,4,8,256]{3,2,1,0:T(8,128)S(1)} %get-tuple-element.21), channel_id=1, source_target_pairs={{0,1},{1,0},{2,3},{3,2},{4,5},{5,4},{6,7},{7,6},{8,9},{9,8},{10,11... | collective-permute-start | bytes 294920 | tf_op jit(solution)/shard_map/ppermute | solution.py:467
  13.0 2.7 %collective-permute-start.4 = (f32[3,4,8,256]{3,2,1,0:T(8,128)S(1)}, f32[3,4,8,256]{3,2,1,0:T(8,128)S(1)}, u32[]{:S(2)}, u32[]{:S(2)}) collective-permute-start(f32[3,4,8,256]{3,2,1,0:T(8,128)S(1)} %get-tuple-element.20), channel_id=1, source_target_pairs={{0,1},{1,0},{2,3},{3,2},{4,5},{5,4},{6,7},{7,6},{8,9},{9,8},{10,11... | collective-permute-start | bytes 294920 | tf_op jit(solution)/shard_map/ppermute | solution.py:467

commit v7 on v6

--- a/solution.py
+++ b/solution.py
@@ -210,15 +210,20 @@
 
 
 def inflow_spread(planes, lines_refs, pick_ref, mix_ref):
-    exact = dict(precision=lax.Precision.HIGHEST, preferred_element_type=jnp.float32)
     lines = jnp.concatenate([ref[...] for ref in lines_refs], axis=0)
-    facing = jnp.dot(pick_ref[...], lines, **exact)
+    pick, first = pick_ref[...].astype(jnp.bfloat16), lines.astype(jnp.bfloat16)
+    second = (lines - first.astype(jnp.float32)).astype(jnp.bfloat16)
+    plain = dict(preferred_element_type=jnp.float32)
+    facing = jnp.dot(pick, first, **plain) + jnp.dot(pick, second, **plain)
     lane = lax.rem(lax.broadcasted_iota(jnp.int32, (ROWS, 2 * LANES), 1), GROUP)
     spread = []
     for plane_no in range(len(planes)):
-        power = jnp.dot(
-            facing[plane_no * 2 * ROWS : (plane_no + 1) * 2 * ROWS], mix_ref[plane_no], **exact
-        )
+        seen = facing[plane_no * 2 * ROWS : (plane_no + 1) * 2 * ROWS]
+        seen_first, mix_first = seen.astype(jnp.bfloat16), mix_ref[plane_no].astype(jnp.bfloat16)
+        seen_second = (seen - seen_first.astype(jnp.float32)).astype(jnp.bfloat16)
+        mix_second = (mix_ref[plane_no] - mix_first.astype(jnp.float32)).astype(jnp.bfloat16)
+        power = jnp.dot(seen_first, mix_first, **plain)
+        power += jnp.dot(seen_second, mix_first, **plain) + jnp.dot(seen_first, mix_second, **plain)
         total = jnp.zeros((ROWS, 2 * LANES), jnp.float32)
         for m in range(SWEEPS + 1):
             weight = jnp.zeros((ROWS, 2 * LANES), jnp.float32)
@@ -441,12 +446,12 @@
     )(here(half), other)
 
     lines, got = line, []
-    for bit in round_bits(spaces):
-        got.append(
-            lax.ppermute(
-                lines, both, [(2 * i + c, 2 * (i ^ (1 << bit)) + 1 - c) for i in range(spaces) for c in (0, 1)]
-            )
-        )
+    for turn, bit in enumerate(round_bits(spaces)):
+        cross = 1 if turn == 0 else 0
+        swaps = [
+            (2 * i + c, 2 * (i ^ (1 << bit)) + (c ^ cross)) for i in range(spaces) for c in (0, 1)
+        ]
+        got.append(lax.ppermute(lines, both, swaps))
         parts = (lines, got[-1])
         lines = jnp.concatenate(parts, axis=0)
 

time: 17.6 us -> 16.9 us (0.960)
  the two profiles are of different devices: /device:TPU:1 before, /device:TPU:0 now
where the time goes in v7:
time: 16.9 us; the launch traced here: 16.8 us
  starting transfers between devices  8.97 us (53%)
  Pallas kernels  4.38 us (26%)
  waiting for transfers between devices  1.68 us (10%)
  local copies, waits for them, and re-layouts  0.97 us (6%)
  between operations  0.74 us (4%)
    ppermute x3, starting transfers between devices, shards(): got.append(lax.ppermute(lines, both, swaps))  7.53 us
    pallas_call x1, Pallas kernels, shards(): pl.pallas_call(functools.partial(step_kernel, planes, len(far)), out_shap...  1.6 us
    ppermute x3, waiting for transfers between devices, shards(): got.append(lax.ppermute(lines, both, swaps))  1.51 us
    pallas_call x1, Pallas kernels, shards(): pl.pallas_call(functools.partial(near_kernel, planes), out_shape=pltpu.VM...  1.24 us
    pallas_call x1, Pallas kernels, shards(): pl.pallas_call(functools.partial(prepare_kernel, planes, spaces), out_sha...  1.1 us
    unnamed x12, local copies, waits for them, and re-layouts  0.95 us
    ppermute x2, starting transfers between devices, shards(): lax.ppermute(near[v:v + cut], 'inst', cores)  0.57 us
    ppermute x1, starting transfers between devices, shards(): other = here(lax.ppermute(flow_state, 'inst', cores))  0.52 us
  transfers between devices with their start and end apart: 7, of which 3 were waited for; matrix products, arithmetic and copies ran while one was open for 0% of the time, Pallas kernels for 15%

profile of v7, /device:TPU:0, one launch (start us, length us, event | category | flops | bytes accessed | tf_op | source)
XLA Modules:
  0.0 16.8 jit_solution(119156902011563650)
XLA Ops:
  0.6 0.5 %collective-permute-start = (f32[6,4,8,256]{3,2,1,0:T(8,128)}, f32[6,4,8,256]{3,2,1,0:T(8,128)S(1)}, u32[]{:S(2)}, u32[]{:S(2)}) collective-permute-start(f32[6,4,8,256]{3,2,1,0:T(8,128)} %flow_ref.1), channel_id=1, source_target_pairs={{0,1},{1,0},{2,3},{3,2},{4,5},{5,4},{6,7},{7,6},{8,9},{9,8},{10,11... | collective-permute-start | bytes 589832 | tf_op jit(solution)/shard_map/ppermute | solution.py:426
  1.1 0.0 copy-start
  1.1 0.9 %copy-done = f32[6,4,8,256]{3,2,1,0:T(8,128)S(1)} copy-done((f32[6,4,8,256]{3,2,1,0:T(8,128)S(1)}, f32[6,4,8,256]{3,2,1,0:T(8,128)}, u32[]{:S(2)}) %copy-start) | copy-done | bytes 196632
  2.1 0.2 %shard_map.77 = (f32[6,4,8,256]{3,2,1,0:T(8,128)S(1)}, f32[8,128]{1,0:T(8,128)S(1)}, bf16[512,256]{1,0:T(8,128)(2,1)S(1)}, bf16[768,256]{1,0:T(8,128)(2,1)S(1)}) custom-call(f32[6,4,8,256]{3,2,1,0:T(8,128)S(1)} %copy-done), custom_call_target="tpu_custom_call" | custom-call | tf_op jit(solution)/shard_map/pallas_call | solution.py:427
  2.3 0.2 collective-permute-done.oth_ref
  2.4 0.2 %shard_map.78.after_ref = f32[8,128]{1,0:T(8,128)S(1)} custom-call(f32[8,128]{1,0:T(8,128)S(1)} %get-tuple-element.12.half_ref, f32[6,4,8,256]{3,2,1,0:T(8,128)S(1)} %collective-permute-done.oth_ref), custom_call_target="tpu_custom_call" | custom-call | tf_op jit(solution)/shard_map/pallas_call | solution.py:440
  2.6 2.6 %collective-permute-start.1 = (f32[8,128]{1,0:T(8,128)S(1)}, f32[8,128]{1,0:T(8,128)S(1)}, u32[]{:S(2)}, u32[]{:S(2)}) collective-permute-start(f32[8,128]{1,0:T(8,128)S(1)} %shard_map.78.after_ref), channel_id=1, source_target_pairs={{0,3},{1,2},{2,1},{3,0},{4,7},{5,6},{6,5},{7,4},{8,11},{9,10},{10,... | collective-permute-start | bytes 12296 | tf_op jit(solution)/shard_map/ppermute | solution.py:454
  5.2 0.0 copy-start.4
  5.2 0.0 copy-start.5
  5.2 0.1 shard_map.80
  5.3 0.0 copy-start.1
  5.3 0.0 copy-start.2
  5.3 0.0 copy-start.3
  5.3 0.4 %collective-permute-start.2 = (f32[6,4,8,256]{3,2,1,0:T(8,128)S(1)}, f32[6,4,8,256]{3,2,1,0:T(8,128)S(1)}, u32[]{:S(2)}, u32[]{:S(2)}) collective-permute-start(f32[6,4,8,256]{3,2,1,0:T(8,128)S(1)} %shard_map.80), channel_id=1, source_target_pairs={{0,2},{1,15},{2,0},{3,5},{4,6},{5,3},{6,4},{7,9},{8,10},{9,7},{10,... | collective-permute-start | bytes 589832 | tf_op jit(solution)/shard_map/ppermute | solution.py:469
  5.7 0.9 %collective-permute-done.1.after_ref = f32[8,128]{1,0:T(8,128)S(1)} collective-permute-done((f32[8,128]{1,0:T(8,128)S(1)}, f32[8,128]{1,0:T(8,128)S(1)}, u32[]{:S(2)}, u32[]{:S(2)}) %collective-permute-start.1) | collective-permute-done | bytes 4128 | tf_op jit(solution)/shard_map/ppermute | solution.py:454
  6.5 3.1 %collective-permute-start.5 = (f32[16,128]{1,0:T(8,128)S(1)}, f32[16,128]{1,0:T(8,128)S(1)}, u32[]{:S(2)}, u32[]{:S(2)}) collective-permute-start(f32[16,128]{1,0:T(8,128)S(1)} %pad_maximum_fusion.1), channel_id=1, source_target_pairs={{0,8},{1,9},{2,10},{3,11},{4,12},{5,13},{6,14},{7,15},{8,0},{9,1},... | collective-permute-start | bytes 24584 | tf_op jit(solution)/shard_map/ppermute | solution.py:454
  9.6 0.0 copy-done.4
  9.6 0.0 copy-done.5
  9.6 0.0 copy-done.1
  9.6 0.0 copy-done.2
  9.6 0.0 copy-done.3
  9.6 1.1 %shard_map.79 = (f32[8,256]{1,0:T(8,128)S(1)}, f32[6,4,8,256]{3,2,1,0:T(8,128)S(1)}, f32[72,256]{1,0:T(8,128)S(1)}, f32[32,64]{1,0:T(8,128)S(1)}, f32[2,128,256]{2,1,0:T(8,128)S(1)}) custom-call(f32[6,6]{1,0:T(8,128)S(1)} %copy-done.2, f32[6,6]{1,0:T(8,128)S(1)} %copy-done.3, s32[2,8]{1,0:T(2,128)S(1)} %copy-done.4, s32[2,8]{1,0:T(2,128)S(1)} %copy-done.5, ...), custom_call_target="tpu_custom_call" | custom-call | tf_op jit(solution)/shard_map/pallas_call | solution.py:475
  10.7 0.6 %collective-permute-done.5 = f32[16,128]{1,0:T(8,128)S(1)} collective-permute-done((f32[16,128]{1,0:T(8,128)S(1)}, f32[16,128]{1,0:T(8,128)S(1)}, u32[]{:S(2)}, u32[]{:S(2)}) %collective-permute-start.5) | collective-permute-done | bytes 8224 | tf_op jit(solution)/shard_map/ppermute | solution.py:454
  11.4 1.9 %collective-permute-start.6 = (f32[32,128]{1,0:T(8,128)S(1)}, f32[32,128]{1,0:T(8,128)S(1)}, u32[]{:S(2)}, u32[]{:S(2)}) collective-permute-start(f32[32,128]{1,0:T(8,128)S(1)} %pad_maximum_fusion.refs_7_), channel_id=1, source_target_pairs={{0,4},{1,5},{2,6},{3,7},{4,0},{5,1},{6,2},{7,3},{8,12},{9,13},{10,... | collective-permute-start | bytes 49160 | tf_op jit(solution)/shard_map/ppermute | solution.py:454
  13.3 0.0 collective-permute-done.2.refs_1_
  13.3 0.1 collective-permute-start.3
  13.4 0.5 %collective-permute-start.4 = (f32[3,4,8,256]{3,2,1,0:T(8,128)S(1)}, f32[3,4,8,256]{3,2,1,0:T(8,128)S(1)}, u32[]{:S(2)}, u32[]{:S(2)}) collective-permute-start(f32[3,4,8,256]{3,2,1,0:T(8,128)S(1)} %get-tuple-element.20), channel_id=1, source_target_pairs={{0,1},{1,0},{2,3},{3,2},{4,5},{5,4},{6,7},{7,6},{8,9},{9,8},{10,11... | collective-permute-start | bytes 294920 | tf_op jit(solution)/shard_map/ppermute | solution.py:472
  13.8 1.2 %shard_map.81.refs_1_ = f32[192,256]{1,0:T(8,128)S(1)} custom-call(f32[6,4,8,256]{3,2,1,0:T(8,128)S(1)} %get-tuple-element.11.own_ref.refs_0_, f32[6,4,8,256]{3,2,1,0:T(8,128)S(1)} %collective-permute-done.2.refs_1_, f32[6,4,8,256]{3,2,1,0:T(8,128)S(1)} %get-tuple-element.14.refs_2_, f32[72,256]{1,0:T(8,128)S(1)} %get-tuple-element.15.refs_3_.refs_4_, ...), custom_call_target="tpu_custom_call" | custom-call | tf_op jit(solution)/shard_map/pallas_call | solution.py:490
  15.1 0.0 collective-permute-done.6.refs_8_
  15.1 0.0 collective-permute-done.3.refs_2_
  15.2 0.0 collective-permute-done.4.refs_3_
  15.2 1.6 %shard_map.82 = (f32[6,4,8,256]{3,2,1,0:T(8,128)}, f32[6,4,8,256]{3,2,1,0:T(8,128)}) custom-call(f32[192,256]{1,0:T(8,128)S(1)} %bitcast.3, f32[192,256]{1,0:T(8,128)S(1)} %shard_map.81.refs_1_, f32[3,4,8,256]{3,2,1,0:T(8,128)S(1)} %collective-permute-done.3.refs_2_, f32[3,4,8,256]{3,2,1,0:T(8,128)S(1)} %collective-permute-done.4.refs_3_, ...), custom_call_target="tpu_custom_call" | custom-call | tf_op jit(solution)/shard_map/pallas_call | solution.py:507
  (4 shorter events, 0.0 us)
Async XLA Ops:
  0.6 1.8 %collective-permute-start = (f32[6,4,8,256]{3,2,1,0:T(8,128)}, f32[6,4,8,256]{3,2,1,0:T(8,128)S(1)}, u32[]{:S(2)}, u32[]{:S(2)}) collective-permute-start(f32[6,4,8,256]{3,2,1,0:T(8,128)} %flow_ref.1), channel_id=1, source_target_pairs={{0,1},{1,0},{2,3},{3,2},{4,5},{5,4},{6,7},{7,6},{8,9},{9,8},{10,11... | collective-permute-start | bytes 589832 | tf_op jit(solution)/shard_map/ppermute | solution.py:426
  1.1 0.9 %copy-start = (f32[6,4,8,256]{3,2,1,0:T(8,128)S(1)}, f32[6,4,8,256]{3,2,1,0:T(8,128)}, u32[]{:S(2)}) copy-start(f32[6,4,8,256]{3,2,1,0:T(8,128)} %flow_ref.1) | copy-start | bytes 589828
  2.6 3.9 %collective-permute-start.1 = (f32[8,128]{1,0:T(8,128)S(1)}, f32[8,128]{1,0:T(8,128)S(1)}, u32[]{:S(2)}, u32[]{:S(2)}) collective-permute-start(f32[8,128]{1,0:T(8,128)S(1)} %shard_map.78.after_ref), channel_id=1, source_target_pairs={{0,3},{1,2},{2,1},{3,0},{4,7},{5,6},{6,5},{7,4},{8,11},{9,10},{10,... | collective-permute-start | bytes 12296 | tf_op jit(solution)/shard_map/ppermute | solution.py:454
  5.2 4.4 %copy-start.4 = (s32[2,8]{1,0:T(2,128)S(1)}, s32[2,8]{1,0:T(2,128)}, u32[]{:S(2)}) copy-start(s32[2,8]{1,0:T(2,128)} %partner_ref.1) | copy-start | bytes 196
  5.2 4.4 %copy-start.5 = (s32[2,8]{1,0:T(2,128)S(1)}, s32[2,8]{1,0:T(2,128)}, u32[]{:S(2)}) copy-start(s32[2,8]{1,0:T(2,128)} %index_ref.1) | copy-start | bytes 196
  5.3 4.3 %copy-start.1 = (f32[8,256]{1,0:T(8,128)S(1)}, f32[8,256]{1,0:T(8,128)}, u32[]{:S(2)}) copy-start(f32[8,256]{1,0:T(8,128)} %step_in_ref.1) | copy-start | bytes 24580
  5.3 4.3 %copy-start.2 = (f32[6,6]{1,0:T(8,128)S(1)}, f32[6,6]{1,0:T(8,128)}, u32[]{:S(2)}) copy-start(f32[6,6]{1,0:T(8,128)} %jac_pitch_ref.1) | copy-start | bytes 436
  5.3 4.3 %copy-start.3 = (f32[6,6]{1,0:T(8,128)S(1)}, f32[6,6]{1,0:T(8,128)}, u32[]{:S(2)}) copy-start(f32[6,6]{1,0:T(8,128)} %jac_axial_ref.1) | copy-start | bytes 436
  5.3 7.9 %collective-permute-start.2 = (f32[6,4,8,256]{3,2,1,0:T(8,128)S(1)}, f32[6,4,8,256]{3,2,1,0:T(8,128)S(1)}, u32[]{:S(2)}, u32[]{:S(2)}) collective-permute-start(f32[6,4,8,256]{3,2,1,0:T(8,128)S(1)} %shard_map.80), channel_id=1, source_target_pairs={{0,2},{1,15},{2,0},{3,5},{4,6},{5,3},{6,4},{7,9},{8,10},{9,7},{10,... | collective-permute-start | bytes 589832 | tf_op jit(solution)/shard_map/ppermute | solution.py:469
  6.5 4.8 %collective-permute-start.5 = (f32[16,128]{1,0:T(8,128)S(1)}, f32[16,128]{1,0:T(8,128)S(1)}, u32[]{:S(2)}, u32[]{:S(2)}) collective-permute-start(f32[16,128]{1,0:T(8,128)S(1)} %pad_maximum_fusion.1), channel_id=1, source_target_pairs={{0,8},{1,9},{2,10},{3,11},{4,12},{5,13},{6,14},{7,15},{8,0},{9,1},... | collective-permute-start | bytes 24584 | tf_op jit(solution)/shard_map/ppermute | solution.py:454
  11.4 3.7 %collective-permute-start.6 = (f32[32,128]{1,0:T(8,128)S(1)}, f32[32,128]{1,0:T(8,128)S(1)}, u32[]{:S(2)}, u32[]{:S(2)}) collective-permute-start(f32[32,128]{1,0:T(8,128)S(1)} %pad_maximum_fusion.refs_7_), channel_id=1, source_target_pairs={{0,4},{1,5},{2,6},{3,7},{4,0},{5,1},{6,2},{7,3},{8,12},{9,13},{10,... | collective-permute-start | bytes 49160 | tf_op jit(solution)/shard_map/ppermute | solution.py:454
  13.3 1.9 %collective-permute-start.3 = (f32[3,4,8,256]{3,2,1,0:T(8,128)S(1)}, f32[3,4,8,256]{3,2,1,0:T(8,128)S(1)}, u32[]{:S(2)}, u32[]{:S(2)}) collective-permute-start(f32[3,4,8,256]{3,2,1,0:T(8,128)S(1)} %get-tuple-element.21), channel_id=1, source_target_pairs={{0,1},{1,0},{2,3},{3,2},{4,5},{5,4},{6,7},{7,6},{8,9},{9,8},{10,11... | collective-permute-start | bytes 294920 | tf_op jit(solution)/shard_map/ppermute | solution.py:472
  13.4 1.8 %collective-permute-start.4 = (f32[3,4,8,256]{3,2,1,0:T(8,128)S(1)}, f32[3,4,8,256]{3,2,1,0:T(8,128)S(1)}, u32[]{:S(2)}, u32[]{:S(2)}) collective-permute-start(f32[3,4,8,256]{3,2,1,0:T(8,128)S(1)} %get-tuple-element.20), channel_id=1, source_target_pairs={{0,1},{1,0},{2,3},{3,2},{4,5},{5,4},{6,7},{7,6},{8,9},{9,8},{10,11... | collective-permute-start | bytes 294920 | tf_op jit(solution)/shard_map/ppermute | solution.py:472

commit v8 on v7

--- a/solution.py
+++ b/solution.py
@@ -467,10 +467,7 @@
         odd = (i + 1) % spaces if i % 2 else (i - 1) % spaces
         pairs += [(2 * i, 2 * (i ^ 1)), (2 * i + 1, 2 * odd + 1)]
     near = lax.ppermute(edge, both, pairs)
-    cut = nvar // 2
-    far = [
-        here(lax.ppermute(near[v : v + cut], "inst", cores)) for v in range(0, nvar, cut)
-    ]
+    far = [here(lax.ppermute(near, "inst", cores))]
 
     step, local, jac, pick, mix = pl.pallas_call(
         functools.partial(prepare_kernel, planes, spaces),

time: 16.9 us -> 16.9 us (level)
  waiting for transfers between devices: 1.68 us -> 2.25 us
  starting transfers between devices: 8.97 us -> 8.41 us
    ppermute x3, waiting for transfers between devices: 1.51 us -> 2.09 us  [shards(): got.append(lax.ppermute(lines, both, swaps))]
    ppermute x2 -> x1, starting transfers between devices: 0.57 us -> 0.01 us  [shards(): far = [here(lax.ppermute(near, 'inst', cores))]]
  transfers between devices with their start and end apart: 7 -> 6, of which waited for: 3 -> 4; matrix products, arithmetic and copies ran while one was open for 0% -> 0% of each run, Pallas kernels for 15% -> 16%
where the time goes in v8:
time: 16.9 us; the launch traced here: 16.7 us
  starting transfers between devices  8.41 us (50%)
  Pallas kernels  4.39 us (26%)
  waiting for transfers between devices  2.25 us (13%)
  local copies, waits for them, and re-layouts  0.95 us (6%)
  between operations  0.7 us (4%)
    ppermute x3, starting transfers between devices, shards(): got.append(lax.ppermute(lines, both, swaps))  7.53 us
    ppermute x3, waiting for transfers between devices, shards(): got.append(lax.ppermute(lines, both, swaps))  2.09 us
    pallas_call x1, Pallas kernels, shards(): pl.pallas_call(functools.partial(step_kernel, planes, len(far)), out_shap...  1.6 us
    pallas_call x1, Pallas kernels, shards(): pl.pallas_call(functools.partial(near_kernel, planes), out_shape=pltpu.VM...  1.25 us
    pallas_call x1, Pallas kernels, shards(): pl.pallas_call(functools.partial(prepare_kernel, planes, spaces), out_sha...  1.1 us
    unnamed x12, local copies, waits for them, and re-layouts  0.95 us
    ppermute x1, starting transfers between devices, shards(): other = here(lax.ppermute(flow_state, 'inst', cores))  0.52 us
    ppermute x1, starting transfers between devices, shards(): near = lax.ppermute(edge, both, pairs)  0.36 us
  transfers between devices with their start and end apart: 6, of which 4 were waited for; matrix products, arithmetic and copies ran while one was open for 0% of the time, Pallas kernels for 16%

profile of v8, /device:TPU:0, one launch (start us, length us, event | category | flops | bytes accessed | tf_op | source)
XLA Modules:
  0.0 16.7 jit_solution(8361836394009466683)
XLA Ops:
  0.6 0.5 %collective-permute-start = (f32[6,4,8,256]{3,2,1,0:T(8,128)}, f32[6,4,8,256]{3,2,1,0:T(8,128)S(1)}, u32[]{:S(2)}, u32[]{:S(2)}) collective-permute-start(f32[6,4,8,256]{3,2,1,0:T(8,128)} %flow_ref.1), channel_id=1, source_target_pairs={{0,1},{1,0},{2,3},{3,2},{4,5},{5,4},{6,7},{7,6},{8,9},{9,8},{10,11... | collective-permute-start | bytes 589832 | tf_op jit(solution)/shard_map/ppermute | solution.py:426
  1.1 0.0 copy-start
  1.1 0.9 %copy-done = f32[6,4,8,256]{3,2,1,0:T(8,128)S(1)} copy-done((f32[6,4,8,256]{3,2,1,0:T(8,128)S(1)}, f32[6,4,8,256]{3,2,1,0:T(8,128)}, u32[]{:S(2)}) %copy-start) | copy-done | bytes 196632
  2.1 0.2 %shard_map.77 = (f32[6,4,8,256]{3,2,1,0:T(8,128)S(1)}, f32[8,128]{1,0:T(8,128)S(1)}, bf16[512,256]{1,0:T(8,128)(2,1)S(1)}, bf16[768,256]{1,0:T(8,128)(2,1)S(1)}) custom-call(f32[6,4,8,256]{3,2,1,0:T(8,128)S(1)} %copy-done), custom_call_target="tpu_custom_call" | custom-call | tf_op jit(solution)/shard_map/pallas_call | solution.py:427
  2.3 0.2 collective-permute-done.oth_ref
  2.4 0.2 %shard_map.78.after_ref = f32[8,128]{1,0:T(8,128)S(1)} custom-call(f32[8,128]{1,0:T(8,128)S(1)} %get-tuple-element.12.half_ref, f32[6,4,8,256]{3,2,1,0:T(8,128)S(1)} %collective-permute-done.oth_ref), custom_call_target="tpu_custom_call" | custom-call | tf_op jit(solution)/shard_map/pallas_call | solution.py:440
  2.6 2.6 %collective-permute-start.1 = (f32[8,128]{1,0:T(8,128)S(1)}, f32[8,128]{1,0:T(8,128)S(1)}, u32[]{:S(2)}, u32[]{:S(2)}) collective-permute-start(f32[8,128]{1,0:T(8,128)S(1)} %shard_map.78.after_ref), channel_id=1, source_target_pairs={{0,3},{1,2},{2,1},{3,0},{4,7},{5,6},{6,5},{7,4},{8,11},{9,10},{10,... | collective-permute-start | bytes 12296 | tf_op jit(solution)/shard_map/ppermute | solution.py:454
  5.2 0.0 copy-start.4
  5.2 0.0 copy-start.5
  5.2 0.1 shard_map.80
  5.3 0.0 copy-start.1
  5.3 0.0 copy-start.2
  5.3 0.0 copy-start.3
  5.3 0.4 %collective-permute-start.2 = (f32[6,4,8,256]{3,2,1,0:T(8,128)S(1)}, f32[6,4,8,256]{3,2,1,0:T(8,128)S(1)}, u32[]{:S(2)}, u32[]{:S(2)}) collective-permute-start(f32[6,4,8,256]{3,2,1,0:T(8,128)S(1)} %shard_map.80), channel_id=1, source_target_pairs={{0,2},{1,15},{2,0},{3,5},{4,6},{5,3},{6,4},{7,9},{8,10},{9,7},{10,... | collective-permute-start | bytes 589832 | tf_op jit(solution)/shard_map/ppermute | solution.py:469
  5.7 0.9 %collective-permute-done.1.after_ref = f32[8,128]{1,0:T(8,128)S(1)} collective-permute-done((f32[8,128]{1,0:T(8,128)S(1)}, f32[8,128]{1,0:T(8,128)S(1)}, u32[]{:S(2)}, u32[]{:S(2)}) %collective-permute-start.1) | collective-permute-done | bytes 4128 | tf_op jit(solution)/shard_map/ppermute | solution.py:454
  6.5 3.1 %collective-permute-start.4 = (f32[16,128]{1,0:T(8,128)S(1)}, f32[16,128]{1,0:T(8,128)S(1)}, u32[]{:S(2)}, u32[]{:S(2)}) collective-permute-start(f32[16,128]{1,0:T(8,128)S(1)} %pad_maximum_fusion.1), channel_id=1, source_target_pairs={{0,8},{1,9},{2,10},{3,11},{4,12},{5,13},{6,14},{7,15},{8,0},{9,1},... | collective-permute-start | bytes 24584 | tf_op jit(solution)/shard_map/ppermute | solution.py:454
  9.6 0.0 copy-done.4
  9.6 0.0 copy-done.5
  9.6 0.0 copy-done.1
  9.6 0.0 copy-done.2
  9.6 0.0 copy-done.3
  9.6 1.1 %shard_map.79 = (f32[8,256]{1,0:T(8,128)S(1)}, f32[6,4,8,256]{3,2,1,0:T(8,128)S(1)}, f32[72,256]{1,0:T(8,128)S(1)}, f32[32,64]{1,0:T(8,128)S(1)}, f32[2,128,256]{2,1,0:T(8,128)S(1)}) custom-call(f32[6,6]{1,0:T(8,128)S(1)} %copy-done.2, f32[6,6]{1,0:T(8,128)S(1)} %copy-done.3, s32[2,8]{1,0:T(2,128)S(1)} %copy-done.4, s32[2,8]{1,0:T(2,128)S(1)} %copy-done.5, ...), custom_call_target="tpu_custom_call" | custom-call | tf_op jit(solution)/shard_map/pallas_call | solution.py:472
  10.7 0.6 %collective-permute-done.4 = f32[16,128]{1,0:T(8,128)S(1)} collective-permute-done((f32[16,128]{1,0:T(8,128)S(1)}, f32[16,128]{1,0:T(8,128)S(1)}, u32[]{:S(2)}, u32[]{:S(2)}) %collective-permute-start.4) | collective-permute-done | bytes 8224 | tf_op jit(solution)/shard_map/ppermute | solution.py:454
  11.4 1.9 %collective-permute-start.5 = (f32[32,128]{1,0:T(8,128)S(1)}, f32[32,128]{1,0:T(8,128)S(1)}, u32[]{:S(2)}, u32[]{:S(2)}) collective-permute-start(f32[32,128]{1,0:T(8,128)S(1)} %pad_maximum_fusion.refs_6_), channel_id=1, source_target_pairs={{0,4},{1,5},{2,6},{3,7},{4,0},{5,1},{6,2},{7,3},{8,12},{9,13},{10,... | collective-permute-start | bytes 49160 | tf_op jit(solution)/shard_map/ppermute | solution.py:454
  13.3 0.0 collective-permute-done.2.refs_1_
  13.3 0.0 collective-permute-start.3
  13.3 1.3 %shard_map.81.refs_1_ = f32[192,256]{1,0:T(8,128)S(1)} custom-call(f32[6,4,8,256]{3,2,1,0:T(8,128)S(1)} %get-tuple-element.11.own_ref.refs_0_, f32[6,4,8,256]{3,2,1,0:T(8,128)S(1)} %collective-permute-done.2.refs_1_, f32[6,4,8,256]{3,2,1,0:T(8,128)S(1)} %get-tuple-element.14.refs_2_, f32[72,256]{1,0:T(8,128)S(1)} %get-tuple-element.15.refs_3_, ...), custom_call_target="tpu_custom_call" | custom-call | tf_op jit(solution)/shard_map/pallas_call | solution.py:487
  14.6 0.6 %collective-permute-done.5.refs_7_ = f32[32,128]{1,0:T(8,128)S(1)} collective-permute-done((f32[32,128]{1,0:T(8,128)S(1)}, f32[32,128]{1,0:T(8,128)S(1)}, u32[]{:S(2)}, u32[]{:S(2)}) %collective-permute-start.5) | collective-permute-done | bytes 16416 | tf_op jit(solution)/shard_map/ppermute | solution.py:454
  15.1 0.0 collective-permute-done.3.refs_2_
  15.1 1.6 %shard_map.82 = (f32[6,4,8,256]{3,2,1,0:T(8,128)}, f32[6,4,8,256]{3,2,1,0:T(8,128)}) custom-call(f32[192,256]{1,0:T(8,128)S(1)} %bitcast.3, f32[192,256]{1,0:T(8,128)S(1)} %shard_map.81.refs_1_, f32[6,4,8,256]{3,2,1,0:T(8,128)S(1)} %collective-permute-done.3.refs_2_, f32[72,256]{1,0:T(8,128)S(1)} %get-tuple-element.15.refs_3_, ...), custom_call_target="tpu_custom_call" | custom-call | tf_op jit(solution)/shard_map/pallas_call | solution.py:504
  (3 shorter events, 0.0 us)
Async XLA Ops:
  0.6 1.8 %collective-permute-start = (f32[6,4,8,256]{3,2,1,0:T(8,128)}, f32[6,4,8,256]{3,2,1,0:T(8,128)S(1)}, u32[]{:S(2)}, u32[]{:S(2)}) collective-permute-start(f32[6,4,8,256]{3,2,1,0:T(8,128)} %flow_ref.1), channel_id=1, source_target_pairs={{0,1},{1,0},{2,3},{3,2},{4,5},{5,4},{6,7},{7,6},{8,9},{9,8},{10,11... | collective-permute-start | bytes 589832 | tf_op jit(solution)/shard_map/ppermute | solution.py:426
  1.1 0.9 %copy-start = (f32[6,4,8,256]{3,2,1,0:T(8,128)S(1)}, f32[6,4,8,256]{3,2,1,0:T(8,128)}, u32[]{:S(2)}) copy-start(f32[6,4,8,256]{3,2,1,0:T(8,128)} %flow_ref.1) | copy-start | bytes 589828
  2.6 3.9 %collective-permute-start.1 = (f32[8,128]{1,0:T(8,128)S(1)}, f32[8,128]{1,0:T(8,128)S(1)}, u32[]{:S(2)}, u32[]{:S(2)}) collective-permute-start(f32[8,128]{1,0:T(8,128)S(1)} %shard_map.78.after_ref), channel_id=1, source_target_pairs={{0,3},{1,2},{2,1},{3,0},{4,7},{5,6},{6,5},{7,4},{8,11},{9,10},{10,... | collective-permute-start | bytes 12296 | tf_op jit(solution)/shard_map/ppermute | solution.py:454
  5.2 4.4 %copy-start.4 = (s32[2,8]{1,0:T(2,128)S(1)}, s32[2,8]{1,0:T(2,128)}, u32[]{:S(2)}) copy-start(s32[2,8]{1,0:T(2,128)} %partner_ref.1) | copy-start | bytes 196
  5.2 4.4 %copy-start.5 = (s32[2,8]{1,0:T(2,128)S(1)}, s32[2,8]{1,0:T(2,128)}, u32[]{:S(2)}) copy-start(s32[2,8]{1,0:T(2,128)} %index_ref.1) | copy-start | bytes 196
  5.3 4.3 %copy-start.1 = (f32[8,256]{1,0:T(8,128)S(1)}, f32[8,256]{1,0:T(8,128)}, u32[]{:S(2)}) copy-start(f32[8,256]{1,0:T(8,128)} %step_in_ref.1) | copy-start | bytes 24580
  5.3 4.3 %copy-start.2 = (f32[6,6]{1,0:T(8,128)S(1)}, f32[6,6]{1,0:T(8,128)}, u32[]{:S(2)}) copy-start(f32[6,6]{1,0:T(8,128)} %jac_pitch_ref.1) | copy-start | bytes 436
  5.3 4.3 %copy-start.3 = (f32[6,6]{1,0:T(8,128)S(1)}, f32[6,6]{1,0:T(8,128)}, u32[]{:S(2)}) copy-start(f32[6,6]{1,0:T(8,128)} %jac_axial_ref.1) | copy-start | bytes 436
  5.3 7.9 %collective-permute-start.2 = (f32[6,4,8,256]{3,2,1,0:T(8,128)S(1)}, f32[6,4,8,256]{3,2,1,0:T(8,128)S(1)}, u32[]{:S(2)}, u32[]{:S(2)}) collective-permute-start(f32[6,4,8,256]{3,2,1,0:T(8,128)S(1)} %shard_map.80), channel_id=1, source_target_pairs={{0,2},{1,15},{2,0},{3,5},{4,6},{5,3},{6,4},{7,9},{8,10},{9,7},{10,... | collective-permute-start | bytes 589832 | tf_op jit(solution)/shard_map/ppermute | solution.py:469
  6.5 4.8 %collective-permute-start.4 = (f32[16,128]{1,0:T(8,128)S(1)}, f32[16,128]{1,0:T(8,128)S(1)}, u32[]{:S(2)}, u32[]{:S(2)}) collective-permute-start(f32[16,128]{1,0:T(8,128)S(1)} %pad_maximum_fusion.1), channel_id=1, source_target_pairs={{0,8},{1,9},{2,10},{3,11},{4,12},{5,13},{6,14},{7,15},{8,0},{9,1},... | collective-permute-start | bytes 24584 | tf_op jit(solution)/shard_map/ppermute | solution.py:454
  11.4 3.7 %collective-permute-start.5 = (f32[32,128]{1,0:T(8,128)S(1)}, f32[32,128]{1,0:T(8,128)S(1)}, u32[]{:S(2)}, u32[]{:S(2)}) collective-permute-start(f32[32,128]{1,0:T(8,128)S(1)} %pad_maximum_fusion.refs_6_), channel_id=1, source_target_pairs={{0,4},{1,5},{2,6},{3,7},{4,0},{5,1},{6,2},{7,3},{8,12},{9,13},{10,... | collective-permute-start | bytes 49160 | tf_op jit(solution)/shard_map/ppermute | solution.py:454
  13.3 1.9 %collective-permute-start.3 = (f32[6,4,8,256]{3,2,1,0:T(8,128)S(1)}, f32[6,4,8,256]{3,2,1,0:T(8,128)S(1)}, u32[]{:S(2)}, u32[]{:S(2)}) collective-permute-start(f32[6,4,8,256]{3,2,1,0:T(8,128)S(1)} %collective-permute-done.2.refs_1_), channel_id=1, source_target_pairs={{0,1},{1,0},{2,3},{3,2},{4,5},{5,4},{6,7},{7,6},{8,9},{9,8},{10,11... | collective-permute-start | bytes 589832 | tf_op jit(solution)/shard_map/ppermute | solution.py:470

commit v9 on v8

--- a/solution.py
+++ b/solution.py
@@ -447,7 +447,7 @@
 
     lines, got = line, []
     for turn, bit in enumerate(round_bits(spaces)):
-        cross = 1 if turn == 0 else 0
+        cross = 1 if turn != 1 else 0
         swaps = [
             (2 * i + c, 2 * (i ^ (1 << bit)) + (c ^ cross)) for i in range(spaces) for c in (0, 1)
         ]

time: 16.9 us -> 17 us (level)
  the two profiles are of different devices: /device:TPU:0 before, /device:TPU:1 now
where the time goes in v9:
time: 17 us; the launch traced here: 16.9 us
  starting transfers between devices  7.32 us (43%)
  Pallas kernels  4.39 us (26%)
  waiting for transfers between devices  3.51 us (21%)
  local copies, waits for them, and re-layouts  0.95 us (6%)
  between operations  0.7 us (4%)
    ppermute x3, starting transfers between devices, shards(): got.append(lax.ppermute(lines, both, swaps))  3.8 us
    ppermute x1, starting transfers between devices, shards(): near = lax.ppermute(edge, both, pairs)  3.36 us
    ppermute x3, waiting for transfers between devices, shards(): got.append(lax.ppermute(lines, both, swaps))  3.03 us
    pallas_call x1, Pallas kernels, shards(): pl.pallas_call(functools.partial(step_kernel, planes, len(far)), out_shap...  1.6 us
    pallas_call x1, Pallas kernels, shards(): pl.pallas_call(functools.partial(near_kernel, planes), out_shape=pltpu.VM...  1.25 us
    pallas_call x1, Pallas kernels, shards(): pl.pallas_call(functools.partial(prepare_kernel, planes, spaces), out_sha...  1.1 us
    unnamed x12, local copies, waits for them, and re-layouts  0.95 us
    ppermute x1, waiting for transfers between devices, shards(): other = here(lax.ppermute(flow_state, 'inst', cores))  0.47 us
  transfers between devices with their start and end apart: 6, of which 3 were waited for; matrix products, arithmetic and copies ran while one was open for 0% of the time, Pallas kernels for 15%

profile of v9, /device:TPU:1, one launch (start us, length us, event | category | flops | bytes accessed | tf_op | source)
XLA Modules:
  0.0 16.9 jit_solution(11142275516081328673)
XLA Ops:
  0.6 0.1 collective-permute-start
  0.8 0.0 copy-start
  0.8 0.9 %copy-done = f32[6,4,8,256]{3,2,1,0:T(8,128)S(1)} copy-done((f32[6,4,8,256]{3,2,1,0:T(8,128)S(1)}, f32[6,4,8,256]{3,2,1,0:T(8,128)}, u32[]{:S(2)}) %copy-start) | copy-done | bytes 196632
  1.7 0.2 %shard_map.77 = (f32[6,4,8,256]{3,2,1,0:T(8,128)S(1)}, f32[8,128]{1,0:T(8,128)S(1)}, bf16[512,256]{1,0:T(8,128)(2,1)S(1)}, bf16[768,256]{1,0:T(8,128)(2,1)S(1)}) custom-call(f32[6,4,8,256]{3,2,1,0:T(8,128)S(1)} %copy-done), custom_call_target="tpu_custom_call" | custom-call | tf_op jit(solution)/shard_map/pallas_call | solution.py:427
  1.9 0.5 %collective-permute-done.oth_ref = f32[6,4,8,256]{3,2,1,0:T(8,128)S(1)} collective-permute-done((f32[6,4,8,256]{3,2,1,0:T(8,128)}, f32[6,4,8,256]{3,2,1,0:T(8,128)S(1)}, u32[]{:S(2)}, u32[]{:S(2)}) %collective-permute-start) | collective-permute-done | bytes 196640 | tf_op jit(solution)/shard_map/ppermute | solution.py:426
  2.3 0.2 %shard_map.78.after_ref = f32[8,128]{1,0:T(8,128)S(1)} custom-call(f32[8,128]{1,0:T(8,128)S(1)} %get-tuple-element.12.half_ref, f32[6,4,8,256]{3,2,1,0:T(8,128)S(1)} %collective-permute-done.oth_ref), custom_call_target="tpu_custom_call" | custom-call | tf_op jit(solution)/shard_map/pallas_call | solution.py:440
  2.5 2.6 %collective-permute-start.1 = (f32[8,128]{1,0:T(8,128)S(1)}, f32[8,128]{1,0:T(8,128)S(1)}, u32[]{:S(2)}, u32[]{:S(2)}) collective-permute-start(f32[8,128]{1,0:T(8,128)S(1)} %shard_map.78.after_ref), channel_id=1, source_target_pairs={{0,3},{1,2},{2,1},{3,0},{4,7},{5,6},{6,5},{7,4},{8,11},{9,10},{10,... | collective-permute-start | bytes 12296 | tf_op jit(solution)/shard_map/ppermute | solution.py:454
  5.1 0.0 copy-start.4
  5.1 0.0 copy-start.5
  5.1 0.1 shard_map.80
  5.2 0.0 copy-start.1
  5.2 0.0 copy-start.2
  5.2 0.0 copy-start.3
  5.2 3.4 %collective-permute-start.2 = (f32[6,4,8,256]{3,2,1,0:T(8,128)S(1)}, f32[6,4,8,256]{3,2,1,0:T(8,128)S(1)}, u32[]{:S(2)}, u32[]{:S(2)}) collective-permute-start(f32[6,4,8,256]{3,2,1,0:T(8,128)S(1)} %shard_map.80), channel_id=1, source_target_pairs={{0,2},{1,15},{2,0},{3,5},{4,6},{5,3},{6,4},{7,9},{8,10},{9,7},{10,... | collective-permute-start | bytes 589832 | tf_op jit(solution)/shard_map/ppermute | solution.py:469
  8.6 0.0 collective-permute-done.1.after_ref
  8.6 0.4 %collective-permute-start.4 = (f32[16,128]{1,0:T(8,128)S(1)}, f32[16,128]{1,0:T(8,128)S(1)}, u32[]{:S(2)}, u32[]{:S(2)}) collective-permute-start(f32[16,128]{1,0:T(8,128)S(1)} %pad_maximum_fusion.1), channel_id=1, source_target_pairs={{0,8},{1,9},{2,10},{3,11},{4,12},{5,13},{6,14},{7,15},{8,0},{9,1},... | collective-permute-start | bytes 24584 | tf_op jit(solution)/shard_map/ppermute | solution.py:454
  9.0 0.0 copy-done.4
  9.0 0.0 copy-done.5
  9.0 0.0 copy-done.1
  9.0 0.0 copy-done.2
  9.0 0.0 copy-done.3
  9.0 1.1 %shard_map.79 = (f32[8,256]{1,0:T(8,128)S(1)}, f32[6,4,8,256]{3,2,1,0:T(8,128)S(1)}, f32[72,256]{1,0:T(8,128)S(1)}, f32[32,64]{1,0:T(8,128)S(1)}, f32[2,128,256]{2,1,0:T(8,128)S(1)}) custom-call(f32[6,6]{1,0:T(8,128)S(1)} %copy-done.2, f32[6,6]{1,0:T(8,128)S(1)} %copy-done.3, s32[2,8]{1,0:T(2,128)S(1)} %copy-done.4, s32[2,8]{1,0:T(2,128)S(1)} %copy-done.5, ...), custom_call_target="tpu_custom_call" | custom-call | tf_op jit(solution)/shard_map/pallas_call | solution.py:472
  10.1 2.0 %collective-permute-done.4 = f32[16,128]{1,0:T(8,128)S(1)} collective-permute-done((f32[16,128]{1,0:T(8,128)S(1)}, f32[16,128]{1,0:T(8,128)S(1)}, u32[]{:S(2)}, u32[]{:S(2)}) %collective-permute-start.4) | collective-permute-done | bytes 8224 | tf_op jit(solution)/shard_map/ppermute | solution.py:454
  12.1 0.8 %collective-permute-start.5 = (f32[32,128]{1,0:T(8,128)S(1)}, f32[32,128]{1,0:T(8,128)S(1)}, u32[]{:S(2)}, u32[]{:S(2)}) collective-permute-start(f32[32,128]{1,0:T(8,128)S(1)} %pad_maximum_fusion.refs_6_), channel_id=1, source_target_pairs={{0,5},{1,4},{2,7},{3,6},{4,1},{5,0},{6,3},{7,2},{8,13},{9,12},{10,... | collective-permute-start | bytes 49160 | tf_op jit(solution)/shard_map/ppermute | solution.py:454
  12.9 0.0 collective-permute-done.2.refs_1_
  12.9 0.0 collective-permute-start.3
  13.0 1.3 %shard_map.81.refs_1_ = f32[192,256]{1,0:T(8,128)S(1)} custom-call(f32[6,4,8,256]{3,2,1,0:T(8,128)S(1)} %get-tuple-element.11.own_ref.refs_0_, f32[6,4,8,256]{3,2,1,0:T(8,128)S(1)} %collective-permute-done.2.refs_1_, f32[6,4,8,256]{3,2,1,0:T(8,128)S(1)} %get-tuple-element.14.refs_2_, f32[72,256]{1,0:T(8,128)S(1)} %get-tuple-element.15.refs_3_, ...), custom_call_target="tpu_custom_call" | custom-call | tf_op jit(solution)/shard_map/pallas_call | solution.py:487
  14.2 1.0 %collective-permute-done.5.refs_7_ = f32[32,128]{1,0:T(8,128)S(1)} collective-permute-done((f32[32,128]{1,0:T(8,128)S(1)}, f32[32,128]{1,0:T(8,128)S(1)}, u32[]{:S(2)}, u32[]{:S(2)}) %collective-permute-start.5) | collective-permute-done | bytes 16416 | tf_op jit(solution)/shard_map/ppermute | solution.py:454
  15.3 0.0 collective-permute-done.3.refs_2_
  15.3 1.6 %shard_map.82 = (f32[6,4,8,256]{3,2,1,0:T(8,128)}, f32[6,4,8,256]{3,2,1,0:T(8,128)}) custom-call(f32[192,256]{1,0:T(8,128)S(1)} %bitcast.3, f32[192,256]{1,0:T(8,128)S(1)} %shard_map.81.refs_1_, f32[6,4,8,256]{3,2,1,0:T(8,128)S(1)} %collective-permute-done.3.refs_2_, f32[72,256]{1,0:T(8,128)S(1)} %get-tuple-element.15.refs_3_, ...), custom_call_target="tpu_custom_call" | custom-call | tf_op jit(solution)/shard_map/pallas_call | solution.py:504
  (3 shorter events, 0.0 us)
Async XLA Ops:
  0.6 1.7 %collective-permute-start = (f32[6,4,8,256]{3,2,1,0:T(8,128)}, f32[6,4,8,256]{3,2,1,0:T(8,128)S(1)}, u32[]{:S(2)}, u32[]{:S(2)}) collective-permute-start(f32[6,4,8,256]{3,2,1,0:T(8,128)} %flow_ref.1), channel_id=1, source_target_pairs={{0,1},{1,0},{2,3},{3,2},{4,5},{5,4},{6,7},{7,6},{8,9},{9,8},{10,11... | collective-permute-start | bytes 589832 | tf_op jit(solution)/shard_map/ppermute | solution.py:426
  0.8 0.9 %copy-start = (f32[6,4,8,256]{3,2,1,0:T(8,128)S(1)}, f32[6,4,8,256]{3,2,1,0:T(8,128)}, u32[]{:S(2)}) copy-start(f32[6,4,8,256]{3,2,1,0:T(8,128)} %flow_ref.1) | copy-start | bytes 589828
  2.5 6.1 %collective-permute-start.1 = (f32[8,128]{1,0:T(8,128)S(1)}, f32[8,128]{1,0:T(8,128)S(1)}, u32[]{:S(2)}, u32[]{:S(2)}) collective-permute-start(f32[8,128]{1,0:T(8,128)S(1)} %shard_map.78.after_ref), channel_id=1, source_target_pairs={{0,3},{1,2},{2,1},{3,0},{4,7},{5,6},{6,5},{7,4},{8,11},{9,10},{10,... | collective-permute-start | bytes 12296 | tf_op jit(solution)/shard_map/ppermute | solution.py:454
  5.1 3.9 %copy-start.4 = (s32[2,8]{1,0:T(2,128)S(1)}, s32[2,8]{1,0:T(2,128)}, u32[]{:S(2)}) copy-start(s32[2,8]{1,0:T(2,128)} %partner_ref.1) | copy-start | bytes 196
  5.1 3.9 %copy-start.5 = (s32[2,8]{1,0:T(2,128)S(1)}, s32[2,8]{1,0:T(2,128)}, u32[]{:S(2)}) copy-start(s32[2,8]{1,0:T(2,128)} %index_ref.1) | copy-start | bytes 196
  5.2 3.8 %copy-start.1 = (f32[8,256]{1,0:T(8,128)S(1)}, f32[8,256]{1,0:T(8,128)}, u32[]{:S(2)}) copy-start(f32[8,256]{1,0:T(8,128)} %step_in_ref.1) | copy-start | bytes 24580
  5.2 3.8 %copy-start.2 = (f32[6,6]{1,0:T(8,128)S(1)}, f32[6,6]{1,0:T(8,128)}, u32[]{:S(2)}) copy-start(f32[6,6]{1,0:T(8,128)} %jac_pitch_ref.1) | copy-start | bytes 436
  5.2 3.8 %copy-start.3 = (f32[6,6]{1,0:T(8,128)S(1)}, f32[6,6]{1,0:T(8,128)}, u32[]{:S(2)}) copy-start(f32[6,6]{1,0:T(8,128)} %jac_axial_ref.1) | copy-start | bytes 436
  5.2 7.7 %collective-permute-start.2 = (f32[6,4,8,256]{3,2,1,0:T(8,128)S(1)}, f32[6,4,8,256]{3,2,1,0:T(8,128)S(1)}, u32[]{:S(2)}, u32[]{:S(2)}) collective-permute-start(f32[6,4,8,256]{3,2,1,0:T(8,128)S(1)} %shard_map.80), channel_id=1, source_target_pairs={{0,2},{1,15},{2,0},{3,5},{4,6},{5,3},{6,4},{7,9},{8,10},{9,7},{10,... | collective-permute-start | bytes 589832 | tf_op jit(solution)/shard_map/ppermute | solution.py:469
  8.6 3.5 %collective-permute-start.4 = (f32[16,128]{1,0:T(8,128)S(1)}, f32[16,128]{1,0:T(8,128)S(1)}, u32[]{:S(2)}, u32[]{:S(2)}) collective-permute-start(f32[16,128]{1,0:T(8,128)S(1)} %pad_maximum_fusion.1), channel_id=1, source_target_pairs={{0,8},{1,9},{2,10},{3,11},{4,12},{5,13},{6,14},{7,15},{8,0},{9,1},... | collective-permute-start | bytes 24584 | tf_op jit(solution)/shard_map/ppermute | solution.py:454
  12.1 3.2 %collective-permute-start.5 = (f32[32,128]{1,0:T(8,128)S(1)}, f32[32,128]{1,0:T(8,128)S(1)}, u32[]{:S(2)}, u32[]{:S(2)}) collective-permute-start(f32[32,128]{1,0:T(8,128)S(1)} %pad_maximum_fusion.refs_6_), channel_id=1, source_target_pairs={{0,5},{1,4},{2,7},{3,6},{4,1},{5,0},{6,3},{7,2},{8,13},{9,12},{10,... | collective-permute-start | bytes 49160 | tf_op jit(solution)/shard_map/ppermute | solution.py:454
  12.9 2.4 %collective-permute-start.3 = (f32[6,4,8,256]{3,2,1,0:T(8,128)S(1)}, f32[6,4,8,256]{3,2,1,0:T(8,128)S(1)}, u32[]{:S(2)}, u32[]{:S(2)}) collective-permute-start(f32[6,4,8,256]{3,2,1,0:T(8,128)S(1)} %collective-permute-done.2.refs_1_), channel_id=1, source_target_pairs={{0,1},{1,0},{2,3},{3,2},{4,5},{5,4},{6,7},{7,6},{8,9},{9,8},{10,11... | collective-permute-start | bytes 589832 | tf_op jit(solution)/shard_map/ppermute | solution.py:470

commit v10 on v8

--- a/solution.py
+++ b/solution.py
@@ -1,4 +1,5 @@
 import functools
+import itertools
 import math
 
 import jax
@@ -307,7 +308,8 @@
     before_ref, base_ref, *refs = refs
     far_refs, refs = refs[:cuts], refs[cuts:]
     jac_ref, shift_ref, sweep_ref, *lines_refs, pick_ref, mix_ref, step_ref = refs[:8]
-    new_ref, out_ref, far_own, far_oth, parts_ref, rest_ref, terms_ref = refs[8:]
+    new_hbm, out_hbm, far_own, far_oth, parts_ref, rest_ref, terms_ref, *refs = refs[8:]
+    new_ref, out_ref, sems = refs
     core = lax.axis_index("inst")
     low = low_side()
     nvar, ninst, _, axial = new_ref.shape
@@ -384,8 +386,10 @@
     step = step_ref[...]
     lane = lax.broadcasted_iota(jnp.int32, (ROWS, LANES), 1)
     reached = side >= HALO
-    for n in range(ninst):
-        for u in range(nvar):
+    copies = []
+    for start in range(0, nvar, nvar // 2):
+        part = slice(start, start + nvar // 2)
+        for u, n in itertools.product(range(part.start, part.stop), range(ninst)):
             far = rest_ref[lines_of(packs, u, n // 2), :]
             turned = pltpu.roll(far, HALO, 0)
             stays = (1 - n % 2) == jnp.where(low, 0, 1)
@@ -395,9 +399,9 @@
             for plane_no, plane in enumerate(planes):
                 tile, at = divmod(plane - SWEEPS, LANES)
                 assert at + GROUP <= LANES
-                start = group // LANES * LANES
+                begin = group // LANES * LANES
                 moved = pltpu.roll(
-                    spread[plane_no][:, start : start + LANES], (at - group) % LANES, 1
+                    spread[plane_no][:, begin : begin + LANES], (at - group) % LANES, 1
                 )
                 inside = (lane >= at) & (lane < at + GROUP)
                 tiles[tile] = tiles[tile] + jnp.where(inside, moved, 0.0)
@@ -405,6 +409,13 @@
             at = lines_of(ninst, u, n)
             out_ref[u, n] = base_ref[at, :] + more
             new_ref[u, n] = before_ref[at, :] - step * more
+        pairs = ((out_ref, out_hbm), (new_ref, new_hbm))
+        for which, (ref, hbm) in enumerate(pairs):
+            sem = sems.at[which, start // (nvar // 2)]
+            copies.append(pltpu.make_async_copy(ref.at[part], hbm.at[part], sem))
+            copies[-1].start()
+    for copy in copies:
+        copy.wait()
 
 
 def here(array):
@@ -505,13 +516,16 @@
         functools.partial(step_kernel, planes, len(far)),
         out_shape=(jax.ShapeDtypeStruct(flow_state.shape, jnp.float32),) * 2,
         in_specs=[vmem] * (10 + len(far)),
-        out_specs=(vmem, vmem),
+        out_specs=(anywhere, anywhere),
         scratch_shapes=[
             block,
             block,
             pltpu.VMEM((lined // 2, 2 * axial), jnp.float32),
             pltpu.VMEM((lined // 2, axial), jnp.float32),
             pltpu.VMEM((lined // 2, SWEEPS * axial), jnp.float32),
+            block,
+            block,
+            pltpu.SemaphoreType.DMA((2, 2)),
         ],
         compiler_params=params,
     )(here(before), here(base), *far, *[here(a) for a in (jac, shift, sweep, *parts, pick, mix, step)])

time: 16.9 us -> 16.9 us (level)
  no operation moved by 1% of the time
where the time goes in v10:
time: 16.9 us; the launch traced here: 16.7 us
  starting transfers between devices  8.41 us (50%)
  Pallas kernels  4.38 us (26%)
  waiting for transfers between devices  2.25 us (13%)
  local copies, waits for them, and re-layouts  0.95 us (6%)
  between operations  0.7 us (4%)
    ppermute x3, starting transfers between devices, shards(): got.append(lax.ppermute(lines, both, swaps))  7.53 us
    ppermute x3, waiting for transfers between devices, shards(): got.append(lax.ppermute(lines, both, swaps))  2.09 us
    pallas_call x1, Pallas kernels, shards(): pl.pallas_call(functools.partial(step_kernel, planes, len(far)), out_shap...  1.6 us
    pallas_call x1, Pallas kernels, shards(): pl.pallas_call(functools.partial(near_kernel, planes), out_shape=pltpu.VM...  1.25 us
    pallas_call x1, Pallas kernels, shards(): pl.pallas_call(functools.partial(prepare_kernel, planes, spaces), out_sha...  1.1 us
    unnamed x12, local copies, waits for them, and re-layouts  0.95 us
    ppermute x1, starting transfers between devices, shards(): other = here(lax.ppermute(flow_state, 'inst', cores))  0.52 us
    ppermute x1, starting transfers between devices, shards(): near = lax.ppermute(edge, both, pairs)  0.36 us
  transfers between devices with their start and end apart: 6, of which 4 were waited for; matrix products, arithmetic and copies ran while one was open for 0% of the time, Pallas kernels for 16%

profile of v10, /device:TPU:0, one launch (start us, length us, event | category | flops | bytes accessed | tf_op | source)
XLA Modules:
  0.0 16.7 jit_solution(9491276973146363479)
XLA Ops:
  0.6 0.5 %collective-permute-start = (f32[6,4,8,256]{3,2,1,0:T(8,128)}, f32[6,4,8,256]{3,2,1,0:T(8,128)S(1)}, u32[]{:S(2)}, u32[]{:S(2)}) collective-permute-start(f32[6,4,8,256]{3,2,1,0:T(8,128)} %flow_ref.1), channel_id=1, source_target_pairs={{0,1},{1,0},{2,3},{3,2},{4,5},{5,4},{6,7},{7,6},{8,9},{9,8},{10,11... | collective-permute-start | bytes 589832 | tf_op jit(solution)/shard_map/ppermute | solution.py:437
  1.1 0.0 copy-start
  1.1 0.9 %copy-done = f32[6,4,8,256]{3,2,1,0:T(8,128)S(1)} copy-done((f32[6,4,8,256]{3,2,1,0:T(8,128)S(1)}, f32[6,4,8,256]{3,2,1,0:T(8,128)}, u32[]{:S(2)}) %copy-start) | copy-done | bytes 196632
  2.1 0.2 %shard_map.77 = (f32[6,4,8,256]{3,2,1,0:T(8,128)S(1)}, f32[8,128]{1,0:T(8,128)S(1)}, bf16[512,256]{1,0:T(8,128)(2,1)S(1)}, bf16[768,256]{1,0:T(8,128)(2,1)S(1)}) custom-call(f32[6,4,8,256]{3,2,1,0:T(8,128)S(1)} %copy-done), custom_call_target="tpu_custom_call" | custom-call | tf_op jit(solution)/shard_map/pallas_call | solution.py:438
  2.3 0.2 collective-permute-done.oth_ref
  2.4 0.2 %shard_map.78.after_ref = f32[8,128]{1,0:T(8,128)S(1)} custom-call(f32[8,128]{1,0:T(8,128)S(1)} %get-tuple-element.12.half_ref, f32[6,4,8,256]{3,2,1,0:T(8,128)S(1)} %collective-permute-done.oth_ref), custom_call_target="tpu_custom_call" | custom-call | tf_op jit(solution)/shard_map/pallas_call | solution.py:451
  2.6 2.6 %collective-permute-start.1 = (f32[8,128]{1,0:T(8,128)S(1)}, f32[8,128]{1,0:T(8,128)S(1)}, u32[]{:S(2)}, u32[]{:S(2)}) collective-permute-start(f32[8,128]{1,0:T(8,128)S(1)} %shard_map.78.after_ref), channel_id=1, source_target_pairs={{0,3},{1,2},{2,1},{3,0},{4,7},{5,6},{6,5},{7,4},{8,11},{9,10},{10,... | collective-permute-start | bytes 12296 | tf_op jit(solution)/shard_map/ppermute | solution.py:465
  5.2 0.0 copy-start.4
  5.2 0.0 copy-start.5
  5.2 0.1 shard_map.80
  5.3 0.0 copy-start.1
  5.3 0.0 copy-start.2
  5.3 0.0 copy-start.3
  5.3 0.4 %collective-permute-start.2 = (f32[6,4,8,256]{3,2,1,0:T(8,128)S(1)}, f32[6,4,8,256]{3,2,1,0:T(8,128)S(1)}, u32[]{:S(2)}, u32[]{:S(2)}) collective-permute-start(f32[6,4,8,256]{3,2,1,0:T(8,128)S(1)} %shard_map.80), channel_id=1, source_target_pairs={{0,2},{1,15},{2,0},{3,5},{4,6},{5,3},{6,4},{7,9},{8,10},{9,7},{10,... | collective-permute-start | bytes 589832 | tf_op jit(solution)/shard_map/ppermute | solution.py:480
  5.7 0.9 %collective-permute-done.1.after_ref = f32[8,128]{1,0:T(8,128)S(1)} collective-permute-done((f32[8,128]{1,0:T(8,128)S(1)}, f32[8,128]{1,0:T(8,128)S(1)}, u32[]{:S(2)}, u32[]{:S(2)}) %collective-permute-start.1) | collective-permute-done | bytes 4128 | tf_op jit(solution)/shard_map/ppermute | solution.py:465
  6.5 3.1 %collective-permute-start.4 = (f32[16,128]{1,0:T(8,128)S(1)}, f32[16,128]{1,0:T(8,128)S(1)}, u32[]{:S(2)}, u32[]{:S(2)}) collective-permute-start(f32[16,128]{1,0:T(8,128)S(1)} %pad_maximum_fusion.1), channel_id=1, source_target_pairs={{0,8},{1,9},{2,10},{3,11},{4,12},{5,13},{6,14},{7,15},{8,0},{9,1},... | collective-permute-start | bytes 24584 | tf_op jit(solution)/shard_map/ppermute | solution.py:465
  9.6 0.0 copy-done.4
  9.6 0.0 copy-done.5
  9.6 0.0 copy-done.1
  9.6 0.0 copy-done.2
  9.6 0.0 copy-done.3
  9.6 1.1 %shard_map.79 = (f32[8,256]{1,0:T(8,128)S(1)}, f32[6,4,8,256]{3,2,1,0:T(8,128)S(1)}, f32[72,256]{1,0:T(8,128)S(1)}, f32[32,64]{1,0:T(8,128)S(1)}, f32[2,128,256]{2,1,0:T(8,128)S(1)}) custom-call(f32[6,6]{1,0:T(8,128)S(1)} %copy-done.2, f32[6,6]{1,0:T(8,128)S(1)} %copy-done.3, s32[2,8]{1,0:T(2,128)S(1)} %copy-done.4, s32[2,8]{1,0:T(2,128)S(1)} %copy-done.5, ...), custom_call_target="tpu_custom_call" | custom-call | tf_op jit(solution)/shard_map/pallas_call | solution.py:483
  10.7 0.6 %collective-permute-done.4 = f32[16,128]{1,0:T(8,128)S(1)} collective-permute-done((f32[16,128]{1,0:T(8,128)S(1)}, f32[16,128]{1,0:T(8,128)S(1)}, u32[]{:S(2)}, u32[]{:S(2)}) %collective-permute-start.4) | collective-permute-done | bytes 8224 | tf_op jit(solution)/shard_map/ppermute | solution.py:465
  11.4 1.9 %collective-permute-start.5 = (f32[32,128]{1,0:T(8,128)S(1)}, f32[32,128]{1,0:T(8,128)S(1)}, u32[]{:S(2)}, u32[]{:S(2)}) collective-permute-start(f32[32,128]{1,0:T(8,128)S(1)} %pad_maximum_fusion.refs_6_), channel_id=1, source_target_pairs={{0,4},{1,5},{2,6},{3,7},{4,0},{5,1},{6,2},{7,3},{8,12},{9,13},{10,... | collective-permute-start | bytes 49160 | tf_op jit(solution)/shard_map/ppermute | solution.py:465
  13.3 0.0 collective-permute-done.2.refs_1_
  13.3 0.0 collective-permute-start.3
  13.3 1.3 %shard_map.81.refs_1_ = f32[192,256]{1,0:T(8,128)S(1)} custom-call(f32[6,4,8,256]{3,2,1,0:T(8,128)S(1)} %get-tuple-element.11.own_ref.refs_0_, f32[6,4,8,256]{3,2,1,0:T(8,128)S(1)} %collective-permute-done.2.refs_1_, f32[6,4,8,256]{3,2,1,0:T(8,128)S(1)} %get-tuple-element.14.refs_2_, f32[72,256]{1,0:T(8,128)S(1)} %get-tuple-element.15.refs_3_, ...), custom_call_target="tpu_custom_call" | custom-call | tf_op jit(solution)/shard_map/pallas_call | solution.py:498
  14.6 0.6 %collective-permute-done.5.refs_7_ = f32[32,128]{1,0:T(8,128)S(1)} collective-permute-done((f32[32,128]{1,0:T(8,128)S(1)}, f32[32,128]{1,0:T(8,128)S(1)}, u32[]{:S(2)}, u32[]{:S(2)}) %collective-permute-start.5) | collective-permute-done | bytes 16416 | tf_op jit(solution)/shard_map/ppermute | solution.py:465
  15.1 0.0 collective-permute-done.3.refs_2_
  15.1 1.6 %shard_map.82 = (f32[6,4,8,256]{3,2,1,0:T(8,128)}, f32[6,4,8,256]{3,2,1,0:T(8,128)}) custom-call(f32[192,256]{1,0:T(8,128)S(1)} %bitcast.3, f32[192,256]{1,0:T(8,128)S(1)} %shard_map.81.refs_1_, f32[6,4,8,256]{3,2,1,0:T(8,128)S(1)} %collective-permute-done.3.refs_2_, f32[72,256]{1,0:T(8,128)S(1)} %get-tuple-element.15.refs_3_, ...), custom_call_target="tpu_custom_call" | custom-call | tf_op jit(solution)/shard_map/pallas_call | solution.py:515
  (3 shorter events, 0.0 us)
Async XLA Ops:
  0.6 1.8 %collective-permute-start = (f32[6,4,8,256]{3,2,1,0:T(8,128)}, f32[6,4,8,256]{3,2,1,0:T(8,128)S(1)}, u32[]{:S(2)}, u32[]{:S(2)}) collective-permute-start(f32[6,4,8,256]{3,2,1,0:T(8,128)} %flow_ref.1), channel_id=1, source_target_pairs={{0,1},{1,0},{2,3},{3,2},{4,5},{5,4},{6,7},{7,6},{8,9},{9,8},{10,11... | collective-permute-start | bytes 589832 | tf_op jit(solution)/shard_map/ppermute | solution.py:437
  1.1 0.9 %copy-start = (f32[6,4,8,256]{3,2,1,0:T(8,128)S(1)}, f32[6,4,8,256]{3,2,1,0:T(8,128)}, u32[]{:S(2)}) copy-start(f32[6,4,8,256]{3,2,1,0:T(8,128)} %flow_ref.1) | copy-start | bytes 589828
  2.6 3.9 %collective-permute-start.1 = (f32[8,128]{1,0:T(8,128)S(1)}, f32[8,128]{1,0:T(8,128)S(1)}, u32[]{:S(2)}, u32[]{:S(2)}) collective-permute-start(f32[8,128]{1,0:T(8,128)S(1)} %shard_map.78.after_ref), channel_id=1, source_target_pairs={{0,3},{1,2},{2,1},{3,0},{4,7},{5,6},{6,5},{7,4},{8,11},{9,10},{10,... | collective-permute-start | bytes 12296 | tf_op jit(solution)/shard_map/ppermute | solution.py:465
  5.2 4.4 %copy-start.4 = (s32[2,8]{1,0:T(2,128)S(1)}, s32[2,8]{1,0:T(2,128)}, u32[]{:S(2)}) copy-start(s32[2,8]{1,0:T(2,128)} %partner_ref.1) | copy-start | bytes 196
  5.2 4.4 %copy-start.5 = (s32[2,8]{1,0:T(2,128)S(1)}, s32[2,8]{1,0:T(2,128)}, u32[]{:S(2)}) copy-start(s32[2,8]{1,0:T(2,128)} %index_ref.1) | copy-start | bytes 196
  5.3 4.3 %copy-start.1 = (f32[8,256]{1,0:T(8,128)S(1)}, f32[8,256]{1,0:T(8,128)}, u32[]{:S(2)}) copy-start(f32[8,256]{1,0:T(8,128)} %step_in_ref.1) | copy-start | bytes 24580
  5.3 4.3 %copy-start.2 = (f32[6,6]{1,0:T(8,128)S(1)}, f32[6,6]{1,0:T(8,128)}, u32[]{:S(2)}) copy-start(f32[6,6]{1,0:T(8,128)} %jac_pitch_ref.1) | copy-start | bytes 436
  5.3 4.3 %copy-start.3 = (f32[6,6]{1,0:T(8,128)S(1)}, f32[6,6]{1,0:T(8,128)}, u32[]{:S(2)}) copy-start(f32[6,6]{1,0:T(8,128)} %jac_axial_ref.1) | copy-start | bytes 436
  5.3 7.9 %collective-permute-start.2 = (f32[6,4,8,256]{3,2,1,0:T(8,128)S(1)}, f32[6,4,8,256]{3,2,1,0:T(8,128)S(1)}, u32[]{:S(2)}, u32[]{:S(2)}) collective-permute-start(f32[6,4,8,256]{3,2,1,0:T(8,128)S(1)} %shard_map.80), channel_id=1, source_target_pairs={{0,2},{1,15},{2,0},{3,5},{4,6},{5,3},{6,4},{7,9},{8,10},{9,7},{10,... | collective-permute-start | bytes 589832 | tf_op jit(solution)/shard_map/ppermute | solution.py:480
  6.5 4.8 %collective-permute-start.4 = (f32[16,128]{1,0:T(8,128)S(1)}, f32[16,128]{1,0:T(8,128)S(1)}, u32[]{:S(2)}, u32[]{:S(2)}) collective-permute-start(f32[16,128]{1,0:T(8,128)S(1)} %pad_maximum_fusion.1), channel_id=1, source_target_pairs={{0,8},{1,9},{2,10},{3,11},{4,12},{5,13},{6,14},{7,15},{8,0},{9,1},... | collective-permute-start | bytes 24584 | tf_op jit(solution)/shard_map/ppermute | solution.py:465
  11.4 3.7 %collective-permute-start.5 = (f32[32,128]{1,0:T(8,128)S(1)}, f32[32,128]{1,0:T(8,128)S(1)}, u32[]{:S(2)}, u32[]{:S(2)}) collective-permute-start(f32[32,128]{1,0:T(8,128)S(1)} %pad_maximum_fusion.refs_6_), channel_id=1, source_target_pairs={{0,4},{1,5},{2,6},{3,7},{4,0},{5,1},{6,2},{7,3},{8,12},{9,13},{10,... | collective-permute-start | bytes 49160 | tf_op jit(solution)/shard_map/ppermute | solution.py:465
  13.3 1.9 %collective-permute-start.3 = (f32[6,4,8,256]{3,2,1,0:T(8,128)S(1)}, f32[6,4,8,256]{3,2,1,0:T(8,128)S(1)}, u32[]{:S(2)}, u32[]{:S(2)}) collective-permute-start(f32[6,4,8,256]{3,2,1,0:T(8,128)S(1)} %collective-permute-done.2.refs_1_), channel_id=1, source_target_pairs={{0,1},{1,0},{2,3},{3,2},{4,5},{5,4},{6,7},{7,6},{8,9},{9,8},{10,11... | collective-permute-start | bytes 589832 | tf_op jit(solution)/shard_map/ppermute | solution.py:481
